TPU v7x, 512 devices: a whole 4x8x8 slice. The times are simulated.
512 devices in a mesh: gx: 16 (over y, core), gy: 4 (over x), gz: 8 (over z).
Axes of the slice: x: 4, y: 8, z: 8, core: 2. Of those that a mesh axis runs over, the one named last changes fastest.
Arguments:
- start_block: float32 [3, 32, 32, 32, 256], P(None, 'gx', 'gy', 'gz'), may hold values from -6 to 6
- node_mass: float32 [3, 32, 32, 32], P(None, 'gx', 'gy', 'gz'), may hold values from 0.5 to 2
- ground_spring: float32 [3, 32, 32, 32], P(None, 'gx', 'gy', 'gz'), may hold values from 0.05 to 0.5
- stiffness: float32 [3, 3, 32, 32, 32], P(None, None, 'gx', 'gy', 'gz'), may hold values from 0.5 to 2
- yield_flags: int32 [3, 16, 32, 32, 32], P(None, None, 'gx', 'gy', 'gz'), may hold values 0 or 1
- stress_old: float32 [3, 16, 32, 32, 32], P(None, None, 'gx', 'gy', 'gz'), may hold values from -6 to 6
Outputs:
- subspace: float32 [3, 32, 32, 32, 256], P(None, 'gx', 'gy', 'gz')
- projected: float32 [256, 256], replicated
- force: float32 [3, 32, 32, 32], P(None, 'gx', 'gy', 'gz')
- stress_new: float32 [3, 16, 32, 32, 32], P(None, None, 'gx', 'gy', 'gz')
All inputs are finite; a program needn't handle non-finite values. No bound on the sum of `yield_flags` on one device may be relied on, other than what follows from the above.
Results may differ from a plain program's by a relative error of at most 0.00015.
Values sent between devices are 32-bit elements; how exact they have to be, the bound alone decides.
No kernel may reach another device: no remote copies, remote signals or barrier semaphores. Data moves between devices by JAX's collectives and lax.ppermute only.
A program may use at most 64 MiB of HBM per device.

v0:
```python
import jax
import jax.numpy as jnp
from jax import lax
from jax.sharding import PartitionSpec as P

DEGREE = 4
ITERS = 2


PRECISE = lax.Precision.HIGHEST


def extended(block, sides, width):
    for axis, dim in sides:
        count = lax.axis_size(axis)
        forward = [(i, i + 1) for i in range(count - 1)]
        backward = [(target, source) for source, target in forward]
        low = lax.ppermute(
            lax.slice_in_dim(block, block.shape[dim] - width, None, axis=dim), axis, forward
        )
        high = lax.ppermute(lax.slice_in_dim(block, 0, width, axis=dim), axis, backward)
        block = jnp.concatenate([low, block, high], axis=dim)
    return block


def neighbour(padded, leading, direction, sense):
    slicer = [slice(None)] * padded.ndim
    for position in range(3):
        slicer[leading + position] = slice(1, -1)
    if sense > 0:
        slicer[leading + direction] = slice(2, None)
    else:
        slicer[leading + direction] = slice(0, -2)
    return padded[tuple(slicer)]


def tangent_of(stiffness, yield_flags):
    share = jnp.mean(yield_flags.astype(jnp.float32), axis=1)
    return stiffness * (1.0 - 0.9 * share)[:, None]


def edge_weights(tangent, padded_t):
    upward = []
    downward = []
    for direction in range(3):
        upward.append(0.5 * (tangent[direction] + neighbour(padded_t, 2, direction, 1)[direction]))
        downward.append(
            0.5 * (tangent[direction] + neighbour(padded_t, 2, direction, -1)[direction])
        )
    return (upward, downward)


def stiffness_times(vectors, padded_v, diagonal_sum, upward, downward):
    result = diagonal_sum[..., None] * vectors
    for direction in range(3):
        result = result - upward[direction][..., None] * neighbour(padded_v, 1, direction, 1)
        result = result - downward[direction][..., None] * neighbour(padded_v, 1, direction, -1)
    return result


def filtered(vectors, apply_k, node_mass, middle, spread):

    def operator_a(field):
        return apply_k(field) / node_mass[..., None]

    earlier = vectors
    current = (operator_a(vectors) - middle * vectors) / spread
    for repeat in range(DEGREE - 1):
        following = 2.0 * (operator_a(current) - middle * current) / spread - earlier
        earlier, current = (current, following)
    return current


def stress_update(displace, padded_u, stiffness, yield_flags, stress_old):
    fibers = stress_old.shape[1]
    heights = (jnp.arange(fibers).astype(jnp.float32) + 0.5) / fibers - 0.5
    results = []
    for direction in range(3):
        above = neighbour(padded_u, 1, direction, 1)
        below = neighbour(padded_u, 1, direction, -1)
        other = (direction + 1) % 3
        axial = 0.5 * (above[direction] - below[direction])
        bending = above[other] - 2.0 * displace[other] + below[other]
        strain = axial[None] + heights[:, None, None, None] * bending[None]
        modulus = stiffness[direction, direction][None] * jnp.where(
            yield_flags[direction] == 1, 0.05, 1.0
        )
        results.append(stress_old[direction] + modulus * strain)
    return jnp.stack(results)


def on_device(start_block, node_mass, ground_spring, stiffness, yield_flags, stress_old):
    tangent = tangent_of(stiffness, yield_flags)
    padded_t = extended(tangent, (("gx", 2), ("gy", 3), ("gz", 4)), 1)
    upward, downward = edge_weights(tangent, padded_t)
    edge_total = sum(upward) + sum(downward)
    diagonal_sum = ground_spring + edge_total
    spectral_top = lax.pmax(jnp.max((diagonal_sum + edge_total) / node_mass), ("gx", "gy", "gz"))
    middle = spectral_top * 9.0 / 16.0
    spread = spectral_top * 7.0 / 16.0

    def apply_k(field):
        padded_v = extended(field, (("gx", 1), ("gy", 2), ("gz", 3)), 1)
        return stiffness_times(field, padded_v, diagonal_sum, upward, downward)

    width = start_block.shape[-1]
    mass_rows = node_mass.reshape(-1)
    count = mass_rows.shape[0] // 3
    vectors = start_block
    for turn in range(ITERS):
        current = filtered(vectors, apply_k, node_mass, middle, spread)
        flat_rows = current.reshape(-1, width)
        weighted = mass_rows[:, None] * flat_rows
        gram = lax.psum(jnp.dot(flat_rows.T, weighted, precision=PRECISE), ("gx", "gy", "gz"))
        factor = jnp.linalg.cholesky(gram)
        basis_t = lax.linalg.triangular_solve(factor, flat_rows.T, left_side=True, lower=True)
        vectors = basis_t.T.reshape(current.shape)
        image = apply_k(vectors).reshape(-1, width)
        projected = lax.psum(jnp.dot(basis_t, image, precision=PRECISE), ("gx", "gy", "gz"))
    lateral = lax.psum(
        jnp.dot(basis_t[:, :count], mass_rows[:count], precision=PRECISE), ("gx", "gy", "gz")
    )
    hfactor = jnp.linalg.cholesky(projected)
    halfway = lax.linalg.triangular_solve(hfactor, lateral[:, None], left_side=True, lower=True)
    weights = lax.linalg.triangular_solve(
        hfactor, halfway, left_side=True, lower=True, transpose_a=True
    )[:, 0]
    displace = jnp.dot(weights, basis_t, precision=PRECISE).reshape(node_mass.shape)
    force = node_mass * displace
    padded_u = extended(displace, (("gx", 1), ("gy", 2), ("gz", 3)), 1)
    stress_new = stress_update(displace, padded_u, stiffness, yield_flags, stress_old)
    total_dofs = (
        3
        * node_mass.shape[1]
        * node_mass.shape[2]
        * node_mass.shape[3]
        * lax.axis_size("gx")
        * lax.axis_size("gy")
        * lax.axis_size("gz")
    )
    subspace = vectors * jnp.sqrt(jnp.float32(total_dofs))
    return (subspace, projected, force, stress_new)


def solution(mesh):
    return jax.shard_map(
        on_device,
        mesh=mesh,
        in_specs=(
            P(None, "gx", "gy", "gz", None),
            P(None, "gx", "gy", "gz"),
            P(None, "gx", "gy", "gz"),
            P(None, None, "gx", "gy", "gz"),
            P(None, None, "gx", "gy", "gz"),
            P(None, None, "gx", "gy", "gz"),
        ),
        out_specs=(
            P(None, "gx", "gy", "gz", None),
            P(),
            P(None, "gx", "gy", "gz"),
            P(None, None, "gx", "gy", "gz"),
        ),
        check_vma=False,
    )
```

profile of v0, /device:TPU:1, one launch (start us, length us, event | category | flops | bytes accessed | tf_op | source)
XLA Modules:
  0.0 1415.0 jit_solution(9056235277101413688)
XLA Ops:
  9.0 8.8 collective-permute-start
  22.5 4.0 collective-permute-start.3
  29.4 4.0 collective-permute-start.5
  33.4 5.6 collective-permute-start.7
  41.9 3.1 collective-permute-done.6
  46.3 4.6 collective-permute-start.9
  51.0 100.1 %pmax.7 = f32[]{:T(128)} all-reduce(f32[]{:T(128)} %fusion.158), channel_id=1, replica_groups=mesh['gx'=16,'gy'=4,'gz'=8] {'gx','gy','gz'}, use_global_device_ids=true, to_apply=%region_2.0 | all-reduce | flops 1 | bytes 8 | tf_op jit(solution)/shard_map/pmax | solution.py:98
  153.0 3.1 collective-permute-start.11
  158.0 3.8 collective-permute-done.10
  162.6 4.2 collective-permute-start.12
  171.8 4.3 collective-permute-start.15
  177.7 3.1 collective-permute-start.17
  183.5 4.3 collective-permute-done.16
  191.0 4.9 collective-permute-start.19
  198.8 4.6 collective-permute-start.21
  204.8 3.9 collective-permute-start.23
  210.5 4.1 collective-permute-done.22
  217.4 6.3 collective-permute-start.25
  226.7 4.6 collective-permute-start.27
  232.6 3.6 collective-permute-start.29
  238.1 3.8 collective-permute-done.28
  244.6 273.4 %all-reduce.5.cloned.1.call-done = f32[256,256]{0,1:T(8,128)} async-done(((f32[256,256]{0,1:T(8,128)}), f32[256,256]{0,1:T(8,128)}) %all-reduce.5.cloned.1.call-update) | async-done | bytes 262160 | tf_op jit(solution)/shard_map/psum | solution.py:114
  519.2 11.7 cholesky.172
  531.0 9.8 custom-call.20
  541.3 11.7 cholesky.189
  555.7 4.4 while.6
  560.1 19.7 %custom-call.21 = f32[2,128,128]{1,2,0:T(8,128)S(1)} custom-call(f32[2,128,128]{2,1,0:T(8,128)S(1)} %get-tuple-element.28), custom_call_target="InvertDiagBlocksLowerTriangular" | custom-call | tf_op jit(solution)/shard_map/triangular_solve/custom-call.0 | solution.py:116
  580.7 2.9 collective-permute-start.31
  585.6 3.9 collective-permute-done.30
  590.9 4.0 collective-permute-start.33
  596.3 3.3 collective-permute-start.35
  601.5 4.1 collective-permute-done.34
  608.4 4.7 collective-permute-start.37
  616.1 4.3 collective-permute-start.39
  626.6 4.1 collective-permute-done.40
  633.7 5.7 collective-permute-start.43
  642.3 4.6 collective-permute-start.45
  652.5 3.8 collective-permute-done.46
  659.1 6.5 collective-permute-start.49
  668.6 4.6 collective-permute-start.51
  674.6 3.4 collective-permute-start.53
  679.9 3.8 collective-permute-done.52
  686.3 275.2 %all-reduce.7.cloned.1.call-done = f32[256,256]{0,1:T(8,128)} async-done(((f32[256,256]{0,1:T(8,128)}), f32[256,256]{0,1:T(8,128)}) %all-reduce.7.cloned.1.call-update) | async-done | bytes 262160 | tf_op jit(solution)/shard_map/psum | solution.py:114
  962.7 11.7 cholesky.206
  974.5 9.8 custom-call.22
  984.8 11.7 cholesky.223
  999.2 4.0 while.7
  1003.2 19.7 %custom-call.23 = f32[2,128,128]{1,2,0:T(8,128)S(1)} custom-call(f32[2,128,128]{2,1,0:T(8,128)S(1)} %get-tuple-element.29), custom_call_target="InvertDiagBlocksLowerTriangular" | custom-call | tf_op jit(solution)/shard_map/triangular_solve/custom-call.0 | solution.py:116
  1023.7 2.9 collective-permute-start.55
  1029.4 3.2 collective-permute-done.54
  1034.0 4.0 collective-permute-start.57
  1039.3 3.3 collective-permute-start.59
  1045.0 3.6 collective-permute-done.58
  1050.8 98.9 %psum.31 = f32[256]{0:T(256)S(1)} all-reduce(f32[256]{0:T(256)S(1)} %bitcast.216), channel_id=1, replica_groups=mesh['gx'=16,'gy'=4,'gz'=8] {'gx','gy','gz'}, use_global_device_ids=true, to_apply=%region_10.13 | all-reduce | flops 256 | bytes 2048 | tf_op jit(solution)/shard_map/psum | solution.py:120
  1149.7 168.5 %all-reduce.9.cloned.1.call-done = f32[256,256]{0,1:T(8,128)} async-done(((f32[256,256]{0,1:T(8,128)}), f32[256,256]{0,1:T(8,128)}) %all-reduce.9.cloned.1.call-update) | async-done | bytes 262160 | tf_op jit(solution)/shard_map/psum | solution.py:119
  1320.1 11.7 cholesky.240
  1331.8 9.8 custom-call.24
  1342.1 11.7 cholesky.257
  1356.5 4.0 while.5
  1360.5 19.9 %custom-call.16 = f32[2,128,128]{1,2,0:T(8,128)S(1)} custom-call(f32[2,128,128]{2,1,0:T(8,128)S(1)} %get-tuple-element.21), custom_call_target="InvertDiagBlocksLowerTriangular" | custom-call | tf_op jit(solution)/shard_map/triangular_solve | solution.py:125
  1382.1 2.9 collective-permute-start.61
  1391.6 4.0 collective-permute-start.63
  1396.5 3.3 collective-permute-start.65
  1402.0 4.3 collective-permute-done.64
  (302 shorter events, 134.6 us)
Async XLA Ops:
  7.2 510.8 %all-reduce.5.cloned.1.call-start = ((), (), s32[]{:S(2)}) async-start(), calls=%async_computation | async-start | bytes 524288 | tf_op jit(solution)/shard_map/psum | solution.py:114
  9.0 10.7 collective-permute-start
  21.0 5.7 collective-permute-start.2
  22.5 5.4 collective-permute-start.3
  28.1 13.0 collective-permute-start.4
  29.4 11.7 collective-permute-start.5
  33.4 8.5 collective-permute-start.7
  39.1 5.9 collective-permute-start.6
  45.0 107.8 %collective-permute-start.8 = (f32[3,4,1,4,256]{4,3,2,1,0:T(4,128)S(1)}, f32[3,4,1,4,256]{4,3,2,1,0:T(4,128)S(1)}, u32[]{:S(2)}, u32[]{:S(2)}) collective-permute-start(f32[3,4,1,4,256]{4,3,2,1,0:T(4,128)S(1)} %get-tuple-element.119), channel_id=1, source_target_pairs={{8,0},{16,8},{24,16},{9,1},{17,9},{25,17},{10,2},{18,10},{26,18},{... | collective-permute-start | bytes 147464 | tf_op jit(solution)/shard_map/ppermute | solution.py:21
  46.3 106.5 %collective-permute-start.9 = (f32[3,4,1,4,256]{4,3,2,1,0:T(4,128)S(1)}, f32[3,4,1,4,256]{4,3,2,1,0:T(4,128)S(1)}, u32[]{:S(2)}, u32[]{:S(2)}) collective-permute-start(f32[3,4,1,4,256]{4,3,2,1,0:T(4,128)S(1)} %get-tuple-element.118), channel_id=1, source_target_pairs={{0,8},{8,16},{16,24},{1,9},{9,17},{17,25},{2,10},{10,18},{18,26},{... | collective-permute-start | bytes 147464 | tf_op jit(solution)/shard_map/ppermute | solution.py:18
  153.0 5.0 collective-permute-start.11
  156.1 5.6 collective-permute-start.10
  162.6 6.6 collective-permute-start.12
  170.5 5.8 collective-permute-start.14
  171.8 5.7 collective-permute-start.15
  177.7 5.9 collective-permute-start.17
  180.8 7.0 collective-permute-start.16
  188.7 7.5 collective-permute-start.18
  191.0 6.5 collective-permute-start.19
  197.5 5.9 collective-permute-start.20
  198.8 5.8 collective-permute-start.21
  204.8 5.7 collective-permute-start.23
  208.7 5.9 collective-permute-start.22
  215.5 8.6 collective-permute-start.24
  217.4 7.9 collective-permute-start.25
  225.4 5.9 collective-permute-start.26
  226.7 5.8 collective-permute-start.27
  232.6 5.5 collective-permute-start.29
  236.3 5.6 collective-permute-start.28
  244.2 717.2 %all-reduce.7.cloned.1.call-start = ((), (), s32[]{:S(2)}) async-start(), calls=%async_computation.1 | async-start | bytes 524288 | tf_op jit(solution)/shard_map/psum | solution.py:114
  580.7 4.9 collective-permute-start.31
  583.6 5.9 collective-permute-start.30
  589.6 5.3 collective-permute-start.32
  590.9 5.2 collective-permute-start.33
  596.3 5.3 collective-permute-start.35
  599.5 6.1 collective-permute-start.34
  606.5 7.0 collective-permute-start.36
  608.4 6.3 collective-permute-start.37
  614.8 5.6 collective-permute-start.38
  616.1 5.5 collective-permute-start.39
  624.3 6.4 collective-permute-start.40
  631.6 8.1 collective-permute-start.42
  633.7 7.3 collective-permute-start.43
  641.0 5.9 collective-permute-start.44
  642.3 5.8 collective-permute-start.45
  650.6 5.7 collective-permute-start.46
  657.2 8.8 collective-permute-start.48
  659.1 8.1 collective-permute-start.49
  667.3 5.9 collective-permute-start.50
  668.6 5.8 collective-permute-start.51
  674.6 5.3 collective-permute-start.53
  678.0 5.6 collective-permute-start.52
  686.0 632.2 %all-reduce.9.cloned.1.call-start = ((), (), s32[]{:S(2)}) async-start(), calls=%async_computation.2 | async-start | bytes 524288 | tf_op jit(solution)/shard_map/psum | solution.py:119
  1023.7 4.9 collective-permute-start.55
  1026.7 5.9 collective-permute-start.54
  1032.7 5.3 collective-permute-start.56
  1034.0 5.2 collective-permute-start.57
  1039.3 5.7 collective-permute-start.59
  1042.6 6.1 collective-permute-start.58
  1382.1 5.4 collective-permute-start.61
  1385.1 5.0 collective-permute-start.60
  1390.3 6.1 collective-permute-start.62
  1396.5 5.5 collective-permute-start.65
  1399.8 6.5 collective-permute-start.64
  (16 other events, 50.0 us)
Sparse Core Ops, SparseCore 0:
  244.4 273.5 all-reduce.4
  686.1 275.3 all-reduce.6
  1050.7 267.3 all-reduce.8
where the time goes:
time: 1420 us
  waiting for transfers between devices  797 us (56%)
  blocking collectives  199 us (14%)
  starting transfers between devices  190 us (13%)
  other arithmetic  176 us (12%)
  local copies, waits for them, and re-layouts  22.5 us (2%)
  between operations  20.8 us (1%)
    psum x2, waiting for transfers between devices, on_device(): lax.psum(jnp.dot(flat_rows.T, weighted, precision=PRECISE), ('gx', 'gy',...  549 us
    psum x1, waiting for transfers between devices, on_device(): lax.psum(jnp.dot(basis_t, image, precision=PRECISE), ('gx', 'gy', 'gz'))  168 us
    ppermute x33, starting transfers between devices, extended(): lax.ppermute(lax.slice_in_dim(block, block.shape[dim] - width, None, axis...  130 us
    pmax x1, blocking collectives, on_device(): lax.pmax(jnp.max((diagonal_sum + edge_total) / node_mass), ('gx', 'gy', '...  100 us
    psum x1, blocking collectives, on_device(): lax.psum(jnp.dot(basis_t[:, :count], mass_rows[:count], precision=PRECISE...  98.9 us
    another operation x14, other arithmetic, on_device(): factor = jnp.linalg.cholesky(gram)  69.2 us
    ppermute x33, starting transfers between devices, extended(): lax.ppermute(lax.slice_in_dim(block, 0, width, axis=dim), axis, backward)  59.4 us
    ppermute x33, waiting for transfers between devices, extended(): lax.ppermute(lax.slice_in_dim(block, 0, width, axis=dim), axis, backward)  55 us
  transfers between devices with their start and end apart: 69, of which 50 were waited for; matrix products, arithmetic and copies ran while one was open for 0% of the time, Pallas kernels for 0%

commit v1 on v0

v1 whole, which is shorter than its diff:
```python
import functools

import jax
import jax.numpy as jnp
from jax import lax
from jax.experimental import pallas as pl
from jax.experimental.pallas import tpu as pltpu
from jax.sharding import PartitionSpec as P

DEGREE = 4
ITERS = 2
PRECISE = lax.Precision.HIGHEST
AXES = ("gx", "gy", "gz")

NODES = 64
DEVICES = 512
BLOCK = 32


def dot(a, b, contract=((1,), (0,))):
    return lax.dot_general(
        a, b, (contract, ((), ())), precision=PRECISE, preferred_element_type=jnp.float32
    )


def pack_kernel(start_ref, coef_ref, out_ref):
    for comp in range(4):
        if comp < 3:
            block = start_ref[comp * NODES : (comp + 1) * NODES, :]
            pairs = jnp.concatenate([block[:, :128], block[:, 128:]], axis=0).T
        else:
            pairs = jnp.zeros((128, 128), jnp.float32)
        source = comp % 3
        rows = [
            jnp.broadcast_to(coef_ref[source * 3 + r : source * 3 + r + 1, :], (8, 128))
            for r in range(3)
        ]
        for gx in range(16):
            first = (gx * 4 + comp) * 32
            out_ref[pl.ds(first, 8, stride=4), :] = pairs[gx * 8 : gx * 8 + 8]
            for r in range(3):
                out_ref[pl.ds(first + r + 1, 8, stride=4), :] = rows[r]


def iota(axis):
    return lax.broadcasted_iota(jnp.int32, (4, 8, 128), axis)


def grid_row(ref, kind, gx):
    return ref[pl.ds(gx * 128 + kind, 32, stride=4), :].reshape(4, 8, 128)


def roll(value, shift, axis=2):
    return pltpu.roll(value, shift, axis)


def both_halves(value):
    lane = iota(2)
    turned = roll(value, 64)
    return jnp.where(lane < 64, value, turned), jnp.where(lane < 64, turned, value)


def x_up(here, above):
    return jnp.where((iota(2) & 32) == 0, roll(here, 96), roll(above, 32))


def x_down(here, below):
    return jnp.where((iota(2) & 32) != 0, roll(here, 32), roll(below, 96))


def y_up(here):
    moved = jnp.concatenate([here[1:], jnp.zeros((1, 8, 128), jnp.float32)], axis=0)
    return jnp.where((iota(2) & 28) != 28, roll(here, 124), roll(moved, 28))


def y_down(here):
    moved = jnp.concatenate([jnp.zeros((1, 8, 128), jnp.float32), here[:-1]], axis=0)
    return jnp.where((iota(2) & 28) != 0, roll(here, 4), roll(moved, 100))


def z_up(here):
    other = jnp.where(iota(1) < 7, roll(roll(here, 3), 7, 1), 0.0)
    return jnp.where((iota(2) & 3) != 3, roll(here, 127), other)


def z_down(here):
    other = jnp.where(iota(1) > 0, roll(roll(here, 125), 1, 1), 0.0)
    return jnp.where((iota(2) & 3) != 0, roll(here, 1), other)


def around(ref, gx):
    here = ref[gx + 1]
    return here, (
        (x_up(here, ref[gx + 2]), x_down(here, ref[gx])),
        (y_up(here), y_down(here)),
        (z_up(here), z_down(here)),
    )


def load_tangents(rows_ref, tangent_ref):
    tangent_ref[0] = jnp.zeros((4, 8, 128), jnp.float32)
    tangent_ref[17] = jnp.zeros((4, 8, 128), jnp.float32)

    def step(gx, carry):
        tangent_ref[gx + 1] = both_halves(grid_row(rows_ref, 1, gx))[0]
        return carry

    lax.fori_loop(0, 16, step, 0, unroll=4)


def edges_at(rows_ref, tangent_ref, gx):
    first = tangent_ref[gx + 1]
    second = both_halves(grid_row(rows_ref, 1, gx))[1]
    third, mass = both_halves(grid_row(rows_ref, 2, gx))
    spring = grid_row(rows_ref, 3, gx)
    ups = [
        0.5 * (first + x_up(first, tangent_ref[gx + 2])),
        0.5 * (second + y_up(second)),
        0.5 * (third + z_up(third)),
    ]
    downs = [
        0.5 * (first + x_down(first, tangent_ref[gx])),
        0.5 * (second + y_down(second)),
        0.5 * (third + z_down(third)),
    ]
    total = (ups[0] + ups[1] + ups[2]) + (downs[0] + downs[1] + downs[2])
    return ups, downs, total, spring + total, mass


def spectrum_kernel(rows_ref, out_ref, tangent_ref):
    load_tangents(rows_ref, tangent_ref)

    def step(gx, best):
        _, _, total, diagonal, mass = edges_at(rows_ref, tangent_ref, gx)
        return jnp.maximum(best, (diagonal + total) / mass)

    best = lax.fori_loop(0, 16, step, jnp.zeros((4, 8, 128), jnp.float32), unroll=4)
    best = jnp.max(jnp.max(best, axis=0), axis=(0, 1), keepdims=True)
    out_ref[...] = jnp.broadcast_to(best, (8, 128))


def filter_kernel(
    comp_ref, rows_ref, top_ref, out_ref, tangent_ref, even_ref, odd_ref, up_ref, down_ref,
    diagonal_ref, inverse_ref
):
    load_tangents(rows_ref, tangent_ref)
    top = jnp.max(jnp.max(top_ref[...], axis=0, keepdims=True), axis=1, keepdims=True)
    middle = top * 9.0 / 16.0
    spread = top * 7.0 / 16.0
    inverse_spread = 1.0 / spread
    ratio = middle * inverse_spread
    for ref in (even_ref, odd_ref):
        ref[0] = jnp.zeros((4, 8, 128), jnp.float32)
        ref[17] = jnp.zeros((4, 8, 128), jnp.float32)

    def prepare(gx, carry):
        ups, downs, _, diagonal, mass = edges_at(rows_ref, tangent_ref, gx)
        for direction in range(3):
            up_ref[direction, gx] = ups[direction]
            down_ref[direction, gx] = downs[direction]
        diagonal_ref[gx] = diagonal
        inverse_ref[gx] = inverse_spread / mass
        even_ref[gx + 1] = grid_row(rows_ref, 0, gx)
        return carry

    lax.fori_loop(0, 16, prepare, 0, unroll=4)

    def stiffness_times(here, sides, gx):
        result = diagonal_ref[gx] * here
        for direction in range(3):
            result = result - up_ref[direction, gx] * sides[direction][0]
            result = result - down_ref[direction, gx] * sides[direction][1]
        return result

    def advance(current_ref, other_ref, first):
        def step(gx, carry):
            here, sides = around(current_ref, gx)
            image = stiffness_times(here, sides, gx) * inverse_ref[gx] - ratio * here
            if first:
                other_ref[gx + 1] = image
            else:
                other_ref[gx + 1] = 2.0 * image - other_ref[gx + 1]
            return carry

        lax.fori_loop(0, 16, step, 0, unroll=4)

    for turn in range(ITERS):
        for repeat in range(DEGREE):
            if repeat % 2 == 0:
                advance(even_ref, odd_ref, repeat == 0)
            else:
                advance(odd_ref, even_ref, False)

    comp = comp_ref[0]

    def finish(gx, carry):
        here, sides = around(even_ref, gx)
        axial = [0.5 * (up - down) for up, down in sides]
        bending = [(up - 2.0 * here) + down for up, down in sides]
        values = [
            here,
            stiffness_times(here, sides, gx),
            jnp.where(comp == 0, axial[0], jnp.where(comp == 1, axial[1], axial[2])),
            jnp.where(comp == 0, bending[2], jnp.where(comp == 1, bending[0], bending[1])),
        ]
        for kind in range(4):
            out_ref[pl.ds(gx * 128 + kind, 32, stride=4), :] = values[kind].reshape(32, 128)
        return carry

    lax.fori_loop(0, 16, finish, 0, unroll=4)


def local_rows(rows_ref, kind):
    lane = lax.broadcasted_iota(jnp.int32, (128, 128), 1)
    parts = []
    for comp in range(3):
        parts.append(
            jnp.concatenate(
                [rows_ref[pl.ds((gx * 4 + comp) * 32 + kind, 8, stride=4), :] for gx in range(16)],
                axis=0,
            )
        )
    turned = [pltpu.roll(part, 64, 1) for part in parts]
    low = lane < 64
    upper = [jnp.where(low, parts[0], turned[1]), jnp.where(low, parts[2], 0.0)]
    lower = [jnp.where(low, turned[0], parts[1]), jnp.where(low, turned[2], 0.0)]
    return jnp.concatenate(
        [jnp.concatenate(upper, axis=1), jnp.concatenate(lower, axis=1)], axis=0
    )


def product_kernel(rows_ref, mass_ref, out_ref):
    vectors = local_rows(rows_ref, 0)
    image = local_rows(rows_ref, 1)
    weighted = vectors * mass_ref[...]
    gram = dot(weighted, vectors, ((1,), (1,)))
    stiff = dot(vectors, image, ((1,), (1,)))
    row = lax.broadcasted_iota(jnp.int32, (256, 256), 0)
    column = lax.broadcasted_iota(jnp.int32, (256, 256), 1)
    both = jnp.where(row >= column, gram, stiff)
    diagonal = jnp.sum(vectors * image, axis=1, keepdims=True)
    lane = lax.broadcasted_iota(jnp.int32, (256, 256), 1)
    lateral = jnp.sum(jnp.where(lane < NODES, weighted, 0.0), axis=1, keepdims=True)
    out_ref[pl.ds(0, 256, stride=2), :] = both[:, :128]
    out_ref[pl.ds(512, 256, stride=2), :] = both[:, 128:]
    out_ref[pl.ds(1, 256, stride=2), :] = jnp.broadcast_to(diagonal, (256, 128))
    out_ref[pl.ds(513, 256, stride=2), :] = jnp.broadcast_to(lateral, (256, 128))


def total_kernel(rows_ref, out_ref):
    total = jnp.sum(rows_ref[...].reshape(128, 8, 128), axis=0)
    total = total + pltpu.roll(total, 2, 0)
    total = total + pltpu.roll(total, 4, 0)
    out_ref[...] = jnp.broadcast_to(total[None], (128, 8, 128)).reshape(1024, 128)


def factor_block(gram, stiff):
    lane = lax.broadcasted_iota(jnp.int32, (BLOCK, 128), 1)
    row = lax.broadcasted_iota(jnp.int32, (BLOCK, 128), 0)
    low = lane < 64
    columns = [
        jnp.where(
            low,
            jnp.broadcast_to(gram[:, j : j + 1], (BLOCK, 128)),
            jnp.broadcast_to(stiff[:, j : j + 1], (BLOCK, 128)),
        )
        for j in range(BLOCK)
    ]
    inverse = jnp.where((lane & 63) == row, 1.0, 0.0)
    pivots = jnp.ones((BLOCK, 128), jnp.float32)
    for k in range(BLOCK):
        column = columns[k]
        pivot = column[k : k + 1, :]
        pivots = jnp.where(row == k, pivot, pivots)
        if k + 1 == BLOCK:
            break
        part = (k + 1) // 8 * 8
        multiple = jnp.where(row[part:] > k, column[part:] * (1.0 / pivot), 0.0)

        def reduced(value):
            tail = value[part:] - multiple * value[k : k + 1, :]
            return tail if part == 0 else jnp.concatenate([value[:part], tail], axis=0)

        for j in range(k + 1, BLOCK):
            columns[j] = reduced(columns[j])
        inverse = reduced(inverse)
    return inverse * lax.rsqrt(pivots)


def final_kernel(sums_ref, rows_ref, subspace_ref, projected_ref, fields_ref, a_ref, e_ref):
    both = jnp.concatenate(
        [sums_ref[pl.ds(0, 256, stride=2), :], sums_ref[pl.ds(512, 256, stride=2), :]], axis=1
    )
    diagonal = sums_ref[pl.ds(1, 256, stride=2), :]
    diagonal = jnp.concatenate([diagonal, diagonal], axis=1)
    lateral = sums_ref[pl.ds(513, 256, stride=2), :]
    turned = both.T
    row = lax.broadcasted_iota(jnp.int32, (256, 256), 0)
    column = lax.broadcasted_iota(jnp.int32, (256, 256), 1)
    gram = jnp.where(row >= column, both, turned)
    stiff = jnp.where(row < column, both, jnp.where(row == column, diagonal, turned))
    a_ref[0] = gram
    a_ref[1] = stiff
    unit = jnp.where(row == column, 1.0, 0.0)
    e_ref[0] = unit
    e_ref[1] = unit
    lane = lax.broadcasted_iota(jnp.int32, (BLOCK, 128), 1)
    for first in range(0, 256, BLOCK):
        tile = first // 128 * 128
        inside = first - tile
        after = first + BLOCK
        small = [a_ref[m, first:after, tile : tile + 128][:, inside : inside + BLOCK] for m in (0, 1)]
        inverse = factor_block(small[0], small[1])
        for m in (0, 1):
            kept = jnp.where((lane >= 64 * m) & (lane < 64 * m + BLOCK), inverse, 0.0)
            shift = (inside - 64 * m) % 128
            spread = pltpu.roll(kept, shift, 1) if shift else kept
            own = kept[:, 64 * m : 64 * m + BLOCK]
            known = slice(0, 128) if after <= 128 else slice(0, 256)
            e_rows = dot(own, e_ref[m, first:after, known])
            e_ref[m, first:after, known] = e_rows
            if after < 256:
                open_ = slice(0, 256) if after < 128 else slice(128, 256)
                a_rows = dot(own, a_ref[m, first:after, open_])
                factor = dot(a_ref[m, after:, tile : tile + 128], spread, ((1,), (1,)))
                a_ref[m, after:, open_] = a_ref[m, after:, open_] - dot(factor, a_rows)
                e_ref[m, after:, known] = e_ref[m, after:, known] - dot(factor, e_rows)
    lower = e_ref[0]
    stiff_lower = e_ref[1]
    vectors = local_rows(rows_ref, 0)
    subspace = dot(vectors.T, lower, ((1,), (1,)))
    subspace_ref[...] = subspace[: 3 * NODES] * jnp.sqrt(jnp.float32(DEVICES * 3 * NODES))
    projected_ref[...] = dot(lower, dot(stiff, lower, ((1,), (1,))))
    weights = dot(stiff_lower.T, dot(stiff_lower, lateral))
    weights = jnp.concatenate([weights, weights], axis=1)
    for place, kind in enumerate((0, 2, 3)):
        value = vectors if kind == 0 else local_rows(rows_ref, kind)
        fields_ref[place : place + 1, :] = jnp.sum(value * weights, axis=0, keepdims=True)
    fields_ref[3:, :] = jnp.zeros((5, 256), jnp.float32)


def call(kernel, shape, scratch=(), smem=(), operands=()):
    return pl.pallas_call(
        kernel,
        out_shape=shape,
        in_specs=[
            pl.BlockSpec(memory_space=pltpu.SMEM if place in smem else pltpu.VMEM)
            for place in range(len(operands))
        ],
        out_specs=jax.tree.map(lambda _: pl.BlockSpec(memory_space=pltpu.VMEM), shape),
        scratch_shapes=list(scratch),
        compiler_params=pltpu.CompilerParams(vmem_limit_bytes=40 * 1024 * 1024),
    )(*operands)


def rows_of(count):
    return jax.ShapeDtypeStruct((count, 128), jnp.float32)


def exchange(rows, per_device):
    blocks = rows.reshape(DEVICES, per_device, 128)
    return lax.all_to_all(blocks, AXES, 0, 0, tiled=True).reshape(rows.shape)


def on_device(start_block, node_mass, ground_spring, stiffness, yield_flags, stress_old):
    width = start_block.shape[-1]
    share = jnp.mean(yield_flags.astype(jnp.float32), axis=1)
    tangent = (stiffness * (1.0 - 0.9 * share)[:, None]).reshape(3, 3, NODES)
    mass = node_mass.reshape(3, NODES)
    spring = ground_spring.reshape(3, NODES)
    coefficients = jnp.stack(
        [
            jnp.concatenate([tangent[0], tangent[1]], axis=1),
            jnp.concatenate([tangent[2], mass], axis=1),
            jnp.concatenate([spring, spring], axis=1),
        ],
        axis=1,
    ).reshape(9, 128)
    padded = pltpu.VMEM((18, 4, 8, 128), jnp.float32)
    plain = pltpu.VMEM((16, 4, 8, 128), jnp.float32)
    sent = call(
        pack_kernel, rows_of(2048), operands=(start_block.reshape(3 * NODES, width), coefficients)
    )
    gathered = exchange(sent, 4)
    own_top = call(spectrum_kernel, rows_of(8), (padded,), operands=(gathered,))
    tops = lax.all_to_all(
        jnp.broadcast_to(own_top[None], (4, 8, 128)), "gy", 0, 0, tiled=True
    ).reshape(32, 128)
    component = lax.axis_index("gy").astype(jnp.int32).reshape(1)
    filtered = call(
        filter_kernel,
        rows_of(2048),
        (
            padded,
            padded,
            padded,
            pltpu.VMEM((3, 16, 4, 8, 128), jnp.float32),
            pltpu.VMEM((3, 16, 4, 8, 128), jnp.float32),
            plain,
            plain,
        ),
        smem=(0,),
        operands=(component, gathered, tops),
    )
    returned = exchange(filtered, 4)
    mass_row = jnp.pad(mass.reshape(1, 3 * NODES), ((0, 0), (0, NODES)))
    products = call(product_kernel, rows_of(1024), operands=(returned, mass_row))
    totals = call(total_kernel, rows_of(1024), operands=(exchange(products, 2),))
    subspace, projected, fields = call(
        final_kernel,
        (
            jax.ShapeDtypeStruct((3 * NODES, width), jnp.float32),
            jax.ShapeDtypeStruct((width, width), jnp.float32),
            jax.ShapeDtypeStruct((8, 256), jnp.float32),
        ),
        (
            pltpu.VMEM((2, 256, 256), jnp.float32),
            pltpu.VMEM((2, 256, 256), jnp.float32),
        ),
        operands=(exchange(totals, 2), returned),
    )
    place = node_mass.shape[1:]
    fields = fields[:3, : 3 * NODES].reshape((3, 3) + place)
    force = node_mass * fields[0]
    axial = fields[1]
    bending = jnp.roll(fields[2], -1, axis=0)
    fibers = stress_old.shape[1]
    heights = ((jnp.arange(fibers).astype(jnp.float32) + 0.5) / fibers - 0.5)[:, None, None, None]
    strain = axial[:, None] + heights * bending[:, None]
    own = jnp.stack([stiffness[d, d] for d in range(3)])[:, None]
    stress_new = stress_old + own * jnp.where(yield_flags == 1, 0.05, 1.0) * strain
    return (subspace.reshape(start_block.shape), projected, force, stress_new)


def solution(mesh):
    return jax.shard_map(
        on_device,
        mesh=mesh,
        in_specs=(
            P(None, "gx", "gy", "gz", None),
            P(None, "gx", "gy", "gz"),
            P(None, "gx", "gy", "gz"),
            P(None, None, "gx", "gy", "gz"),
            P(None, None, "gx", "gy", "gz"),
            P(None, None, "gx", "gy", "gz"),
        ),
        out_specs=(
            P(None, "gx", "gy", "gz", None),
            P(),
            P(None, "gx", "gy", "gz"),
            P(None, None, "gx", "gy", "gz"),
        ),
        check_vma=False,
    )
```

time: 1420 us -> 210 us (0.15)
  waiting for transfers between devices: 797 us -> 58.6 us
  other arithmetic: 176 us -> 2.08 us
  starting transfers between devices: 190 us -> 23.9 us
  blocking collectives: 199 us -> 86.2 us
  Pallas kernels: 0 us -> 32 us
  between operations: 20.8 us -> 0.81 us
  local copies, waits for them, and re-layouts: 22.5 us -> 5.57 us
    psum x3 -> x0, waiting for transfers between devices: 717 us -> none  [the longest x2 549 us: on_device(): lax.psum(jnp.dot(flat_rows.T, weighted, precision=PRECISE), ('gx', 'gy',...]
    ppermute x66 -> x0, starting transfers between devices: 189 us -> none  [the longest x33 130 us: extended(): lax.ppermute(lax.slice_in_dim(block, block.shape[dim] - width, None, axis...]
    another operation x29 -> x4, other arithmetic: 164 us -> 0.17 us  [the longest x3 0.16 us: on_device(): jnp.stack([jnp.concatenate([tangent[0], tangent[1]], axis=1), jnp.concate...]
    pmax x1 -> x0, blocking collectives: 100 us -> none  [on_device(): lax.pmax(jnp.max((diagonal_sum + edge_total) / node_mass), ('gx', 'gy', '...]
    psum x1 -> x0, blocking collectives: 98.9 us -> none  [on_device(): lax.psum(jnp.dot(basis_t[:, :count], mass_rows[:count], precision=PRECISE...]
    all_to_all x0 -> x2, blocking collectives: none -> 86.2 us  [exchange(): return lax.all_to_all(blocks, AXES, 0, 0, tiled=True).reshape(rows.shape)]
    ppermute x66 -> x0, waiting for transfers between devices: 80.1 us -> none  [the longest x33 55 us: extended(): lax.ppermute(lax.slice_in_dim(block, 0, width, axis=dim), axis, backward)]
    all_to_all x0 -> x3, waiting for transfers between devices: none -> 58.6 us  [the longest x2 54.4 us: exchange(): return lax.all_to_all(blocks, AXES, 0, 0, tiled=True).reshape(rows.shape)]
  transfers between devices with their start and end apart: 69 -> 3, of which waited for: 50 -> 3; matrix products, arithmetic and copies ran while one was open for 0% -> 0% of each run, Pallas kernels for 0% -> 0%
where the time goes in v1:
time: 210 us; the launch traced here: 209 us
  blocking collectives  86.2 us (41%)
  waiting for transfers between devices  58.6 us (28%)
  Pallas kernels  32 us (15%)
  starting transfers between devices  23.9 us (11%)
  local copies, waits for them, and re-layouts  5.57 us (3%)
    all_to_all x2, blocking collectives, exchange(): return lax.all_to_all(blocks, AXES, 0, 0, tiled=True).reshape(rows.shape)  86.2 us
    all_to_all x2, waiting for transfers between devices, exchange(): return lax.all_to_all(blocks, AXES, 0, 0, tiled=True).reshape(rows.shape)  54.4 us
    pallas_call x6, Pallas kernels, call(): pl.pallas_call(kernel, out_shape=shape, in_specs=[pl.BlockSpec(memory_spa...  32 us
    all_to_all x2, starting transfers between devices, exchange(): return lax.all_to_all(blocks, AXES, 0, 0, tiled=True).reshape(rows.shape)  20.7 us
  transfers between devices with their start and end apart: 3, of which 3 were waited for; matrix products, arithmetic and copies ran while one was open for 0% of the time, Pallas kernels for 0%

profile of v1, /device:TPU:1, one launch (start us, length us, event | category | flops | bytes accessed | tf_op | source)
XLA Modules:
  0.0 209.2 jit_solution(14419581557449473909)
XLA Ops:
  0.6 1.0 convert_reduce_fusion
  1.7 0.0 copy-start.3
  1.7 0.1 copy.23
  1.8 0.6 copy-done.3
  2.4 0.0 copy-start.4
  2.4 0.0 copy-start.1
  2.5 0.1 copy.24
  2.6 0.1 squeeze.13
  2.7 0.1 copy.25
  2.8 0.1 squeeze.14
  2.9 0.1 copy.26
  3.0 0.1 squeeze.15
  3.1 0.1 copy-done.4
  3.1 0.1 copy.27
  3.2 0.0 copy-start.5
  3.3 0.1 reshape.86
  3.3 0.6 copy-done.5
  4.0 0.1 copy.28
  4.1 0.1 reshape.87
  4.2 0.1 maximum_bitcast_fusion.2
  4.2 0.1 maximum_bitcast_fusion
  4.3 0.0 copy-done.1
  4.3 0.1 reshape.85.start_ref
  4.4 0.1 shard_map.93
  4.6 54.8 %all_to_all.25 = f32[512,4,128]{2,1,0:T(4,128)S(1)} all-to-all(f32[512,4,128]{2,1,0:T(4,128)S(1)} %bitcast.41), channel_id=1, replica_groups=mesh['gx'=16,'gy'=4,'gz'=8] {'gx','gy','gz'}, dimensions={0} | all-to-all | bytes 2097152 | tf_op jit(solution)/shard_map/all_to_all | solution.py:362
  59.4 2.1 %shard_map.94 = f32[8,128]{1,0:T(8,128)S(1)} custom-call(f32[2048,128]{1,0:T(8,128)S(1)} %bitcast.37), custom_call_target="tpu_custom_call" | custom-call | tf_op jit(solution)/shard_map/pallas_call | solution.py:343
  61.5 0.6 broadcast_in_dim.8
  62.1 3.3 %all-to-all-start.1 = ((f32[4,8,128]{2,1,0:T(8,128)}), f32[4,8,128]{2,1,0:T(8,128)S(1)}, u32[]{:S(2)}, u32[]{:S(2)}) async-start(f32[4,8,128]{2,1,0:T(8,128)} %broadcast_in_dim.8), calls=%async_computation.1 | async-start | bytes 32768 | tf_op jit(solution)/shard_map/all_to_all | solution.py:386
  65.4 4.2 %all-to-all-done.1 = f32[4,8,128]{2,1,0:T(8,128)S(1)} async-done(((f32[4,8,128]{2,1,0:T(8,128)}), f32[4,8,128]{2,1,0:T(8,128)S(1)}, u32[]{:S(2)}, u32[]{:S(2)}) %all-to-all-start.1) | async-done | bytes 16416 | tf_op jit(solution)/shard_map/all_to_all | solution.py:386
  69.6 12.7 %shard_map.95 = f32[2048,128]{1,0:T(8,128)} custom-call(s32[1]{0:T(128)} %bitcast.comp_ref, f32[2048,128]{1,0:T(8,128)S(1)} %bitcast.38, f32[32,128]{1,0:T(8,128)S(1)} %bitcast.45), custom_call_target="tpu_custom_call" | custom-call | tf_op jit(solution)/shard_map/pallas_call | solution.py:343
  82.3 10.5 %all-to-all-start.2 = ((f32[512,4,128]{2,1,0:T(4,128)}), f32[512,4,128]{2,1,0:T(4,128)S(1)}, u32[]{:S(2)}, u32[]{:S(2)}) async-start(f32[512,4,128]{2,1,0:T(4,128)} %bitcast.7), calls=%async_computation.2 | async-start | bytes 2097152 | tf_op jit(solution)/shard_map/all_to_all | solution.py:362
  92.8 0.1 reshape_reshape.3
  92.9 32.9 %all-to-all-done.2 = f32[512,4,128]{2,1,0:T(4,128)S(1)} async-done(((f32[512,4,128]{2,1,0:T(4,128)}), f32[512,4,128]{2,1,0:T(4,128)S(1)}, u32[]{:S(2)}, u32[]{:S(2)}) %all-to-all-start.2) | async-done | bytes 1048608 | tf_op jit(solution)/shard_map/all_to_all | solution.py:362
  125.8 0.7 shard_map.96
  126.5 31.4 %all_to_all.26 = f32[512,2,128]{2,1,0:T(2,128)S(1)} all-to-all(f32[512,2,128]{2,1,0:T(2,128)S(1)} %bitcast.44), channel_id=1, replica_groups=mesh['gx'=16,'gy'=4,'gz'=8] {'gx','gy','gz'}, dimensions={0} | all-to-all | bytes 1048576 | tf_op jit(solution)/shard_map/all_to_all | solution.py:362
  157.9 1.0 shard_map.97
  158.9 10.1 %all-to-all-start.4 = ((f32[512,2,128]{2,1,0:T(2,128)}), f32[512,2,128]{2,1,0:T(2,128)S(1)}, u32[]{:S(2)}, u32[]{:S(2)}) async-start(f32[512,2,128]{2,1,0:T(2,128)} %bitcast.11), calls=%async_computation.4 | async-start | bytes 1048576 | tf_op jit(solution)/shard_map/all_to_all | solution.py:362
  169.1 0.1 copy.32
  169.2 21.6 %all-to-all-done.4 = f32[512,2,128]{2,1,0:T(2,128)S(1)} async-done(((f32[512,2,128]{2,1,0:T(2,128)}), f32[512,2,128]{2,1,0:T(2,128)S(1)}, u32[]{:S(2)}, u32[]{:S(2)}) %all-to-all-start.4) | async-done | bytes 524320 | tf_op jit(solution)/shard_map/all_to_all | solution.py:362
  190.7 15.3 %shard_map.98 = (f32[192,256]{1,0:T(8,128)S(1)}, f32[256,256]{1,0:T(8,128)}, f32[8,256]{1,0:T(8,128)S(1)}) custom-call(f32[1024,128]{1,0:T(8,128)S(1)} %bitcast.42, f32[2048,128]{1,0:T(8,128)S(1)} %bitcast.40), custom_call_target="tpu_custom_call" | custom-call | tf_op jit(solution)/shard_map/pallas_call | solution.py:343
  206.1 0.1 slice_reduce_fusion.3
  206.2 0.1 slice.60
  206.3 0.1 slice.62
  206.4 0.1 add.27
  206.5 0.1 squeeze.16
  206.6 0.7 copy.33
  207.3 0.0 copy-start
  207.3 0.0 copy-start.2
  207.3 0.7 reshape.98
  208.1 0.1 copy-done
  208.2 0.1 copy-done.2
  208.3 0.9 multiply_add_fusion
  (14 shorter events, 0.1 us)
Async XLA Ops:
  1.7 0.8 copy-start.3
  2.4 0.7 copy-start.4
  2.4 1.9 copy-start.1
  3.2 0.7 copy-start.5
  62.1 7.4 %all-to-all-start.1 = ((f32[4,8,128]{2,1,0:T(8,128)}), f32[4,8,128]{2,1,0:T(8,128)S(1)}, u32[]{:S(2)}, u32[]{:S(2)}) async-start(f32[4,8,128]{2,1,0:T(8,128)} %broadcast_in_dim.8), calls=%async_computation.1 | async-start | bytes 32768 | tf_op jit(solution)/shard_map/all_to_all | solution.py:386
  82.3 43.5 %all-to-all-start.2 = ((f32[512,4,128]{2,1,0:T(4,128)}), f32[512,4,128]{2,1,0:T(4,128)S(1)}, u32[]{:S(2)}, u32[]{:S(2)}) async-start(f32[512,4,128]{2,1,0:T(4,128)} %bitcast.7), calls=%async_computation.2 | async-start | bytes 2097152 | tf_op jit(solution)/shard_map/all_to_all | solution.py:362
  158.9 31.8 %all-to-all-start.4 = ((f32[512,2,128]{2,1,0:T(2,128)}), f32[512,2,128]{2,1,0:T(2,128)S(1)}, u32[]{:S(2)}, u32[]{:S(2)}) async-start(f32[512,2,128]{2,1,0:T(2,128)} %bitcast.11), calls=%async_computation.4 | async-start | bytes 1048576 | tf_op jit(solution)/shard_map/all_to_all | solution.py:362
  207.3 0.9 copy-start
  207.3 1.0 copy-start.2

commit v2 on v1

--- a/solution.py
+++ b/solution.py
@@ -15,6 +15,8 @@
 NODES = 64
 DEVICES = 512
 BLOCK = 32
+STIFF_LANE = 5
+MASS_LANE = 6
 
 
 def dot(a, b, contract=((1,), (0,))):
@@ -60,12 +62,26 @@
     return jnp.where(lane < 64, value, turned), jnp.where(lane < 64, turned, value)
 
 
-def x_up(here, above):
-    return jnp.where((iota(2) & 32) == 0, roll(here, 96), roll(above, 32))
-
-
-def x_down(here, below):
-    return jnp.where((iota(2) & 32) != 0, roll(here, 32), roll(below, 96))
+class Turned:
+    def __init__(self, ref):
+        self.ref = ref
+        self.planes = {}
+
+    def at(self, place):
+        if place not in self.planes:
+            if place in (0, 17):
+                zero = jnp.zeros((4, 8, 128), jnp.float32)
+                self.planes[place] = (zero, zero)
+            else:
+                here = self.ref[place]
+                self.planes[place] = (roll(here, 96), roll(here, 32))
+        return self.planes[place]
+
+    def sides(self, gx):
+        first = (iota(2) & 32) == 0
+        up = jnp.where(first, self.at(gx + 1)[0], self.at(gx + 2)[1])
+        down = jnp.where(first, self.at(gx)[0], self.at(gx + 1)[1])
+        return up, down
 
 
 def y_up(here):
@@ -88,82 +104,58 @@
     return jnp.where((iota(2) & 3) != 0, roll(here, 1), other)
 
 
-def around(ref, gx):
+def around(ref, turned, gx):
     here = ref[gx + 1]
-    return here, (
-        (x_up(here, ref[gx + 2]), x_down(here, ref[gx])),
-        (y_up(here), y_down(here)),
-        (z_up(here), z_down(here)),
-    )
+    return here, (turned.sides(gx), (y_up(here), y_down(here)), (z_up(here), z_down(here)))
 
 
 def load_tangents(rows_ref, tangent_ref):
-    tangent_ref[0] = jnp.zeros((4, 8, 128), jnp.float32)
-    tangent_ref[17] = jnp.zeros((4, 8, 128), jnp.float32)
-
-    def step(gx, carry):
+    for gx in range(16):
         tangent_ref[gx + 1] = both_halves(grid_row(rows_ref, 1, gx))[0]
-        return carry
-
-    lax.fori_loop(0, 16, step, 0, unroll=4)
-
-
-def edges_at(rows_ref, tangent_ref, gx):
-    first = tangent_ref[gx + 1]
+    return Turned(tangent_ref)
+
+
+def edges_at(rows_ref, turned, gx):
+    first = turned.ref[gx + 1]
+    above, below = turned.sides(gx)
     second = both_halves(grid_row(rows_ref, 1, gx))[1]
     third, mass = both_halves(grid_row(rows_ref, 2, gx))
     spring = grid_row(rows_ref, 3, gx)
-    ups = [
-        0.5 * (first + x_up(first, tangent_ref[gx + 2])),
-        0.5 * (second + y_up(second)),
-        0.5 * (third + z_up(third)),
-    ]
-    downs = [
-        0.5 * (first + x_down(first, tangent_ref[gx])),
-        0.5 * (second + y_down(second)),
-        0.5 * (third + z_down(third)),
-    ]
+    ups = [0.5 * (first + above), 0.5 * (second + y_up(second)), 0.5 * (third + z_up(third))]
+    downs = [0.5 * (first + below), 0.5 * (second + y_down(second)), 0.5 * (third + z_down(third))]
     total = (ups[0] + ups[1] + ups[2]) + (downs[0] + downs[1] + downs[2])
     return ups, downs, total, spring + total, mass
 
 
 def spectrum_kernel(rows_ref, out_ref, tangent_ref):
-    load_tangents(rows_ref, tangent_ref)
-
-    def step(gx, best):
-        _, _, total, diagonal, mass = edges_at(rows_ref, tangent_ref, gx)
-        return jnp.maximum(best, (diagonal + total) / mass)
-
-    best = lax.fori_loop(0, 16, step, jnp.zeros((4, 8, 128), jnp.float32), unroll=4)
+    turned = load_tangents(rows_ref, tangent_ref)
+    best = jnp.zeros((4, 8, 128), jnp.float32)
+    for gx in range(16):
+        _, _, total, diagonal, mass = edges_at(rows_ref, turned, gx)
+        best = jnp.maximum(best, (diagonal + total) / mass)
     best = jnp.max(jnp.max(best, axis=0), axis=(0, 1), keepdims=True)
-    out_ref[...] = jnp.broadcast_to(best, (8, 128))
+    out_ref[...] = jnp.broadcast_to(best, (32, 128))
 
 
 def filter_kernel(
     comp_ref, rows_ref, top_ref, out_ref, tangent_ref, even_ref, odd_ref, up_ref, down_ref,
     diagonal_ref, inverse_ref
 ):
-    load_tangents(rows_ref, tangent_ref)
+    turned = load_tangents(rows_ref, tangent_ref)
     top = jnp.max(jnp.max(top_ref[...], axis=0, keepdims=True), axis=1, keepdims=True)
     middle = top * 9.0 / 16.0
     spread = top * 7.0 / 16.0
     inverse_spread = 1.0 / spread
     ratio = middle * inverse_spread
-    for ref in (even_ref, odd_ref):
-        ref[0] = jnp.zeros((4, 8, 128), jnp.float32)
-        ref[17] = jnp.zeros((4, 8, 128), jnp.float32)
-
-    def prepare(gx, carry):
-        ups, downs, _, diagonal, mass = edges_at(rows_ref, tangent_ref, gx)
+
+    for gx in range(16):
+        ups, downs, _, diagonal, mass = edges_at(rows_ref, turned, gx)
         for direction in range(3):
             up_ref[direction, gx] = ups[direction]
             down_ref[direction, gx] = downs[direction]
         diagonal_ref[gx] = diagonal
         inverse_ref[gx] = inverse_spread / mass
         even_ref[gx + 1] = grid_row(rows_ref, 0, gx)
-        return carry
-
-    lax.fori_loop(0, 16, prepare, 0, unroll=4)
 
     def stiffness_times(here, sides, gx):
         result = diagonal_ref[gx] * here
@@ -172,56 +164,62 @@
             result = result - down_ref[direction, gx] * sides[direction][1]
         return result
 
-    def advance(current_ref, other_ref, first):
-        def step(gx, carry):
-            here, sides = around(current_ref, gx)
-            image = stiffness_times(here, sides, gx) * inverse_ref[gx] - ratio * here
-            if first:
-                other_ref[gx + 1] = image
-            else:
-                other_ref[gx + 1] = 2.0 * image - other_ref[gx + 1]
-            return carry
-
-        lax.fori_loop(0, 16, step, 0, unroll=4)
-
     for turn in range(ITERS):
         for repeat in range(DEGREE):
-            if repeat % 2 == 0:
-                advance(even_ref, odd_ref, repeat == 0)
-            else:
-                advance(odd_ref, even_ref, False)
+            current_ref, other_ref = (even_ref, odd_ref) if repeat % 2 == 0 else (odd_ref, even_ref)
+            turned = Turned(current_ref)
+            for gx in range(16):
+                here, sides = around(current_ref, turned, gx)
+                image = stiffness_times(here, sides, gx) * inverse_ref[gx] - ratio * here
+                if repeat > 0:
+                    image = 2.0 * image - other_ref[gx + 1]
+                other_ref[gx + 1] = image
 
     comp = comp_ref[0]
-
-    def finish(gx, carry):
-        here, sides = around(even_ref, gx)
+    turned = Turned(even_ref)
+    stiff_sum = jnp.zeros((4, 8, 128), jnp.float32)
+    mass_sum = jnp.zeros((4, 8, 128), jnp.float32)
+    for gx in range(16):
+        here, sides = around(even_ref, turned, gx)
         axial = [0.5 * (up - down) for up, down in sides]
         bending = [(up - 2.0 * here) + down for up, down in sides]
+        image = stiffness_times(here, sides, gx)
         values = [
             here,
-            stiffness_times(here, sides, gx),
-            jnp.where(comp == 0, axial[0], jnp.where(comp == 1, axial[1], axial[2])),
-            jnp.where(comp == 0, bending[2], jnp.where(comp == 1, bending[0], bending[1])),
+            image,
+            jnp.where(comp == 0, bending[2], jnp.where(comp == 1, axial[1], axial[2])),
+            jnp.where(comp == 0, axial[0], jnp.where(comp == 1, bending[0], bending[1])),
         ]
         for kind in range(4):
             out_ref[pl.ds(gx * 128 + kind, 32, stride=4), :] = values[kind].reshape(32, 128)
-        return carry
-
-    lax.fori_loop(0, 16, finish, 0, unroll=4)
-
-
-def local_rows(rows_ref, kind):
-    lane = lax.broadcasted_iota(jnp.int32, (128, 128), 1)
-    parts = []
-    for comp in range(3):
-        parts.append(
-            jnp.concatenate(
-                [rows_ref[pl.ds((gx * 4 + comp) * 32 + kind, 8, stride=4), :] for gx in range(16)],
-                axis=0,
-            )
+        stiff_sum = stiff_sum + here * image
+        mass_sum = mass_sum + here * both_halves(grid_row(rows_ref, 2, gx))[1]
+    lane = lax.broadcasted_iota(jnp.int32, (1, 128), 1)
+    sums = []
+    for value in (stiff_sum, mass_sum):
+        value = jnp.sum(jnp.sum(value, axis=0), axis=0, keepdims=True)
+        low = jnp.sum(jnp.where(lane < 64, value, 0.0), axis=1, keepdims=True)
+        high = jnp.sum(jnp.where(lane < 64, 0.0, value), axis=1, keepdims=True)
+        sums.append(jnp.where(lane < 64, low, high))
+    for gx in range(16):
+        rows = pl.ds(gx * 128 + 2, 32, stride=4)
+        value = jnp.where((lane & 63) == STIFF_LANE, sums[0], out_ref[rows, :])
+        out_ref[rows, :] = jnp.where((lane & 63) == MASS_LANE, sums[1], value)
+
+
+def parts_of(rows_ref, kind):
+    return [
+        jnp.concatenate(
+            [rows_ref[pl.ds((gx * 4 + comp) * 32 + kind, 8, stride=4), :] for gx in range(16)],
+            axis=0,
         )
+        for comp in range(3)
+    ]
+
+
+def by_vector(parts):
+    low = lax.broadcasted_iota(jnp.int32, (128, 128), 1) < 64
     turned = [pltpu.roll(part, 64, 1) for part in parts]
-    low = lane < 64
     upper = [jnp.where(low, parts[0], turned[1]), jnp.where(low, parts[2], 0.0)]
     lower = [jnp.where(low, turned[0], parts[1]), jnp.where(low, turned[2], 0.0)]
     return jnp.concatenate(
@@ -229,29 +227,41 @@
     )
 
 
+def one_lane(part, place):
+    return jnp.concatenate(
+        [jnp.broadcast_to(part[:, at : at + 1], (128, 128)) for at in (place, 64 + place)], axis=0
+    )
+
+
+def untucked(vectors, mixed):
+    lane = lax.broadcasted_iota(jnp.int32, (128, 128), 1) & 63
+    fixed = []
+    for comp in range(3):
+        here = vectors[comp]
+        step = 4 if comp == 1 else 1
+        above = pltpu.roll(here, 128 - step, 1)
+        below = pltpu.roll(here, step, 1)
+        value = (above - 2.0 * here) + below if comp == 0 else 0.5 * (above - below)
+        held = (lane == STIFF_LANE) | (lane == MASS_LANE)
+        fixed.append(jnp.where(held, value, mixed[comp]))
+    return fixed
+
+
 def product_kernel(rows_ref, mass_ref, out_ref):
-    vectors = local_rows(rows_ref, 0)
-    image = local_rows(rows_ref, 1)
-    weighted = vectors * mass_ref[...]
-    gram = dot(weighted, vectors, ((1,), (1,)))
+    vectors = by_vector(parts_of(rows_ref, 0))
+    image = by_vector(parts_of(rows_ref, 1))
+    gram = dot(vectors * mass_ref[...], vectors, ((1,), (1,)))
     stiff = dot(vectors, image, ((1,), (1,)))
     row = lax.broadcasted_iota(jnp.int32, (256, 256), 0)
     column = lax.broadcasted_iota(jnp.int32, (256, 256), 1)
     both = jnp.where(row >= column, gram, stiff)
-    diagonal = jnp.sum(vectors * image, axis=1, keepdims=True)
-    lane = lax.broadcasted_iota(jnp.int32, (256, 256), 1)
-    lateral = jnp.sum(jnp.where(lane < NODES, weighted, 0.0), axis=1, keepdims=True)
-    out_ref[pl.ds(0, 256, stride=2), :] = both[:, :128]
-    out_ref[pl.ds(512, 256, stride=2), :] = both[:, 128:]
-    out_ref[pl.ds(1, 256, stride=2), :] = jnp.broadcast_to(diagonal, (256, 128))
-    out_ref[pl.ds(513, 256, stride=2), :] = jnp.broadcast_to(lateral, (256, 128))
+    out_ref[:256, :] = both[:, :128]
+    out_ref[256:, :] = both[:, 128:]
 
 
 def total_kernel(rows_ref, out_ref):
-    total = jnp.sum(rows_ref[...].reshape(128, 8, 128), axis=0)
-    total = total + pltpu.roll(total, 2, 0)
-    total = total + pltpu.roll(total, 4, 0)
-    out_ref[...] = jnp.broadcast_to(total[None], (128, 8, 128)).reshape(1024, 128)
+    total = jnp.sum(jnp.sum(rows_ref[...].reshape(64, 8, 128), axis=0), axis=0, keepdims=True)
+    out_ref[...] = jnp.broadcast_to(total, (512, 128))
 
 
 def factor_block(gram, stiff):
@@ -288,12 +298,11 @@
 
 
 def final_kernel(sums_ref, rows_ref, subspace_ref, projected_ref, fields_ref, a_ref, e_ref):
-    both = jnp.concatenate(
-        [sums_ref[pl.ds(0, 256, stride=2), :], sums_ref[pl.ds(512, 256, stride=2), :]], axis=1
-    )
-    diagonal = sums_ref[pl.ds(1, 256, stride=2), :]
+    both = jnp.concatenate([sums_ref[:256, :], sums_ref[256:, :]], axis=1)
+    mixed = parts_of(rows_ref, 2)
+    diagonal = one_lane(mixed[0] + mixed[1] + mixed[2], STIFF_LANE)
     diagonal = jnp.concatenate([diagonal, diagonal], axis=1)
-    lateral = sums_ref[pl.ds(513, 256, stride=2), :]
+    lateral = one_lane(mixed[0], MASS_LANE)
     turned = both.T
     row = lax.broadcasted_iota(jnp.int32, (256, 256), 0)
     column = lax.broadcasted_iota(jnp.int32, (256, 256), 1)
@@ -327,14 +336,18 @@
                 e_ref[m, after:, known] = e_ref[m, after:, known] - dot(factor, e_rows)
     lower = e_ref[0]
     stiff_lower = e_ref[1]
-    vectors = local_rows(rows_ref, 0)
+    parts = parts_of(rows_ref, 0)
+    vectors = by_vector(parts)
+    mixed = untucked(parts, mixed)
+    other = parts_of(rows_ref, 3)
     subspace = dot(vectors.T, lower, ((1,), (1,)))
     subspace_ref[...] = subspace[: 3 * NODES] * jnp.sqrt(jnp.float32(DEVICES * 3 * NODES))
     projected_ref[...] = dot(lower, dot(stiff, lower, ((1,), (1,))))
     weights = dot(stiff_lower.T, dot(stiff_lower, lateral))
     weights = jnp.concatenate([weights, weights], axis=1)
-    for place, kind in enumerate((0, 2, 3)):
-        value = vectors if kind == 0 else local_rows(rows_ref, kind)
+    axial = by_vector([other[0], mixed[1], mixed[2]])
+    bending = by_vector([mixed[0], other[1], other[2]])
+    for place, value in enumerate((vectors, axial, bending)):
         fields_ref[place : place + 1, :] = jnp.sum(value * weights, axis=0, keepdims=True)
     fields_ref[3:, :] = jnp.zeros((5, 256), jnp.float32)
 
@@ -382,9 +395,9 @@
         pack_kernel, rows_of(2048), operands=(start_block.reshape(3 * NODES, width), coefficients)
     )
     gathered = exchange(sent, 4)
-    own_top = call(spectrum_kernel, rows_of(8), (padded,), operands=(gathered,))
+    own_top = call(spectrum_kernel, rows_of(32), (padded,), operands=(gathered,))
     tops = lax.all_to_all(
-        jnp.broadcast_to(own_top[None], (4, 8, 128)), "gy", 0, 0, tiled=True
+        own_top.reshape(4, 8, 128), "gy", 0, 0, tiled=True
     ).reshape(32, 128)
     component = lax.axis_index("gy").astype(jnp.int32).reshape(1)
     filtered = call(
@@ -404,8 +417,8 @@
     )
     returned = exchange(filtered, 4)
     mass_row = jnp.pad(mass.reshape(1, 3 * NODES), ((0, 0), (0, NODES)))
-    products = call(product_kernel, rows_of(1024), operands=(returned, mass_row))
-    totals = call(total_kernel, rows_of(1024), operands=(exchange(products, 2),))
+    products = call(product_kernel, rows_of(512), operands=(returned, mass_row))
+    totals = call(total_kernel, rows_of(512), operands=(exchange(products, 1),))
     subspace, projected, fields = call(
         final_kernel,
         (
@@ -417,7 +430,7 @@
             pltpu.VMEM((2, 256, 256), jnp.float32),
             pltpu.VMEM((2, 256, 256), jnp.float32),
         ),
-        operands=(exchange(totals, 2), returned),
+        operands=(exchange(totals, 1), returned),
     )
     place = node_mass.shape[1:]
     fields = fields[:3, : 3 * NODES].reshape((3, 3) + place)

time: 210 us -> 195 us (0.929)
  waiting for transfers between devices: 58.6 us -> 53.5 us
  blocking collectives: 86.2 us -> 81.5 us
  Pallas kernels: 32 us -> 28.1 us
    all_to_all x2, waiting for transfers between devices: 54.4 us -> 49.3 us  [exchange(): return lax.all_to_all(blocks, AXES, 0, 0, tiled=True).reshape(rows.shape)]
    all_to_all x2, blocking collectives: 86.2 us -> 81.5 us  [exchange(): return lax.all_to_all(blocks, AXES, 0, 0, tiled=True).reshape(rows.shape)]
    pallas_call x6, Pallas kernels: 32 us -> 28.1 us  [call(): pl.pallas_call(kernel, out_shape=shape, in_specs=[pl.BlockSpec(memory_spa...]
where the time goes in v2:
time: 195 us
  blocking collectives  81.5 us (42%)
  waiting for transfers between devices  53.5 us (27%)
  Pallas kernels  28.1 us (14%)
  starting transfers between devices  23.6 us (12%)
  local copies, waits for them, and re-layouts  4.96 us (3%)
  other arithmetic  2.08 us (1%)
    all_to_all x2, blocking collectives, exchange(): return lax.all_to_all(blocks, AXES, 0, 0, tiled=True).reshape(rows.shape)  81.5 us
    all_to_all x2, waiting for transfers between devices, exchange(): return lax.all_to_all(blocks, AXES, 0, 0, tiled=True).reshape(rows.shape)  49.3 us
    pallas_call x6, Pallas kernels, call(): pl.pallas_call(kernel, out_shape=shape, in_specs=[pl.BlockSpec(memory_spa...  28.1 us
    all_to_all x2, starting transfers between devices, exchange(): return lax.all_to_all(blocks, AXES, 0, 0, tiled=True).reshape(rows.shape)  20.3 us
    all_to_all x1, waiting for transfers between devices, on_device(): lax.all_to_all(own_top.reshape(4, 8, 128), 'gy', 0, 0, tiled=True)  4.17 us
  transfers between devices with their start and end apart: 3, of which 3 were waited for; matrix products, arithmetic and copies ran while one was open for 0% of the time, Pallas kernels for 0%

profile of v2, /device:TPU:1, one launch (start us, length us, event | category | flops | bytes accessed | tf_op | source)
XLA Modules:
  0.0 194.5 jit_solution(6870644330357264756)
XLA Ops:
  0.6 1.0 convert_reduce_fusion
  1.7 0.0 copy-start.3
  1.7 0.1 copy.23
  1.8 0.6 copy-done.3
  2.4 0.0 copy-start.4
  2.4 0.0 copy-start.1
  2.5 0.1 copy.24
  2.6 0.1 squeeze.13
  2.7 0.1 copy.25
  2.8 0.1 squeeze.14
  2.9 0.1 copy.26
  3.0 0.1 squeeze.15
  3.1 0.1 copy-done.4
  3.1 0.1 copy.27
  3.2 0.0 copy-start.5
  3.3 0.1 reshape.88
  3.3 0.6 copy-done.5
  4.0 0.1 copy.28
  4.1 0.1 reshape.89
  4.2 0.1 maximum_bitcast_fusion.2
  4.2 0.1 maximum_bitcast_fusion
  4.3 0.0 copy-done.1
  4.3 0.1 reshape.87.start_ref
  4.4 0.1 shard_map.93
  4.6 54.8 %all_to_all.25 = f32[512,4,128]{2,1,0:T(4,128)S(1)} all-to-all(f32[512,4,128]{2,1,0:T(4,128)S(1)} %bitcast.46), channel_id=1, replica_groups=mesh['gx'=16,'gy'=4,'gz'=8] {'gx','gy','gz'}, dimensions={0} | all-to-all | bytes 2097152 | tf_op jit(solution)/shard_map/all_to_all | solution.py:375
  59.4 2.5 %shard_map.94 = f32[32,128]{1,0:T(8,128)} custom-call(f32[2048,128]{1,0:T(8,128)S(1)} %bitcast.44), custom_call_target="tpu_custom_call" | custom-call | tf_op jit(solution)/shard_map/pallas_call | solution.py:356
  61.8 3.3 %all-to-all-start.1 = ((f32[4,8,128]{2,1,0:T(8,128)}), f32[4,8,128]{2,1,0:T(8,128)S(1)}, u32[]{:S(2)}, u32[]{:S(2)}) async-start(f32[4,8,128]{2,1,0:T(8,128)} %bitcast.6), calls=%async_computation.1 | async-start | bytes 32768 | tf_op jit(solution)/shard_map/all_to_all | solution.py:399
  65.1 4.2 %all-to-all-done.1 = f32[4,8,128]{2,1,0:T(8,128)S(1)} async-done(((f32[4,8,128]{2,1,0:T(8,128)}), f32[4,8,128]{2,1,0:T(8,128)S(1)}, u32[]{:S(2)}, u32[]{:S(2)}) %all-to-all-start.1) | async-done | bytes 16416 | tf_op jit(solution)/shard_map/all_to_all | solution.py:399
  69.3 8.9 %shard_map.95 = f32[2048,128]{1,0:T(8,128)} custom-call(s32[1]{0:T(128)} %bitcast.comp_ref, f32[2048,128]{1,0:T(8,128)S(1)} %bitcast.45, f32[32,128]{1,0:T(8,128)S(1)} %bitcast.50), custom_call_target="tpu_custom_call" | custom-call | tf_op jit(solution)/shard_map/pallas_call | solution.py:356
  78.2 10.7 %all-to-all-start.2 = ((f32[512,4,128]{2,1,0:T(4,128)}), f32[512,4,128]{2,1,0:T(4,128)S(1)}, u32[]{:S(2)}, u32[]{:S(2)}) async-start(f32[512,4,128]{2,1,0:T(4,128)} %bitcast.8), calls=%async_computation.2 | async-start | bytes 2097152 | tf_op jit(solution)/shard_map/all_to_all | solution.py:375
  88.9 0.1 reshape_reshape.3
  89.0 32.9 %all-to-all-done.2 = f32[512,4,128]{2,1,0:T(4,128)S(1)} async-done(((f32[512,4,128]{2,1,0:T(4,128)}), f32[512,4,128]{2,1,0:T(4,128)S(1)}, u32[]{:S(2)}, u32[]{:S(2)}) %all-to-all-start.2) | async-done | bytes 1048608 | tf_op jit(solution)/shard_map/all_to_all | solution.py:375
  121.9 0.7 shard_map.96
  122.6 26.6 %all_to_all.26 = f32[512,1,128]{2,1,0:T(1,128)S(1)} all-to-all(f32[512,1,128]{2,1,0:T(1,128)S(1)} %bitcast.49), channel_id=1, replica_groups=mesh['gx'=16,'gy'=4,'gz'=8] {'gx','gy','gz'}, dimensions={0} | all-to-all | bytes 524288 | tf_op jit(solution)/shard_map/all_to_all | solution.py:375
  149.3 0.8 shard_map.97
  150.1 9.6 %all-to-all-start.4 = ((f32[512,1,128]{2,1,0:T(1,128)}), f32[512,1,128]{2,1,0:T(1,128)S(1)}, u32[]{:S(2)}, u32[]{:S(2)}) async-start(f32[512,1,128]{2,1,0:T(1,128)} %bitcast.14), calls=%async_computation.4 | async-start | bytes 524288 | tf_op jit(solution)/shard_map/all_to_all | solution.py:375
  159.7 0.1 copy.34
  159.8 16.5 %all-to-all-done.4 = f32[512,1,128]{2,1,0:T(1,128)S(1)} async-done(((f32[512,1,128]{2,1,0:T(1,128)}), f32[512,1,128]{2,1,0:T(1,128)S(1)}, u32[]{:S(2)}, u32[]{:S(2)}) %all-to-all-start.4) | async-done | bytes 262176 | tf_op jit(solution)/shard_map/all_to_all | solution.py:375
  176.3 15.1 %shard_map.98 = (f32[192,256]{1,0:T(8,128)S(1)}, f32[256,256]{1,0:T(8,128)}, f32[8,256]{1,0:T(8,128)S(1)}) custom-call(f32[512,128]{1,0:T(8,128)S(1)} %bitcast.47, f32[2048,128]{1,0:T(8,128)S(1)} %bitcast.43), custom_call_target="tpu_custom_call" | custom-call | tf_op jit(solution)/shard_map/pallas_call | solution.py:356
  191.4 0.1 slice_reduce_fusion.3
  191.5 0.1 slice.60
  191.6 0.1 slice.62
  191.7 0.1 add.27
  191.8 0.1 squeeze.16
  192.0 0.7 copy.35
  192.7 0.0 copy-start
  192.7 0.0 copy-start.2
  192.7 0.7 reshape.101
  193.4 0.1 copy-done
  193.5 0.1 copy-done.2
  193.6 0.9 multiply_add_fusion
  (14 shorter events, 0.1 us)
Async XLA Ops:
  1.7 0.8 copy-start.3
  2.4 0.7 copy-start.4
  2.4 1.9 copy-start.1
  3.2 0.7 copy-start.5
  61.8 7.4 %all-to-all-start.1 = ((f32[4,8,128]{2,1,0:T(8,128)}), f32[4,8,128]{2,1,0:T(8,128)S(1)}, u32[]{:S(2)}, u32[]{:S(2)}) async-start(f32[4,8,128]{2,1,0:T(8,128)} %bitcast.6), calls=%async_computation.1 | async-start | bytes 32768 | tf_op jit(solution)/shard_map/all_to_all | solution.py:399
  78.2 43.7 %all-to-all-start.2 = ((f32[512,4,128]{2,1,0:T(4,128)}), f32[512,4,128]{2,1,0:T(4,128)S(1)}, u32[]{:S(2)}, u32[]{:S(2)}) async-start(f32[512,4,128]{2,1,0:T(4,128)} %bitcast.8), calls=%async_computation.2 | async-start | bytes 2097152 | tf_op jit(solution)/shard_map/all_to_all | solution.py:375
  150.1 26.2 %all-to-all-start.4 = ((f32[512,1,128]{2,1,0:T(1,128)}), f32[512,1,128]{2,1,0:T(1,128)S(1)}, u32[]{:S(2)}, u32[]{:S(2)}) async-start(f32[512,1,128]{2,1,0:T(1,128)} %bitcast.14), calls=%async_computation.4 | async-start | bytes 524288 | tf_op jit(solution)/shard_map/all_to_all | solution.py:375
  192.7 0.9 copy-start
  192.7 1.0 copy-start.2

commit v3 on v2

--- a/solution.py
+++ b/solution.py
@@ -5,15 +5,18 @@
 from jax import lax
 from jax.experimental import pallas as pl
 from jax.experimental.pallas import tpu as pltpu
-from jax.sharding import PartitionSpec as P
+from jax.sharding import Mesh, PartitionSpec as P
 
 DEGREE = 4
 ITERS = 2
 PRECISE = lax.Precision.HIGHEST
-AXES = ("gx", "gy", "gz")
+GX = ("cy", "core")
+AXES = ("cy", "core", "gy", "gz")
+CHIPS = ("cy", "gy", "gz")
 
 NODES = 64
 DEVICES = 512
+OUT_ROWS = 5
 BLOCK = 32
 STIFF_LANE = 5
 MASS_LANE = 6
@@ -37,19 +40,22 @@
             jnp.broadcast_to(coef_ref[source * 3 + r : source * 3 + r + 1, :], (8, 128))
             for r in range(3)
         ]
-        for gx in range(16):
-            first = (gx * 4 + comp) * 32
-            out_ref[pl.ds(first, 8, stride=4), :] = pairs[gx * 8 : gx * 8 + 8]
+        for cy in range(8):
+            first = (cy * 4 + comp) * 8 * OUT_ROWS
+            for core in range(2):
+                at = (cy * 2 + core) * 8
+                out_ref[pl.ds(first + core, 8, stride=OUT_ROWS), :] = pairs[at : at + 8]
             for r in range(3):
-                out_ref[pl.ds(first + r + 1, 8, stride=4), :] = rows[r]
+                out_ref[pl.ds(first + 2 + r, 8, stride=OUT_ROWS), :] = rows[r]
 
 
 def iota(axis):
     return lax.broadcasted_iota(jnp.int32, (4, 8, 128), axis)
 
 
-def grid_row(ref, kind, gx):
-    return ref[pl.ds(gx * 128 + kind, 32, stride=4), :].reshape(4, 8, 128)
+def grid_row(refs, kind, gx, core):
+    rows = [ref[pl.ds(gx // 2 * 32 * OUT_ROWS + kind, 32, stride=OUT_ROWS), :] for ref in refs]
+    return jnp.where(core == gx % 2, rows[0], rows[1]).reshape(4, 8, 128)
 
 
 def roll(value, shift, axis=2):
@@ -67,20 +73,20 @@
         self.ref = ref
         self.planes = {}
 
-    def at(self, place):
-        if place not in self.planes:
-            if place in (0, 17):
+    def at(self, gx):
+        if gx not in self.planes:
+            if gx in (-1, 16):
                 zero = jnp.zeros((4, 8, 128), jnp.float32)
-                self.planes[place] = (zero, zero)
+                self.planes[gx] = (zero, zero)
             else:
-                here = self.ref[place]
-                self.planes[place] = (roll(here, 96), roll(here, 32))
-        return self.planes[place]
+                here = self.ref[gx]
+                self.planes[gx] = (roll(here, 96), roll(here, 32))
+        return self.planes[gx]
 
     def sides(self, gx):
         first = (iota(2) & 32) == 0
-        up = jnp.where(first, self.at(gx + 1)[0], self.at(gx + 2)[1])
-        down = jnp.where(first, self.at(gx)[0], self.at(gx + 1)[1])
+        up = jnp.where(first, self.at(gx)[0], self.at(gx + 1)[1])
+        down = jnp.where(first, self.at(gx - 1)[0], self.at(gx)[1])
         return up, down
 
 
@@ -105,57 +111,62 @@
 
 
 def around(ref, turned, gx):
-    here = ref[gx + 1]
+    here = ref[gx]
     return here, (turned.sides(gx), (y_up(here), y_down(here)), (z_up(here), z_down(here)))
 
 
-def load_tangents(rows_ref, tangent_ref):
+def weights_kernel(
+    core_ref, own_ref, other_ref, vectors_ref, up_ref, down_ref, diagonal_ref, mass_ref, top_ref,
+    tangent_ref
+):
+    core = core_ref[0]
+    refs = (own_ref, other_ref)
+    second = []
     for gx in range(16):
-        tangent_ref[gx + 1] = both_halves(grid_row(rows_ref, 1, gx))[0]
-    return Turned(tangent_ref)
-
-
-def edges_at(rows_ref, turned, gx):
-    first = turned.ref[gx + 1]
-    above, below = turned.sides(gx)
-    second = both_halves(grid_row(rows_ref, 1, gx))[1]
-    third, mass = both_halves(grid_row(rows_ref, 2, gx))
-    spring = grid_row(rows_ref, 3, gx)
-    ups = [0.5 * (first + above), 0.5 * (second + y_up(second)), 0.5 * (third + z_up(third))]
-    downs = [0.5 * (first + below), 0.5 * (second + y_down(second)), 0.5 * (third + z_down(third))]
-    total = (ups[0] + ups[1] + ups[2]) + (downs[0] + downs[1] + downs[2])
-    return ups, downs, total, spring + total, mass
-
-
-def spectrum_kernel(rows_ref, out_ref, tangent_ref):
-    turned = load_tangents(rows_ref, tangent_ref)
+        vectors_ref[gx] = grid_row(refs, core, gx, core)
+        first, along_y = both_halves(grid_row(refs, 2, gx, core))
+        tangent_ref[gx] = first
+        second.append(along_y)
+    turned = Turned(tangent_ref)
     best = jnp.zeros((4, 8, 128), jnp.float32)
     for gx in range(16):
-        _, _, total, diagonal, mass = edges_at(rows_ref, turned, gx)
+        first = tangent_ref[gx]
+        above, below = turned.sides(gx)
+        third, mass = both_halves(grid_row(refs, 3, gx, core))
+        spring = grid_row(refs, 4, gx, core)
+        ups = [
+            0.5 * (first + above),
+            0.5 * (second[gx] + y_up(second[gx])),
+            0.5 * (third + z_up(third)),
+        ]
+        downs = [
+            0.5 * (first + below),
+            0.5 * (second[gx] + y_down(second[gx])),
+            0.5 * (third + z_down(third)),
+        ]
+        total = (ups[0] + ups[1] + ups[2]) + (downs[0] + downs[1] + downs[2])
+        for direction in range(3):
+            up_ref[direction, gx] = ups[direction]
+            down_ref[direction, gx] = downs[direction]
+        diagonal = spring + total
+        diagonal_ref[gx] = diagonal
+        mass_ref[gx] = mass
         best = jnp.maximum(best, (diagonal + total) / mass)
     best = jnp.max(jnp.max(best, axis=0), axis=(0, 1), keepdims=True)
-    out_ref[...] = jnp.broadcast_to(best, (32, 128))
+    top_ref[...] = jnp.broadcast_to(best, (32, 128))
 
 
 def filter_kernel(
-    comp_ref, rows_ref, top_ref, out_ref, tangent_ref, even_ref, odd_ref, up_ref, down_ref,
-    diagonal_ref, inverse_ref
+    comp_ref, vectors_ref, up_ref, down_ref, diagonal_ref, mass_ref, top_ref, out_ref, even_ref,
+    odd_ref, inverse_ref
 ):
-    turned = load_tangents(rows_ref, tangent_ref)
     top = jnp.max(jnp.max(top_ref[...], axis=0, keepdims=True), axis=1, keepdims=True)
     middle = top * 9.0 / 16.0
     spread = top * 7.0 / 16.0
     inverse_spread = 1.0 / spread
     ratio = middle * inverse_spread
-
     for gx in range(16):
-        ups, downs, _, diagonal, mass = edges_at(rows_ref, turned, gx)
-        for direction in range(3):
-            up_ref[direction, gx] = ups[direction]
-            down_ref[direction, gx] = downs[direction]
-        diagonal_ref[gx] = diagonal
-        inverse_ref[gx] = inverse_spread / mass
-        even_ref[gx + 1] = grid_row(rows_ref, 0, gx)
+        inverse_ref[gx] = inverse_spread / mass_ref[gx]
 
     def stiffness_times(here, sides, gx):
         result = diagonal_ref[gx] * here
@@ -167,13 +178,17 @@
     for turn in range(ITERS):
         for repeat in range(DEGREE):
             current_ref, other_ref = (even_ref, odd_ref) if repeat % 2 == 0 else (odd_ref, even_ref)
+            earlier_ref = other_ref
+            if turn == 0:
+                current_ref = vectors_ref if repeat == 0 else current_ref
+                earlier_ref = vectors_ref if repeat == 1 else earlier_ref
             turned = Turned(current_ref)
             for gx in range(16):
                 here, sides = around(current_ref, turned, gx)
                 image = stiffness_times(here, sides, gx) * inverse_ref[gx] - ratio * here
                 if repeat > 0:
-                    image = 2.0 * image - other_ref[gx + 1]
-                other_ref[gx + 1] = image
+                    image = 2.0 * image - earlier_ref[gx]
+                other_ref[gx] = image
 
     comp = comp_ref[0]
     turned = Turned(even_ref)
@@ -193,7 +208,7 @@
         for kind in range(4):
             out_ref[pl.ds(gx * 128 + kind, 32, stride=4), :] = values[kind].reshape(32, 128)
         stiff_sum = stiff_sum + here * image
-        mass_sum = mass_sum + here * both_halves(grid_row(rows_ref, 2, gx))[1]
+        mass_sum = mass_sum + here * mass_ref[gx]
     lane = lax.broadcasted_iota(jnp.int32, (1, 128), 1)
     sums = []
     for value in (stiff_sum, mass_sum):
@@ -259,9 +274,9 @@
     out_ref[256:, :] = both[:, 128:]
 
 
-def total_kernel(rows_ref, out_ref):
-    total = jnp.sum(jnp.sum(rows_ref[...].reshape(64, 8, 128), axis=0), axis=0, keepdims=True)
-    out_ref[...] = jnp.broadcast_to(total, (512, 128))
+def total_kernel(count, copies, rows_ref, out_ref):
+    total = jnp.sum(rows_ref[...].reshape(count, 16, 128), axis=0)
+    out_ref[...] = jnp.broadcast_to(total[None], (copies, 16, 128)).reshape(copies * 16, 128)
 
 
 def factor_block(gram, stiff):
@@ -370,9 +385,13 @@
     return jax.ShapeDtypeStruct((count, 128), jnp.float32)
 
 
-def exchange(rows, per_device):
-    blocks = rows.reshape(DEVICES, per_device, 128)
-    return lax.all_to_all(blocks, AXES, 0, 0, tiled=True).reshape(rows.shape)
+def exchange(rows, axes, devices):
+    per_device = rows.shape[0] // devices
+    if per_device % 8 == 0:
+        blocks = rows.reshape(devices, per_device, 128)
+    else:
+        blocks = rows.reshape(devices, per_device, 1, 128)
+    return lax.all_to_all(blocks, axes, 0, 0, tiled=True).reshape(rows.shape)
 
 
 def on_device(start_block, node_mass, ground_spring, stiffness, yield_flags, stress_old):
@@ -389,36 +408,47 @@
         ],
         axis=1,
     ).reshape(9, 128)
-    padded = pltpu.VMEM((18, 4, 8, 128), jnp.float32)
-    plain = pltpu.VMEM((16, 4, 8, 128), jnp.float32)
+    grid_shape = (16, 4, 8, 128)
+    plain = pltpu.VMEM(grid_shape, jnp.float32)
+    grid = jax.ShapeDtypeStruct(grid_shape, jnp.float32)
+    grids = jax.ShapeDtypeStruct((3,) + grid_shape, jnp.float32)
     sent = call(
-        pack_kernel, rows_of(2048), operands=(start_block.reshape(3 * NODES, width), coefficients)
-    )
-    gathered = exchange(sent, 4)
-    own_top = call(spectrum_kernel, rows_of(32), (padded,), operands=(gathered,))
-    tops = lax.all_to_all(
-        own_top.reshape(4, 8, 128), "gy", 0, 0, tiled=True
-    ).reshape(32, 128)
+        pack_kernel,
+        rows_of(256 * OUT_ROWS),
+        operands=(start_block.reshape(3 * NODES, width), coefficients),
+    )
+    own = exchange(sent, CHIPS, 256)
+    other = lax.ppermute(own, "core", [(0, 1), (1, 0)])
+    core = lax.axis_index("core").astype(jnp.int32).reshape(1)
     component = lax.axis_index("gy").astype(jnp.int32).reshape(1)
+    *weights, own_top = call(
+        weights_kernel,
+        (grid, grids, grids, grid, grid, rows_of(32)),
+        (plain,),
+        smem=(0,),
+        operands=(core, own, other),
+    )
+    tops = exchange(own_top, "gy", 4)
     filtered = call(
         filter_kernel,
         rows_of(2048),
-        (
-            padded,
-            padded,
-            padded,
-            pltpu.VMEM((3, 16, 4, 8, 128), jnp.float32),
-            pltpu.VMEM((3, 16, 4, 8, 128), jnp.float32),
-            plain,
-            plain,
-        ),
+        (plain, plain, plain),
         smem=(0,),
-        operands=(component, gathered, tops),
-    )
-    returned = exchange(filtered, 4)
+        operands=(component, *weights, tops),
+    )
+    returned = exchange(filtered, AXES, DEVICES)
     mass_row = jnp.pad(mass.reshape(1, 3 * NODES), ((0, 0), (0, NODES)))
     products = call(product_kernel, rows_of(512), operands=(returned, mass_row))
-    totals = call(total_kernel, rows_of(512), operands=(exchange(products, 1),))
+    partial = call(
+        functools.partial(total_kernel, 32, 16),
+        rows_of(256),
+        operands=(exchange(products, ("cy", "gy"), 32),),
+    )
+    totals = call(
+        functools.partial(total_kernel, 16, 32),
+        rows_of(512),
+        operands=(exchange(partial, ("core", "gz"), 16),),
+    )
     subspace, projected, fields = call(
         final_kernel,
         (
@@ -430,7 +460,7 @@
             pltpu.VMEM((2, 256, 256), jnp.float32),
             pltpu.VMEM((2, 256, 256), jnp.float32),
         ),
-        operands=(exchange(totals, 1), returned),
+        operands=(exchange(totals, ("cy", "gy"), 32), returned),
     )
     place = node_mass.shape[1:]
     fields = fields[:3, : 3 * NODES].reshape((3, 3) + place)
@@ -446,22 +476,23 @@
 
 
 def solution(mesh):
+    chips = Mesh(mesh.devices.reshape(8, 2, 4, 8), AXES)
     return jax.shard_map(
         on_device,
-        mesh=mesh,
+        mesh=chips,
         in_specs=(
-            P(None, "gx", "gy", "gz", None),
-            P(None, "gx", "gy", "gz"),
-            P(None, "gx", "gy", "gz"),
-            P(None, None, "gx", "gy", "gz"),
-            P(None, None, "gx", "gy", "gz"),
-            P(None, None, "gx", "gy", "gz"),
+            P(None, GX, "gy", "gz", None),
+            P(None, GX, "gy", "gz"),
+            P(None, GX, "gy", "gz"),
+            P(None, None, GX, "gy", "gz"),
+            P(None, None, GX, "gy", "gz"),
+            P(None, None, GX, "gy", "gz"),
         ),
         out_specs=(
-            P(None, "gx", "gy", "gz", None),
+            P(None, GX, "gy", "gz", None),
             P(),
-            P(None, "gx", "gy", "gz"),
-            P(None, None, "gx", "gy", "gz"),
+            P(None, GX, "gy", "gz"),
+            P(None, None, GX, "gy", "gz"),
         ),
         check_vma=False,
     )

time: 195 us -> 182 us (0.933); the launches traced: 195 us -> 179 us
  blocking collectives: 81.5 us -> 72.6 us
  waiting for transfers between devices: 53.5 us -> 49.2 us
  Pallas kernels: 28.1 us -> 26 us
    all_to_all x2 -> x3, blocking collectives: 81.5 us -> 72.6 us  [exchange(): return lax.all_to_all(blocks, axes, 0, 0, tiled=True).reshape(rows.shape)]
    all_to_all x3, waiting for transfers between devices: 53.5 us -> 47.5 us  [exchange(): return lax.all_to_all(blocks, axes, 0, 0, tiled=True).reshape(rows.shape)]
    all_to_all x3, starting transfers between devices: 23.6 us -> 17.8 us  [exchange(): return lax.all_to_all(blocks, axes, 0, 0, tiled=True).reshape(rows.shape)]
    ppermute x0 -> x1, starting transfers between devices: none -> 4.51 us  [on_device(): other = lax.ppermute(own, 'core', [(0, 1), (1, 0)])]
    pallas_call x6 -> x7, Pallas kernels: 28.1 us -> 26 us  [call(): pl.pallas_call(kernel, out_shape=shape, in_specs=[pl.BlockSpec(memory_spa...]
    unnamed x15 -> x19, local copies, waits for them, and re-layouts: 2.51 us -> 4 us
  transfers between devices with their start and end apart: 3 -> 4, of which waited for: 3 -> 4; matrix products, arithmetic and copies ran while one was open for 0% -> 0% of each run, Pallas kernels for 0% -> 0%
where the time goes in v3:
time: 182 us; the launch traced here: 179 us
  blocking collectives  72.6 us (40%)
  waiting for transfers between devices  49.2 us (27%)
  Pallas kernels  26 us (14%)
  starting transfers between devices  22.3 us (12%)
  local copies, waits for them, and re-layouts  6.44 us (4%)
  other arithmetic  2.08 us (1%)
    all_to_all x3, blocking collectives, exchange(): return lax.all_to_all(blocks, axes, 0, 0, tiled=True).reshape(rows.shape)  72.6 us
    all_to_all x3, waiting for transfers between devices, exchange(): return lax.all_to_all(blocks, axes, 0, 0, tiled=True).reshape(rows.shape)  47.5 us
    pallas_call x7, Pallas kernels, call(): pl.pallas_call(kernel, out_shape=shape, in_specs=[pl.BlockSpec(memory_spa...  26 us
    all_to_all x3, starting transfers between devices, exchange(): return lax.all_to_all(blocks, axes, 0, 0, tiled=True).reshape(rows.shape)  17.8 us
    ppermute x1, starting transfers between devices, on_device(): other = lax.ppermute(own, 'core', [(0, 1), (1, 0)])  4.51 us
    unnamed x19, local copies, waits for them, and re-layouts  4 us
  transfers between devices with their start and end apart: 4, of which 4 were waited for; matrix products, arithmetic and copies ran while one was open for 0% of the time, Pallas kernels for 0%

profile of v3, /device:TPU:1, one launch (start us, length us, event | category | flops | bytes accessed | tf_op | source)
XLA Modules:
  0.0 179.5 jit_solution(5864396729048260932)
XLA Ops:
  0.6 1.0 convert_reduce_fusion
  1.7 0.0 copy-start.5
  1.7 0.1 copy.23
  1.8 0.6 copy-done.5
  2.4 0.0 copy-start.6
  2.4 0.0 copy-start.3
  2.5 0.1 copy.24
  2.6 0.1 squeeze.13
  2.7 0.1 copy.25
  2.8 0.1 squeeze.14
  2.9 0.1 copy.26
  3.0 0.1 squeeze.15
  3.1 0.1 copy-done.6
  3.1 0.1 copy.27
  3.2 0.0 copy-start.7
  3.2 0.1 reshape.98
  3.3 0.6 copy-done.7
  4.0 0.1 copy.28
  4.1 0.1 reshape.99
  4.2 0.1 maximum_bitcast_fusion.2
  4.2 0.1 maximum_bitcast_fusion
  4.3 0.0 copy-done.3
  4.3 0.1 reshape.97.start_ref
  4.4 0.1 shard_map.93
  4.6 44.3 %all_to_all.30 = f32[256,5,1,128]{3,2,1,0:T(1,128)S(1)} all-to-all(f32[256,5,1,128]{3,2,1,0:T(1,128)S(1)} %bitcast.47), channel_id=1, replica_groups=mesh['cy'=8,'core'=2,'gy'=4,'gz'=8] {'cy','gy','gz'}, dimensions={0} | all-to-all | bytes 1310720 | tf_op jit(solution)/shard_map/all_to_all | solution.py:394
  48.9 4.5 %collective-permute-start = (f32[1280,128]{1,0:T(8,128)S(1)}, f32[1280,128]{1,0:T(8,128)S(1)}, u32[]{:S(2)}, u32[]{:S(2)}) collective-permute-start(f32[1280,128]{1,0:T(8,128)S(1)} %bitcast.45), channel_id=1, source_target_pairs={{0,32},{32,0},{1,33},{33,1},{2,34},{34,2},{3,35},{35,3},{4,36},{36... | collective-permute-start | bytes 1966088 | tf_op jit(solution)/shard_map/ppermute | solution.py:421
  53.4 1.7 collective-permute-done.other_ref
  55.1 2.3 %shard_map.94 = (f32[16,4,8,128]{3,2,1,0:T(8,128)S(1)}, f32[3,16,4,8,128]{4,3,2,1,0:T(8,128)S(1)}, f32[3,16,4,8,128]{4,3,2,1,0:T(8,128)S(1)}, f32[16,4,8,128]{3,...) custom-call(s32[1]{0:T(128)} %bitcast.1.core_ref, f32[1280,128]{1,0:T(8,128)S(1)} %bitcast.46, ...), custom_call_target="tpu_custom_call" | custom-call | tf_op jit(solution)/shard_map/pallas_call | solution.py:371
  57.5 0.0 copy-start
  57.5 0.7 copy-done
  58.2 3.8 %all-to-all-start.1 = ((f32[4,8,128]{2,1,0:T(8,128)}), f32[4,8,128]{2,1,0:T(8,128)S(1)}, u32[]{:S(2)}, u32[]{:S(2)}) async-start(f32[4,8,128]{2,1,0:T(8,128)} %bitcast.7), calls=%async_computation.1 | async-start | bytes 32768 | tf_op jit(solution)/shard_map/all_to_all | solution.py:394
  61.9 4.2 %all-to-all-done.1 = f32[4,8,128]{2,1,0:T(8,128)S(1)} async-done(((f32[4,8,128]{2,1,0:T(8,128)}), f32[4,8,128]{2,1,0:T(8,128)S(1)}, u32[]{:S(2)}, u32[]{:S(2)}) %all-to-all-start.1) | async-done | bytes 16416 | tf_op jit(solution)/shard_map/all_to_all | solution.py:394
  66.1 0.0 copy-start.1
  66.1 0.9 copy-done.1
  67.1 6.9 %shard_map.95 = f32[2048,128]{1,0:T(8,128)} custom-call(s32[1]{0:T(128)} %bitcast.comp_ref, f32[16,4,8,128]{3,2,1,0:T(8,128)S(1)} %get-tuple-element.13.vectors_ref, f32[3,16,4,8,128]{4,3,2,1,0:T(8,128)S(1)} %get-tuple-element.14.up_ref, f32[3,16,4,8,128]{4,3,2,1,0:T(8,128)S(1)} %get-tuple-element.15.down_ref, ...), custom_call_target="tpu_custom_call" | custom-call | tf_op jit(solution)/shard_map/pallas_call | solution.py:371
  74.0 10.2 %all-to-all-start.2 = ((f32[512,4,1,128]{3,1,2,0:T(4,128)}), f32[512,4,1,128]{3,1,2,0:T(4,128)S(1)}, u32[]{:S(2)}, u32[]{:S(2)}) async-start(f32[512,4,1,128]{3,1,2,0:T(4,128)} %bitcast.10), calls=%async_computation.2 | async-start | bytes 2097152 | tf_op jit(solution)/shard_map/all_to_all | solution.py:394
  84.2 0.1 reshape_reshape.3
  84.4 32.9 %all-to-all-done.2 = f32[512,4,1,128]{3,1,2,0:T(4,128)S(1)} async-done(((f32[512,4,1,128]{3,1,2,0:T(4,128)}), f32[512,4,1,128]{3,1,2,0:T(4,128)S(1)}, u32[]{:S(2)}, u32[]{:S(2)}) %all-to-all-start.2) | async-done | bytes 1048608 | tf_op jit(solution)/shard_map/all_to_all | solution.py:394
  117.2 0.7 shard_map.96
  118.0 15.1 %all_to_all.31 = f32[32,16,128]{2,1,0:T(8,128)S(1)} all-to-all(f32[32,16,128]{2,1,0:T(8,128)S(1)} %bitcast.50), channel_id=1, replica_groups=mesh['cy'=8,'core'=2,'gy'=4,'gz'=8] {'cy','gy'}, dimensions={0} | all-to-all | bytes 524288 | tf_op jit(solution)/shard_map/all_to_all | solution.py:394
  133.1 13.1 %all_to_all.32 = f32[16,16,128]{2,1,0:T(8,128)S(1)} all-to-all(f32[16,16,128]{2,1,0:T(8,128)S(1)} %bitcast.51), channel_id=1, replica_groups=mesh['cy'=8,'core'=2,'gy'=4,'gz'=8] {'core','gz'}, dimensions={0} | all-to-all | bytes 262144 | tf_op jit(solution)/shard_map/all_to_all | solution.py:394
  146.3 0.7 shard_map.98
  147.0 3.9 %all-to-all-start.5 = ((f32[32,16,128]{2,1,0:T(8,128)}), f32[32,16,128]{2,1,0:T(8,128)S(1)}, u32[]{:S(2)}, u32[]{:S(2)}) async-start(f32[32,16,128]{2,1,0:T(8,128)} %bitcast.16), calls=%async_computation.5 | async-start | bytes 524288 | tf_op jit(solution)/shard_map/all_to_all | solution.py:394
  150.9 0.1 copy.34
  151.0 10.4 %all-to-all-done.5 = f32[32,16,128]{2,1,0:T(8,128)S(1)} async-done(((f32[32,16,128]{2,1,0:T(8,128)}), f32[32,16,128]{2,1,0:T(8,128)S(1)}, u32[]{:S(2)}, u32[]{:S(2)}) %all-to-all-start.5) | async-done | bytes 262176 | tf_op jit(solution)/shard_map/all_to_all | solution.py:394
  161.4 15.1 %shard_map.99 = (f32[192,256]{1,0:T(8,128)S(1)}, f32[256,256]{1,0:T(8,128)}, f32[8,256]{1,0:T(8,128)S(1)}) custom-call(f32[512,128]{1,0:T(8,128)S(1)} %bitcast.48, f32[2048,128]{1,0:T(8,128)S(1)} %bitcast.44), custom_call_target="tpu_custom_call" | custom-call | tf_op jit(solution)/shard_map/pallas_call | solution.py:371
  176.5 0.1 slice_reduce_fusion.3
  176.6 0.1 slice.60
  176.7 0.1 slice.62
  176.8 0.1 add.27
  176.9 0.0 copy-start.4
  177.0 0.7 reshape.113
  177.7 0.0 copy-start.2
  177.7 0.1 squeeze.16
  177.8 0.7 copy.35
  178.5 0.0 copy-done.4
  178.5 0.1 copy-done.2
  178.6 0.9 multiply_add_fusion
  (15 shorter events, 0.2 us)
Async XLA Ops:
  1.7 0.8 copy-start.5
  2.4 0.7 copy-start.6
  2.4 1.9 %copy-start.3 = (f32[3,2,8,4,256]{4,3,2,1,0:T(4,128)S(1)}, f32[3,2,8,4,256]{4,3,2,1,0:T(4,128)}, u32[]{:S(2)}) copy-start(f32[3,2,8,4,256]{4,3,2,1,0:T(4,128)} %param.6) | copy-start | bytes 589828
  3.2 0.7 copy-start.7
  48.9 6.2 %collective-permute-start = (f32[1280,128]{1,0:T(8,128)S(1)}, f32[1280,128]{1,0:T(8,128)S(1)}, u32[]{:S(2)}, u32[]{:S(2)}) collective-permute-start(f32[1280,128]{1,0:T(8,128)S(1)} %bitcast.45), channel_id=1, source_target_pairs={{0,32},{32,0},{1,33},{33,1},{2,34},{34,2},{3,35},{35,3},{4,36},{36... | collective-permute-start | bytes 1966088 | tf_op jit(solution)/shard_map/ppermute | solution.py:421
  57.5 0.7 copy-start
  58.2 8.0 %all-to-all-start.1 = ((f32[4,8,128]{2,1,0:T(8,128)}), f32[4,8,128]{2,1,0:T(8,128)S(1)}, u32[]{:S(2)}, u32[]{:S(2)}) async-start(f32[4,8,128]{2,1,0:T(8,128)} %bitcast.7), calls=%async_computation.1 | async-start | bytes 32768 | tf_op jit(solution)/shard_map/all_to_all | solution.py:394
  66.1 1.0 copy-start.1
  74.0 43.2 %all-to-all-start.2 = ((f32[512,4,1,128]{3,1,2,0:T(4,128)}), f32[512,4,1,128]{3,1,2,0:T(4,128)S(1)}, u32[]{:S(2)}, u32[]{:S(2)}) async-start(f32[512,4,1,128]{3,1,2,0:T(4,128)} %bitcast.10), calls=%async_computation.2 | async-start | bytes 2097152 | tf_op jit(solution)/shard_map/all_to_all | solution.py:394
  147.0 14.4 %all-to-all-start.5 = ((f32[32,16,128]{2,1,0:T(8,128)}), f32[32,16,128]{2,1,0:T(8,128)S(1)}, u32[]{:S(2)}, u32[]{:S(2)}) async-start(f32[32,16,128]{2,1,0:T(8,128)} %bitcast.16), calls=%async_computation.5 | async-start | bytes 524288 | tf_op jit(solution)/shard_map/all_to_all | solution.py:394
  176.9 1.6 copy-start.4
  177.7 0.9 copy-start.2

commit v4 on v3

--- a/solution.py
+++ b/solution.py
@@ -17,6 +17,7 @@
 NODES = 64
 DEVICES = 512
 OUT_ROWS = 5
+LEAST_PIVOT = 0.1
 BLOCK = 32
 STIFF_LANE = 5
 MASS_LANE = 6
@@ -292,27 +293,117 @@
         for j in range(BLOCK)
     ]
     inverse = jnp.where((lane & 63) == row, 1.0, 0.0)
-    pivots = jnp.ones((BLOCK, 128), jnp.float32)
-    for k in range(BLOCK):
-        column = columns[k]
-        pivot = column[k : k + 1, :]
-        pivots = jnp.where(row == k, pivot, pivots)
-        if k + 1 == BLOCK:
+    scale = jnp.ones((BLOCK, 128), jnp.float32)
+    link = jnp.zeros((BLOCK, 128), jnp.float32)
+    for k in range(0, BLOCK, 2):
+        one, two = columns[k], columns[k + 1]
+        top = one[k : k + 1, :]
+        side = one[k + 1 : k + 2, :]
+        corner = two[k + 1 : k + 2, :]
+        rest = top * corner - side * side
+        scale = jnp.where(row == k, top, jnp.where(row == k + 1, rest / top, scale))
+        link = jnp.where(row == k + 1, side / top, link)
+        if k + 2 == BLOCK:
             break
-        part = (k + 1) // 8 * 8
-        multiple = jnp.where(row[part:] > k, column[part:] * (1.0 / pivot), 0.0)
+        part = (k + 2) // 8 * 8
+        factor = 1.0 / rest
+        below = row[part:] > k + 1
+        first = jnp.where(below, (one[part:] * corner - two[part:] * side) * factor, 0.0)
+        second = jnp.where(below, (two[part:] * top - one[part:] * side) * factor, 0.0)
 
         def reduced(value):
-            tail = value[part:] - multiple * value[k : k + 1, :]
+            tail = value[part:] - (first * value[k : k + 1, :] + second * value[k + 1 : k + 2, :])
             return tail if part == 0 else jnp.concatenate([value[:part], tail], axis=0)
 
-        for j in range(k + 1, BLOCK):
+        for j in range(k + 2, BLOCK):
             columns[j] = reduced(columns[j])
         inverse = reduced(inverse)
-    return inverse * lax.rsqrt(pivots)
-
-
-def final_kernel(sums_ref, rows_ref, subspace_ref, projected_ref, fields_ref, a_ref, e_ref):
+    inverse = inverse - link * pltpu.roll(inverse, 1, 0)
+    return inverse * lax.rsqrt(scale), scale
+
+
+def rounded(value):
+    return value.astype(jnp.bfloat16).astype(jnp.float32)
+
+
+def three_parts(value):
+    high = rounded(value)
+    rest = value - high
+    middle = rounded(rest)
+    return high, middle, rest - middle
+
+
+def four_copies(value):
+    value = value + pltpu.roll(value, 32, 1)
+    return value + pltpu.roll(value, 64, 1)
+
+
+def left_groups(first, second):
+    group = lax.broadcasted_iota(jnp.int32, first.shape, 1) // BLOCK
+    high, middle, _ = three_parts(first)
+    parts = three_parts(second)
+    one = jnp.where(group < 2, high, middle)
+    two = jnp.where(group == 0, parts[0], jnp.where(group == 1, parts[2], 0.0))
+    return jnp.concatenate([one, two], axis=1).astype(jnp.bfloat16)
+
+
+def right_lanes(copies):
+    group = lax.broadcasted_iota(jnp.int32, copies.shape, 1) // BLOCK
+    high, middle, low = three_parts(copies)
+    one = jnp.where(group % 2 == 0, high, middle)
+    two = jnp.where(group == 0, low, high)
+    return jnp.concatenate([one, two], axis=1).astype(jnp.bfloat16)
+
+
+def right_rows(value):
+    high, middle, low = [part.astype(jnp.bfloat16) for part in three_parts(value)]
+    return jnp.concatenate([high, middle, high, middle, low, high, high, high], axis=0)
+
+
+def product(left, right, contract):
+    return lax.dot_general(
+        left, right, (contract, ((), ())), preferred_element_type=jnp.float32
+    )
+
+
+def invert_factors(m_ref, diagonal):
+    lane = lax.broadcasted_iota(jnp.int32, (BLOCK, 128), 1)
+    least = jnp.ones((BLOCK, 128), jnp.float32)
+    for first in range(0, 256, BLOCK):
+        tile = first // 128 * 128
+        inside = first - tile
+        after = first + BLOCK
+        small = [m_ref[m, first:after, tile : tile + 128][:, inside : inside + BLOCK] for m in (0, 1)]
+        inverse, pivots = factor_block(small[0], small[1])
+        least = jnp.minimum(least, pivots / diagonal[first:after, :])
+        for m in (0, 1):
+            own = four_copies(
+                jnp.where((lane >= 64 * m) & (lane < 64 * m + BLOCK), inverse, 0.0)
+            )
+            row = lax.broadcasted_iota(jnp.int32, (BLOCK, 256), 0)
+            column = lax.broadcasted_iota(jnp.int32, (BLOCK, 256), 1) - first
+            rows = m_ref[m, first:after, :]
+            unit = jnp.where(column == row, 1.0, 0.0)
+            rows = jnp.where((column >= 0) & (column < BLOCK), unit, rows)
+            result = product(left_groups(own, own), right_rows(rows), ((1,), (0,)))
+            m_ref[m, first:after, :] = result
+            if after < 256:
+                count = 256 - after
+                lanes = lax.broadcasted_iota(jnp.int32, (count, 128), 1)
+                held = (lanes >= inside) & (lanes < inside + BLOCK)
+                left = four_copies(jnp.where(held, m_ref[m, after:, tile : tile + 128], 0.0))
+                right = jnp.concatenate([right_lanes(own)] * 8, axis=0)
+                factor = product(left_groups(left, left), right, ((1,), (1,)))
+                column = lax.broadcasted_iota(jnp.int32, (count, 256), 1)
+                rows = m_ref[m, after:, :]
+                rows = jnp.where((column >= first) & (column < after), 0.0, rows)
+                m_ref[m, after:, :] = rows - product(
+                    left_groups(factor[:, :128], factor[:, 128:]), right_rows(result), ((1,), (0,))
+                )
+    return jnp.min(least, axis=(0, 1), keepdims=True)
+
+
+def final_kernel(sums_ref, rows_ref, subspace_ref, projected_ref, fields_ref, least_ref, m_ref):
     both = jnp.concatenate([sums_ref[:256, :], sums_ref[256:, :]], axis=1)
     mixed = parts_of(rows_ref, 2)
     diagonal = one_lane(mixed[0] + mixed[1] + mixed[2], STIFF_LANE)
@@ -323,34 +414,14 @@
     column = lax.broadcasted_iota(jnp.int32, (256, 256), 1)
     gram = jnp.where(row >= column, both, turned)
     stiff = jnp.where(row < column, both, jnp.where(row == column, diagonal, turned))
-    a_ref[0] = gram
-    a_ref[1] = stiff
-    unit = jnp.where(row == column, 1.0, 0.0)
-    e_ref[0] = unit
-    e_ref[1] = unit
-    lane = lax.broadcasted_iota(jnp.int32, (BLOCK, 128), 1)
-    for first in range(0, 256, BLOCK):
-        tile = first // 128 * 128
-        inside = first - tile
-        after = first + BLOCK
-        small = [a_ref[m, first:after, tile : tile + 128][:, inside : inside + BLOCK] for m in (0, 1)]
-        inverse = factor_block(small[0], small[1])
-        for m in (0, 1):
-            kept = jnp.where((lane >= 64 * m) & (lane < 64 * m + BLOCK), inverse, 0.0)
-            shift = (inside - 64 * m) % 128
-            spread = pltpu.roll(kept, shift, 1) if shift else kept
-            own = kept[:, 64 * m : 64 * m + BLOCK]
-            known = slice(0, 128) if after <= 128 else slice(0, 256)
-            e_rows = dot(own, e_ref[m, first:after, known])
-            e_ref[m, first:after, known] = e_rows
-            if after < 256:
-                open_ = slice(0, 256) if after < 128 else slice(128, 256)
-                a_rows = dot(own, a_ref[m, first:after, open_])
-                factor = dot(a_ref[m, after:, tile : tile + 128], spread, ((1,), (1,)))
-                a_ref[m, after:, open_] = a_ref[m, after:, open_] - dot(factor, a_rows)
-                e_ref[m, after:, known] = e_ref[m, after:, known] - dot(factor, e_rows)
-    lower = e_ref[0]
-    stiff_lower = e_ref[1]
+    m_ref[0] = gram
+    m_ref[1] = stiff
+    half = lax.broadcasted_iota(jnp.int32, (256, 128), 1) < 64
+    gram_diagonal = jnp.sum(jnp.where(row == column, gram, 0.0), axis=1, keepdims=True)
+    least = invert_factors(m_ref, jnp.where(half, gram_diagonal, diagonal[:, :128]))
+    least_ref[...] = jnp.broadcast_to(least, (8, 128))
+    lower = jnp.where(row >= column, m_ref[0], 0.0)
+    stiff_lower = jnp.where(row >= column, m_ref[1], 0.0)
     parts = parts_of(rows_ref, 0)
     vectors = by_vector(parts)
     mixed = untucked(parts, mixed)
@@ -365,6 +436,86 @@
     for place, value in enumerate((vectors, axial, bending)):
         fields_ref[place : place + 1, :] = jnp.sum(value * weights, axis=0, keepdims=True)
     fields_ref[3:, :] = jnp.zeros((5, 256), jnp.float32)
+
+
+def extended(block, first_dim):
+    for place, axis in enumerate((GX, "gy", "gz")):
+        dim = first_dim + place
+        count = lax.axis_size(axis)
+        forward = [(i, i + 1) for i in range(count - 1)]
+        backward = [(target, source) for source, target in forward]
+        last = block.shape[dim]
+        low = lax.ppermute(lax.slice_in_dim(block, last - 1, last, axis=dim), axis, forward)
+        high = lax.ppermute(lax.slice_in_dim(block, 0, 1, axis=dim), axis, backward)
+        block = jnp.concatenate([low, block, high], axis=dim)
+    return block
+
+
+def neighbour(padded, leading, direction, sense):
+    slicer = [slice(None)] * padded.ndim
+    for position in range(3):
+        slicer[leading + position] = slice(1, -1)
+    slicer[leading + direction] = slice(2, None) if sense > 0 else slice(0, -2)
+    return padded[tuple(slicer)]
+
+
+def step_by_step(start_block, node_mass, ground_spring, stiffness, yield_flags):
+    share = jnp.mean(yield_flags.astype(jnp.float32), axis=1)
+    tangent = stiffness * (1.0 - 0.9 * share)[:, None]
+    padded = extended(tangent, 2)
+    edges = [
+        [0.5 * (tangent[d] + neighbour(padded, 2, d, sense)[d]) for d in range(3)]
+        for sense in (1, -1)
+    ]
+    edge_total = sum(edges[0]) + sum(edges[1])
+    diagonal = ground_spring + edge_total
+    top = lax.pmax(jnp.max((diagonal + edge_total) / node_mass), AXES)
+    middle = top * 9.0 / 16.0
+    spread = top * 7.0 / 16.0
+
+    def apply_k(field):
+        around_field = extended(field, 1)
+        result = diagonal[..., None] * field
+        for d in range(3):
+            for sense, weights in ((1, edges[0]), (-1, edges[1])):
+                result = result - weights[d][..., None] * neighbour(around_field, 1, d, sense)
+        return result
+
+    def shifted(field):
+        return (apply_k(field) / node_mass[..., None] - middle * field) / spread
+
+    width = start_block.shape[-1]
+    mass_rows = node_mass.reshape(-1)
+    vectors = start_block
+    for turn in range(ITERS):
+        earlier, current = vectors, shifted(vectors)
+        for repeat in range(DEGREE - 1):
+            earlier, current = current, 2.0 * shifted(current) - earlier
+        flat_rows = current.reshape(-1, width)
+        gram = lax.psum(dot(flat_rows.T, mass_rows[:, None] * flat_rows), AXES)
+        factor = jnp.linalg.cholesky(gram)
+        basis = lax.linalg.triangular_solve(factor, flat_rows.T, left_side=True, lower=True)
+        vectors = basis.T.reshape(current.shape)
+    image = apply_k(vectors).reshape(-1, width)
+    projected = lax.psum(dot(basis, image), AXES)
+    lateral = lax.psum(dot(basis[:, :NODES], mass_rows[:NODES, None]), AXES)
+    factor = jnp.linalg.cholesky(projected)
+    halfway = lax.linalg.triangular_solve(factor, lateral, left_side=True, lower=True)
+    weights = lax.linalg.triangular_solve(
+        factor, halfway, left_side=True, lower=True, transpose_a=True
+    )
+    displace = dot(weights.T, basis).reshape(node_mass.shape)
+    padded = extended(displace, 1)
+    axial = []
+    bending = []
+    for d in range(3):
+        above = neighbour(padded, 1, d, 1)
+        below = neighbour(padded, 1, d, -1)
+        other = (d + 1) % 3
+        axial.append(0.5 * (above[d] - below[d]))
+        bending.append(above[other] - 2.0 * displace[other] + below[other])
+    fields = jnp.stack([displace, jnp.stack(axial), jnp.roll(jnp.stack(bending), 1, axis=0)])
+    return vectors * jnp.sqrt(jnp.float32(DEVICES * 3 * NODES)), projected, fields
 
 
 def call(kernel, shape, scratch=(), smem=(), operands=()):
@@ -449,30 +600,41 @@
         rows_of(512),
         operands=(exchange(partial, ("core", "gz"), 16),),
     )
-    subspace, projected, fields = call(
+    subspace, projected, fields, least = call(
         final_kernel,
         (
             jax.ShapeDtypeStruct((3 * NODES, width), jnp.float32),
             jax.ShapeDtypeStruct((width, width), jnp.float32),
             jax.ShapeDtypeStruct((8, 256), jnp.float32),
+            rows_of(8),
         ),
-        (
-            pltpu.VMEM((2, 256, 256), jnp.float32),
-            pltpu.VMEM((2, 256, 256), jnp.float32),
-        ),
+        (pltpu.VMEM((2, 256, 256), jnp.float32),),
         operands=(exchange(totals, ("cy", "gy"), 32), returned),
     )
     place = node_mass.shape[1:]
     fields = fields[:3, : 3 * NODES].reshape((3, 3) + place)
+    subspace, projected, fields = lax.cond(
+        least[0, 0] > LEAST_PIVOT,
+        lambda *operands: operands[:3],
+        lambda *operands: step_by_step(*operands[3:]),
+        subspace.reshape(start_block.shape),
+        projected,
+        fields,
+        start_block,
+        node_mass,
+        ground_spring,
+        stiffness,
+        yield_flags,
+    )
     force = node_mass * fields[0]
     axial = fields[1]
     bending = jnp.roll(fields[2], -1, axis=0)
     fibers = stress_old.shape[1]
     heights = ((jnp.arange(fibers).astype(jnp.float32) + 0.5) / fibers - 0.5)[:, None, None, None]
     strain = axial[:, None] + heights * bending[:, None]
-    own = jnp.stack([stiffness[d, d] for d in range(3)])[:, None]
-    stress_new = stress_old + own * jnp.where(yield_flags == 1, 0.05, 1.0) * strain
-    return (subspace.reshape(start_block.shape), projected, force, stress_new)
+    own_stiffness = jnp.stack([stiffness[d, d] for d in range(3)])[:, None]
+    stress_new = stress_old + own_stiffness * jnp.where(yield_flags == 1, 0.05, 1.0) * strain
+    return (subspace, projected, force, stress_new)
 
 
 def solution(mesh):

time: 182 us -> 194 us (1.066)
  between operations: 0.81 us -> 14.9 us
    unnamed x19 -> x22, local copies, waits for them, and re-layouts: 4 us -> 3.23 us
where the time goes in v4:
time: 194 us; the launch traced here: 192 us
  blocking collectives  72.6 us (37%)
  waiting for transfers between devices  48.8 us (25%)
  Pallas kernels  24.2 us (12%)
  starting transfers between devices  22.7 us (12%)
  between operations  14.9 us (8%)
  local copies, waits for them, and re-layouts  5.58 us (3%)
  other arithmetic  2.69 us (1%)
    all_to_all x3, blocking collectives, exchange(): return lax.all_to_all(blocks, axes, 0, 0, tiled=True).reshape(rows.shape)  72.6 us
    all_to_all x3, waiting for transfers between devices, exchange(): return lax.all_to_all(blocks, axes, 0, 0, tiled=True).reshape(rows.shape)  47.1 us
    pallas_call x7, Pallas kernels, call(): pl.pallas_call(kernel, out_shape=shape, in_specs=[pl.BlockSpec(memory_spa...  24.2 us
    all_to_all x3, starting transfers between devices, exchange(): return lax.all_to_all(blocks, axes, 0, 0, tiled=True).reshape(rows.shape)  18.2 us
    ppermute x1, starting transfers between devices, on_device(): other = lax.ppermute(own, 'core', [(0, 1), (1, 0)])  4.51 us
  transfers between devices with their start and end apart: 4, of which 4 were waited for; matrix products, arithmetic and copies ran while one was open for 0% of the time, Pallas kernels for 0%

profile of v4, /device:TPU:1, one launch (start us, length us, event | category | flops | bytes accessed | tf_op | source)
XLA Modules:
  0.0 191.7 jit_solution(15245471585515892096)
XLA Ops:
  7.2 1.0 convert_reduce_fusion.1
  8.2 0.0 copy-start.10
  8.2 0.1 copy.244
  8.3 0.6 copy-done.10
  9.0 0.0 copy-start.9
  9.0 0.0 copy-start.2
  9.0 0.1 copy.245
  9.1 0.1 squeeze.20
  9.2 0.1 copy.246
  9.3 0.1 squeeze.21
  9.4 0.1 copy.247
  9.5 0.1 squeeze.22
  9.6 0.1 copy-done.9
  9.7 0.1 copy.248
  9.8 0.0 copy-start.12
  9.8 0.1 reshape.322
  9.9 0.6 copy-done.12
  10.5 0.1 copy.249
  10.6 0.1 reshape.323
  10.7 0.1 maximum_bitcast_fusion.5
  10.8 0.1 maximum_bitcast_fusion.3
  10.9 0.0 copy-done.2
  10.9 0.1 reshape.321.start_ref
  11.0 0.1 shard_map.93
  11.1 44.3 %all_to_all.30 = f32[256,5,1,128]{3,2,1,0:T(1,128)S(1)} all-to-all(f32[256,5,1,128]{3,2,1,0:T(1,128)S(1)} %bitcast.262), channel_id=1, replica_groups=mesh['cy'=8,'core'=2,'gy'=4,'gz'=8] {'cy','gy','gz'}, dimensions={0} | all-to-all | bytes 1310720 | tf_op jit(solution)/shard_map/all_to_all | solution.py:545
  55.4 4.5 %collective-permute-start.66 = (f32[1280,128]{1,0:T(8,128)S(1)}, f32[1280,128]{1,0:T(8,128)S(1)}, u32[]{:S(2)}, u32[]{:S(2)}) collective-permute-start(f32[1280,128]{1,0:T(8,128)S(1)} %bitcast.260), channel_id=1, source_target_pairs={{0,32},{32,0},{1,33},{33,1},{2,34},{34,2},{3,35},{35,3},{4,36},{36... | collective-permute-start | bytes 1966088 | tf_op jit(solution)/shard_map/ppermute | solution.py:572
  60.0 1.7 collective-permute-done.66.other_ref
  61.7 2.3 %shard_map.94 = (f32[16,4,8,128]{3,2,1,0:T(8,128)S(1)}, f32[3,16,4,8,128]{4,3,2,1,0:T(8,128)S(1)}, f32[3,16,4,8,128]{4,3,2,1,0:T(8,128)S(1)}, f32[16,4,8,128]{3,...) custom-call(s32[1]{0:T(128)} %bitcast.59.core_ref, f32[1280,128]{1,0:T(8,128)S(1)} %bitcast.261, ...), custom_call_target="tpu_custom_call" | custom-call | tf_op jit(solution)/shard_map/pallas_call | solution.py:522
  64.0 0.0 copy-start
  64.0 0.7 copy-done
  64.7 3.8 %all-to-all-start.1 = ((f32[4,8,128]{2,1,0:T(8,128)}), f32[4,8,128]{2,1,0:T(8,128)S(1)}, u32[]{:S(2)}, u32[]{:S(2)}) async-start(f32[4,8,128]{2,1,0:T(8,128)} %bitcast.65), calls=%async_computation.1 | async-start | bytes 32768 | tf_op jit(solution)/shard_map/all_to_all | solution.py:545
  68.4 4.2 %all-to-all-done.1 = f32[4,8,128]{2,1,0:T(8,128)S(1)} async-done(((f32[4,8,128]{2,1,0:T(8,128)}), f32[4,8,128]{2,1,0:T(8,128)S(1)}, u32[]{:S(2)}, u32[]{:S(2)}) %all-to-all-start.1) | async-done | bytes 16416 | tf_op jit(solution)/shard_map/all_to_all | solution.py:545
  72.7 0.0 copy-start.1
  72.7 0.9 copy-done.1
  73.6 7.4 %shard_map.95 = f32[2048,128]{1,0:T(8,128)} custom-call(s32[1]{0:T(128)} %bitcast.58.comp_ref, f32[16,4,8,128]{3,2,1,0:T(8,128)S(1)} %get-tuple-element.49.vectors_ref, f32[3,16,4,8,128]{4,3,2,1,0:T(8,128)S(1)} %get-tuple-element.50.up_ref, f32[3,16,4,8,128]{4,3,2,1,0:T(8,128)S(1)} %get-tuple-element.51.down_ref, ...), custom_call_target="tpu_custom_call" | custom-call | tf_op jit(solution)/shard_map/pallas_call | solution.py:522
  81.0 10.2 %all-to-all-start.2 = ((f32[512,4,1,128]{3,1,2,0:T(4,128)}), f32[512,4,1,128]{3,1,2,0:T(4,128)S(1)}, u32[]{:S(2)}, u32[]{:S(2)}) async-start(f32[512,4,1,128]{3,1,2,0:T(4,128)} %bitcast.68), calls=%async_computation.2 | async-start | bytes 2097152 | tf_op jit(solution)/shard_map/all_to_all | solution.py:545
  91.2 0.1 reshape_reshape.3
  91.3 32.9 %all-to-all-done.2 = f32[512,4,1,128]{3,1,2,0:T(4,128)S(1)} async-done(((f32[512,4,1,128]{3,1,2,0:T(4,128)}), f32[512,4,1,128]{3,1,2,0:T(4,128)S(1)}, u32[]{:S(2)}, u32[]{:S(2)}) %all-to-all-start.2) | async-done | bytes 1048608 | tf_op jit(solution)/shard_map/all_to_all | solution.py:545
  124.2 0.7 shard_map.96
  124.9 15.1 %all_to_all.31 = f32[32,16,128]{2,1,0:T(8,128)S(1)} all-to-all(f32[32,16,128]{2,1,0:T(8,128)S(1)} %bitcast.265), channel_id=1, replica_groups=mesh['cy'=8,'core'=2,'gy'=4,'gz'=8] {'cy','gy'}, dimensions={0} | all-to-all | bytes 524288 | tf_op jit(solution)/shard_map/all_to_all | solution.py:545
  140.1 13.1 %all_to_all.32 = f32[16,16,128]{2,1,0:T(8,128)S(1)} all-to-all(f32[16,16,128]{2,1,0:T(8,128)S(1)} %bitcast.266), channel_id=1, replica_groups=mesh['cy'=8,'core'=2,'gy'=4,'gz'=8] {'core','gz'}, dimensions={0} | all-to-all | bytes 262144 | tf_op jit(solution)/shard_map/all_to_all | solution.py:545
  153.2 0.7 shard_map.98
  154.0 4.2 %all-to-all-start.5 = ((f32[32,16,128]{2,1,0:T(8,128)}), f32[32,16,128]{2,1,0:T(8,128)S(1)}, u32[]{:S(2)}, u32[]{:S(2)}) async-start(f32[32,16,128]{2,1,0:T(8,128)} %bitcast.74), calls=%async_computation.5 | async-start | bytes 524288 | tf_op jit(solution)/shard_map/all_to_all | solution.py:545
  158.2 0.1 copy.256
  158.3 10.0 %all-to-all-done.5 = f32[32,16,128]{2,1,0:T(8,128)S(1)} async-done(((f32[32,16,128]{2,1,0:T(8,128)}), f32[32,16,128]{2,1,0:T(8,128)S(1)}, u32[]{:S(2)}, u32[]{:S(2)}) %all-to-all-start.5) | async-done | bytes 262176 | tf_op jit(solution)/shard_map/all_to_all | solution.py:545
  168.4 0.0 copy-start.3
  168.4 0.0 copy-start.7
  168.4 12.8 %shard_map.99 = (f32[192,256]{1,0:T(8,128)S(1)}, f32[256,256]{1,0:T(8,128)}, f32[8,256]{1,0:T(8,128)S(1)}, f32[8,128]{1,0:T(8,128)S(1)}) custom-call(f32[512,128]{1,0:T(8,128)S(1)} %bitcast.263, f32[2048,128]{1,0:T(8,128)S(1)} %bitcast.259), custom_call_target="tpu_custom_call" | custom-call | tf_op jit(solution)/shard_map/pallas_call | solution.py:522
  181.2 0.5 slice.682
  182.4 0.0 copy-done.3
  182.4 0.0 copy-done.7
  182.4 0.5 conditional.1
  182.7 0.1 reshape.299
  182.7 0.1 reshape.300
  182.8 0.0 copy-start.11
  182.9 0.0 copy-start.13
  182.9 0.2 copy.255
  183.1 0.1 copy.257
  183.2 0.1 copy.258
  183.3 0.1 copy.259
  183.4 0.6 fusion.171
  184.0 0.0 copy-done.13
  184.0 0.9 multiply_add_fusion
  184.9 0.0 copy-done.11
  (16 shorter events, 0.1 us)
Async XLA Ops:
  8.2 0.8 copy-start.10
  9.0 0.7 copy-start.9
  9.0 1.9 copy-start.2
  9.8 0.7 copy-start.12
  55.4 6.2 %collective-permute-start.66 = (f32[1280,128]{1,0:T(8,128)S(1)}, f32[1280,128]{1,0:T(8,128)S(1)}, u32[]{:S(2)}, u32[]{:S(2)}) collective-permute-start(f32[1280,128]{1,0:T(8,128)S(1)} %bitcast.260), channel_id=1, source_target_pairs={{0,32},{32,0},{1,33},{33,1},{2,34},{34,2},{3,35},{35,3},{4,36},{36... | collective-permute-start | bytes 1966088 | tf_op jit(solution)/shard_map/ppermute | solution.py:572
  64.0 0.7 copy-start
  64.7 8.0 %all-to-all-start.1 = ((f32[4,8,128]{2,1,0:T(8,128)}), f32[4,8,128]{2,1,0:T(8,128)S(1)}, u32[]{:S(2)}, u32[]{:S(2)}) async-start(f32[4,8,128]{2,1,0:T(8,128)} %bitcast.65), calls=%async_computation.1 | async-start | bytes 32768 | tf_op jit(solution)/shard_map/all_to_all | solution.py:545
  72.7 1.0 copy-start.1
  81.0 43.2 %all-to-all-start.2 = ((f32[512,4,1,128]{3,1,2,0:T(4,128)}), f32[512,4,1,128]{3,1,2,0:T(4,128)S(1)}, u32[]{:S(2)}, u32[]{:S(2)}) async-start(f32[512,4,1,128]{3,1,2,0:T(4,128)} %bitcast.68), calls=%async_computation.2 | async-start | bytes 2097152 | tf_op jit(solution)/shard_map/all_to_all | solution.py:545
  154.0 14.4 %all-to-all-start.5 = ((f32[32,16,128]{2,1,0:T(8,128)}), f32[32,16,128]{2,1,0:T(8,128)S(1)}, u32[]{:S(2)}, u32[]{:S(2)}) async-start(f32[32,16,128]{2,1,0:T(8,128)} %bitcast.74), calls=%async_computation.5 | async-start | bytes 524288 | tf_op jit(solution)/shard_map/all_to_all | solution.py:545
  168.4 14.0 %copy-start.3 = (f32[3,2,8,4,256]{4,3,2,1,0:T(4,128)S(1)}, f32[3,2,8,4,256]{4,3,2,1,0:T(4,128)}, u32[]{:S(2)}) copy-start(f32[3,2,8,4,256]{4,3,2,1,0:T(4,128)} %param.11) | copy-start | bytes 589828
  168.4 14.0 %copy-start.7 = (s32[3,16,2,8,4]{1,4,3,2,0:T(4,128)S(1)}, s32[3,16,2,8,4]{1,4,3,2,0:T(4,128)}, u32[]{:S(2)}) copy-start(s32[3,16,2,8,4]{1,4,3,2,0:T(4,128)} %param.15) | copy-start | bytes 36868
  182.8 2.0 %copy-start.11 = (f32[3,2,8,4,256]{4,3,2,1,0:T(4,128)}, f32[3,2,8,4,256]{4,3,2,1,0:T(4,128)S(1)}, u32[]{:S(2)}) copy-start(f32[3,2,8,4,256]{4,3,2,1,0:T(4,128)S(1)} %get-tuple-element.127) | copy-start | bytes 589828
  182.9 1.1 copy-start.13

commit v5 on v4

--- a/solution.py
+++ b/solution.py
@@ -2,6 +2,7 @@
 
 import jax
 import jax.numpy as jnp
+import numpy as np
 from jax import lax
 from jax.experimental import pallas as pl
 from jax.experimental.pallas import tpu as pltpu
@@ -9,6 +10,7 @@
 
 DEGREE = 4
 ITERS = 2
+TOTAL = DEGREE * ITERS
 PRECISE = lax.Precision.HIGHEST
 GX = ("cy", "core")
 AXES = ("cy", "core", "gy", "gz")
@@ -19,8 +21,8 @@
 OUT_ROWS = 5
 LEAST_PIVOT = 0.1
 BLOCK = 32
-STIFF_LANE = 5
-MASS_LANE = 6
+STIFF_LANE = 9
+MASS_LANE = 10
 
 
 def dot(a, b, contract=((1,), (0,))):
@@ -29,17 +31,55 @@
     )
 
 
-def pack_kernel(start_ref, coef_ref, out_ref):
+def spread_nodes(values, keep):
+    groups = jnp.where(keep, values.reshape((-1,) + keep.shape), 0.0)
+    return jnp.sum(groups, axis=1)
+
+
+def pack_kernel(start_ref, stiffness_ref, node_ref, flags_ref, out_ref):
+    lane = lax.broadcasted_iota(jnp.int32, (8, 128), 1)
+    place = lax.broadcasted_iota(jnp.int32, (8, 128), 0)
+    repeated = jnp.where((lane & 7) == place, 1.0, 0.0)
+    keep = ((lane >> 3) & 7) == place
+    stiffness = spread_nodes(dot(stiffness_ref[...], repeated), keep)
+    nodes = spread_nodes(dot(node_ref[...], repeated), keep)
+    counts = jnp.dot(
+        flags_ref[...].astype(jnp.bfloat16),
+        jnp.ones((16, 128), jnp.bfloat16),
+        preferred_element_type=jnp.float32,
+    )
+    lane = lax.broadcasted_iota(jnp.int32, (NODES, 128), 1)
+    place = lax.broadcasted_iota(jnp.int32, (NODES, 128), 0)
+    own = ((place >> 5) * 32 + (place & 3) * 8 + ((place >> 2) & 7)) == (lane & 63)
+    softening = 1.0 - 0.9 * (spread_nodes(counts, own) / 16.0)
+    low = lax.broadcasted_iota(jnp.int32, (1, 128), 1) < 64
     for comp in range(4):
+        source = comp % 3
         if comp < 3:
-            block = start_ref[comp * NODES : (comp + 1) * NODES, :]
+            block = jnp.concatenate(
+                [
+                    start_ref[comp * 16 + x * 8 : comp * 16 + x * 8 + 8, z, :]
+                    for x in range(2)
+                    for z in range(4)
+                ],
+                axis=0,
+            )
             pairs = jnp.concatenate([block[:, :128], block[:, 128:]], axis=0).T
         else:
             pairs = jnp.zeros((128, 128), jnp.float32)
-        source = comp % 3
+        tangent = [
+            stiffness[3 * d + source : 3 * d + source + 1, :] * softening[d : d + 1, :]
+            for d in range(3)
+        ]
+        mass = nodes[source : source + 1, :]
+        spring = nodes[3 + source : 4 + source, :]
         rows = [
-            jnp.broadcast_to(coef_ref[source * 3 + r : source * 3 + r + 1, :], (8, 128))
-            for r in range(3)
+            jnp.broadcast_to(row, (8, 128))
+            for row in (
+                jnp.where(low, tangent[0], tangent[1]),
+                jnp.where(low, tangent[2], mass),
+                spring,
+            )
         ]
         for cy in range(8):
             first = (cy * 4 + comp) * 8 * OUT_ROWS
@@ -93,22 +133,22 @@
 
 def y_up(here):
     moved = jnp.concatenate([here[1:], jnp.zeros((1, 8, 128), jnp.float32)], axis=0)
-    return jnp.where((iota(2) & 28) != 28, roll(here, 124), roll(moved, 28))
+    return jnp.where((iota(2) & 7) != 7, roll(here, 127), roll(moved, 7))
 
 
 def y_down(here):
     moved = jnp.concatenate([jnp.zeros((1, 8, 128), jnp.float32), here[:-1]], axis=0)
-    return jnp.where((iota(2) & 28) != 0, roll(here, 4), roll(moved, 100))
+    return jnp.where((iota(2) & 7) != 0, roll(here, 1), roll(moved, 121))
 
 
 def z_up(here):
-    other = jnp.where(iota(1) < 7, roll(roll(here, 3), 7, 1), 0.0)
-    return jnp.where((iota(2) & 3) != 3, roll(here, 127), other)
+    other = jnp.where(iota(1) < 7, roll(roll(here, 24), 7, 1), 0.0)
+    return jnp.where((iota(2) & 24) != 24, roll(here, 120), other)
 
 
 def z_down(here):
-    other = jnp.where(iota(1) > 0, roll(roll(here, 125), 1, 1), 0.0)
-    return jnp.where((iota(2) & 3) != 0, roll(here, 1), other)
+    other = jnp.where(iota(1) > 0, roll(roll(here, 104), 1, 1), 0.0)
+    return jnp.where((iota(2) & 24) != 0, roll(here, 8), other)
 
 
 def around(ref, turned, gx):
@@ -158,38 +198,52 @@
 
 
 def filter_kernel(
-    comp_ref, vectors_ref, up_ref, down_ref, diagonal_ref, mass_ref, top_ref, out_ref, even_ref,
-    odd_ref, inverse_ref
+    vectors_ref, up_ref, down_ref, diagonal_ref, mass_ref, top_ref, terms_ref, inverse_ref
+):
+    top = top_ref[0:1, :]
+    inverse_spread = 1.0 / (top * 7.0 / 16.0)
+    ratio = (top * 9.0 / 16.0) * inverse_spread
+    for gx in range(16):
+        inverse_ref[gx] = inverse_spread / mass_ref[gx]
+        terms_ref[0, gx] = vectors_ref[gx]
+        terms_ref[TOTAL + 2, gx] = mass_ref[gx]
+    for degree in range(1, TOTAL + 2):
+        current_ref = vectors_ref if degree == 1 else terms_ref.at[degree - 1]
+        turned = Turned(current_ref)
+        for gx in range(16):
+            here, sides = around(current_ref, turned, gx)
+            image = diagonal_ref[gx] * here
+            for direction in range(3):
+                image = image - up_ref[direction, gx] * sides[direction][0]
+                image = image - down_ref[direction, gx] * sides[direction][1]
+            image = image * inverse_ref[gx] - ratio * here
+            if degree > 1:
+                image = 2.0 * image - terms_ref[degree - 2, gx]
+            terms_ref[degree, gx] = image
+
+
+def combine_kernel(
+    comp_ref, terms_ref, own_top_ref, top_ref, nodes_ref, out_ref, even_ref, image_ref
 ):
     top = jnp.max(jnp.max(top_ref[...], axis=0, keepdims=True), axis=1, keepdims=True)
-    middle = top * 9.0 / 16.0
-    spread = top * 7.0 / 16.0
-    inverse_spread = 1.0 / spread
-    ratio = middle * inverse_spread
+    own_top = own_top_ref[0:1, :]
+    part = own_top / top
+    place = part * nodes_ref[0:1, :] + (part - 1.0) * (9.0 / 7.0)
+    square = place * place
+    once = 8.0 * square * square - 8.0 * square + 1.0
+    coefficients = jnp.sum(nodes_ref[8:40, :] * (once * once), axis=1, keepdims=True)
+    middle = own_top * 9.0 / 16.0
+    spread = own_top * 7.0 / 16.0
     for gx in range(16):
-        inverse_ref[gx] = inverse_spread / mass_ref[gx]
-
-    def stiffness_times(here, sides, gx):
-        result = diagonal_ref[gx] * here
-        for direction in range(3):
-            result = result - up_ref[direction, gx] * sides[direction][0]
-            result = result - down_ref[direction, gx] * sides[direction][1]
-        return result
-
-    for turn in range(ITERS):
-        for repeat in range(DEGREE):
-            current_ref, other_ref = (even_ref, odd_ref) if repeat % 2 == 0 else (odd_ref, even_ref)
-            earlier_ref = other_ref
-            if turn == 0:
-                current_ref = vectors_ref if repeat == 0 else current_ref
-                earlier_ref = vectors_ref if repeat == 1 else earlier_ref
-            turned = Turned(current_ref)
-            for gx in range(16):
-                here, sides = around(current_ref, turned, gx)
-                image = stiffness_times(here, sides, gx) * inverse_ref[gx] - ratio * here
-                if repeat > 0:
-                    image = 2.0 * image - earlier_ref[gx]
-                other_ref[gx] = image
+        total = coefficients[0:1, :] * terms_ref[0, gx]
+        scaled = coefficients[16:17, :] * terms_ref[0, gx]
+        for degree in range(1, TOTAL + 2):
+            term = terms_ref[degree, gx]
+            if degree <= TOTAL:
+                total = total + coefficients[degree : degree + 1, :] * term
+            scaled = scaled + coefficients[16 + degree : 17 + degree, :] * term
+        even_ref[gx] = total
+        image_ref[gx] = terms_ref[TOTAL + 2, gx] * (middle * total + spread * scaled)
 
     comp = comp_ref[0]
     turned = Turned(even_ref)
@@ -199,7 +253,7 @@
         here, sides = around(even_ref, turned, gx)
         axial = [0.5 * (up - down) for up, down in sides]
         bending = [(up - 2.0 * here) + down for up, down in sides]
-        image = stiffness_times(here, sides, gx)
+        image = image_ref[gx]
         values = [
             here,
             image,
@@ -209,7 +263,7 @@
         for kind in range(4):
             out_ref[pl.ds(gx * 128 + kind, 32, stride=4), :] = values[kind].reshape(32, 128)
         stiff_sum = stiff_sum + here * image
-        mass_sum = mass_sum + here * mass_ref[gx]
+        mass_sum = mass_sum + here * terms_ref[TOTAL + 2, gx]
     lane = lax.broadcasted_iota(jnp.int32, (1, 128), 1)
     sums = []
     for value in (stiff_sum, mass_sum):
@@ -254,7 +308,7 @@
     fixed = []
     for comp in range(3):
         here = vectors[comp]
-        step = 4 if comp == 1 else 1
+        step = 1 if comp == 1 else 8
         above = pltpu.roll(here, 128 - step, 1)
         below = pltpu.roll(here, step, 1)
         value = (above - 2.0 * here) + below if comp == 0 else 0.5 * (above - below)
@@ -403,7 +457,10 @@
     return jnp.min(least, axis=(0, 1), keepdims=True)
 
 
-def final_kernel(sums_ref, rows_ref, subspace_ref, projected_ref, fields_ref, least_ref, m_ref):
+def final_kernel(
+    sums_ref, rows_ref, mass_ref, modulus_ref, stress_ref, subspace_ref, projected_ref, force_ref,
+    stress_new_ref, least_ref, m_ref
+):
     both = jnp.concatenate([sums_ref[:256, :], sums_ref[256:, :]], axis=1)
     mixed = parts_of(rows_ref, 2)
     diagonal = one_lane(mixed[0] + mixed[1] + mixed[2], STIFF_LANE)
@@ -427,15 +484,44 @@
     mixed = untucked(parts, mixed)
     other = parts_of(rows_ref, 3)
     subspace = dot(vectors.T, lower, ((1,), (1,)))
-    subspace_ref[...] = subspace[: 3 * NODES] * jnp.sqrt(jnp.float32(DEVICES * 3 * NODES))
+    subspace = subspace * jnp.sqrt(jnp.float32(DEVICES * 3 * NODES))
     projected_ref[...] = dot(lower, dot(stiff, lower, ((1,), (1,))))
     weights = dot(stiff_lower.T, dot(stiff_lower, lateral))
     weights = jnp.concatenate([weights, weights], axis=1)
     axial = by_vector([other[0], mixed[1], mixed[2]])
     bending = by_vector([mixed[0], other[1], other[2]])
-    for place, value in enumerate((vectors, axial, bending)):
-        fields_ref[place : place + 1, :] = jnp.sum(value * weights, axis=0, keepdims=True)
-    fields_ref[3:, :] = jnp.zeros((5, 256), jnp.float32)
+    fields = [
+        jnp.sum(value * weights, axis=0, keepdims=True) for value in (vectors, axial, bending)
+    ]
+    lane = lax.broadcasted_iota(jnp.int32, (24, 256), 1)
+    group = lax.broadcasted_iota(jnp.int32, (24, 256), 0)
+    laid = jnp.where((lane >> 3) == group, fields[0] * mass_ref[...], 0.0)
+    column = lax.broadcasted_iota(jnp.int32, (256, 128), 0)
+    place = lax.broadcasted_iota(jnp.int32, (256, 128), 1)
+    force_ref[...] = dot(laid, jnp.where((column & 7) == place, 1.0, 0.0))[:, :8]
+    columns = jnp.concatenate(
+        [fields[1], fields[2], jnp.zeros((126, 256), jnp.float32)], axis=0
+    ).T
+    axial = jnp.broadcast_to(columns[:, 0:1], (256, 16))
+    bending = jnp.broadcast_to(columns[:, 1:2], (256, 16))
+    fiber = lax.broadcasted_iota(jnp.int32, (8, 16), 1).astype(jnp.float32)
+    heights = (fiber + 0.5) / 16.0 - 0.5
+    for direction in range(3):
+        other = (direction + 1) % 3
+        for x in range(2):
+            for z in range(4):
+                rows = slice(direction * 16 + x * 8, direction * 16 + x * 8 + 8)
+                inner = x * 32 + z * 8
+                one = direction * NODES + inner
+                two = other * NODES + inner
+                subspace_ref[rows, z, :] = subspace[one : one + 8]
+                strain = axial[one : one + 8] + heights * bending[two : two + 8]
+                stress_new_ref[rows, z, :] = stress_ref[rows, z, :] + modulus_ref[rows, z, :] * strain
+
+
+def fiber_modulus(stiffness, yield_flags):
+    own = jnp.stack([stiffness[d, d] for d in range(3)])[:, None]
+    return own * jnp.where(yield_flags == 1, 0.05, 1.0)
 
 
 def extended(block, first_dim):
@@ -459,7 +545,16 @@
     return padded[tuple(slicer)]
 
 
-def step_by_step(start_block, node_mass, ground_spring, stiffness, yield_flags):
+def summed(square):
+    rows = jnp.concatenate([square[:, :128], square[:, 128:]], axis=0)
+    for axes, count, copies in ((("cy", "gy"), 32, 16), (("core", "gz"), 16, 32)):
+        rows = jnp.sum(exchange(rows, axes, count).reshape(count, 16, 128), axis=0)
+        rows = jnp.tile(rows, (copies, 1))
+    rows = exchange(rows, ("cy", "gy"), 32)
+    return jnp.concatenate([rows[:256], rows[256:]], axis=1)
+
+
+def step_by_step(start_block, node_mass, ground_spring, stiffness, yield_flags, stress_old):
     share = jnp.mean(yield_flags.astype(jnp.float32), axis=1)
     tangent = stiffness * (1.0 - 0.9 * share)[:, None]
     padded = extended(tangent, 2)
@@ -469,7 +564,10 @@
     ]
     edge_total = sum(edges[0]) + sum(edges[1])
     diagonal = ground_spring + edge_total
-    top = lax.pmax(jnp.max((diagonal + edge_total) / node_mass), AXES)
+    top = jnp.broadcast_to(jnp.max((diagonal + edge_total) / node_mass), (128, 128))
+    for axes, count in ((("cy", "core"), 16), ("gy", 4), ("gz", 8)):
+        top = jnp.broadcast_to(jnp.max(exchange(top, axes, count)), (128, 128))
+    top = top[0, 0]
     middle = top * 9.0 / 16.0
     spread = top * 7.0 / 16.0
 
@@ -492,13 +590,14 @@
         for repeat in range(DEGREE - 1):
             earlier, current = current, 2.0 * shifted(current) - earlier
         flat_rows = current.reshape(-1, width)
-        gram = lax.psum(dot(flat_rows.T, mass_rows[:, None] * flat_rows), AXES)
+        gram = summed(dot(flat_rows.T, mass_rows[:, None] * flat_rows))
         factor = jnp.linalg.cholesky(gram)
         basis = lax.linalg.triangular_solve(factor, flat_rows.T, left_side=True, lower=True)
         vectors = basis.T.reshape(current.shape)
     image = apply_k(vectors).reshape(-1, width)
-    projected = lax.psum(dot(basis, image), AXES)
-    lateral = lax.psum(dot(basis[:, :NODES], mass_rows[:NODES, None]), AXES)
+    projected = summed(dot(basis, image))
+    lateral = dot(basis[:, :NODES], mass_rows[:NODES, None])
+    lateral = summed(jnp.broadcast_to(lateral, (width, width)))[:, :1]
     factor = jnp.linalg.cholesky(projected)
     halfway = lax.linalg.triangular_solve(factor, lateral, left_side=True, lower=True)
     weights = lax.linalg.triangular_solve(
@@ -514,8 +613,12 @@
         other = (d + 1) % 3
         axial.append(0.5 * (above[d] - below[d]))
         bending.append(above[other] - 2.0 * displace[other] + below[other])
-    fields = jnp.stack([displace, jnp.stack(axial), jnp.roll(jnp.stack(bending), 1, axis=0)])
-    return vectors * jnp.sqrt(jnp.float32(DEVICES * 3 * NODES)), projected, fields
+    fibers = stress_old.shape[1]
+    heights = ((jnp.arange(fibers).astype(jnp.float32) + 0.5) / fibers - 0.5)[:, None, None, None]
+    strain = jnp.stack(axial)[:, None] + heights * jnp.stack(bending)[:, None]
+    stress_new = stress_old + fiber_modulus(stiffness, yield_flags) * strain
+    subspace = vectors * jnp.sqrt(jnp.float32(DEVICES * 3 * NODES))
+    return subspace, projected, node_mass * displace, stress_new
 
 
 def call(kernel, shape, scratch=(), smem=(), operands=()):
@@ -545,20 +648,33 @@
     return lax.all_to_all(blocks, axes, 0, 0, tiled=True).reshape(rows.shape)
 
 
+def chebyshev_nodes():
+    count = TOTAL + 1
+    angles = np.pi * (np.arange(count) + 0.5) / count
+    plain = np.zeros((count, count))
+    timesx = np.zeros((count + 1, count))
+    for degree in range(count):
+        plain[degree] = (2.0 if degree else 1.0) / count * np.cos(degree * angles)
+        timesx[degree + 1] += plain[degree] * (0.5 if degree else 1.0)
+        if degree:
+            timesx[degree - 1] += plain[degree] * 0.5
+    table = np.zeros((40, 128), np.float32)
+    table[0, :count] = np.cos(angles)
+    table[8 : 8 + count, :count] = plain
+    table[24 : 25 + count, :count] = timesx
+    return jnp.asarray(table)
+
+
 def on_device(start_block, node_mass, ground_spring, stiffness, yield_flags, stress_old):
     width = start_block.shape[-1]
-    share = jnp.mean(yield_flags.astype(jnp.float32), axis=1)
-    tangent = (stiffness * (1.0 - 0.9 * share)[:, None]).reshape(3, 3, NODES)
-    mass = node_mass.reshape(3, NODES)
-    spring = ground_spring.reshape(3, NODES)
-    coefficients = jnp.stack(
-        [
-            jnp.concatenate([tangent[0], tangent[1]], axis=1),
-            jnp.concatenate([tangent[2], mass], axis=1),
-            jnp.concatenate([spring, spring], axis=1),
-        ],
-        axis=1,
-    ).reshape(9, 128)
+    fibers = stress_old.shape[1]
+
+    def node_rows(value):
+        return jnp.swapaxes(value, -1, -2).reshape(-1, 8)
+
+    def fibers_last(value):
+        return jnp.moveaxis(value, 1, -1).reshape(48, 4, fibers)
+
     grid_shape = (16, 4, 8, 128)
     plain = pltpu.VMEM(grid_shape, jnp.float32)
     grid = jax.ShapeDtypeStruct(grid_shape, jnp.float32)
@@ -566,7 +682,12 @@
     sent = call(
         pack_kernel,
         rows_of(256 * OUT_ROWS),
-        operands=(start_block.reshape(3 * NODES, width), coefficients),
+        operands=(
+            start_block.reshape(48, 4, width),
+            node_rows(stiffness),
+            jnp.concatenate([node_rows(node_mass), node_rows(ground_spring)], axis=0),
+            fibers_last(yield_flags).reshape(3 * NODES, fibers),
+        ),
     )
     own = exchange(sent, CHIPS, 256)
     other = lax.ppermute(own, "core", [(0, 1), (1, 0)])
@@ -580,15 +701,22 @@
         operands=(core, own, other),
     )
     tops = exchange(own_top, "gy", 4)
+    terms = call(
+        filter_kernel,
+        jax.ShapeDtypeStruct((TOTAL + 3,) + grid_shape, jnp.float32),
+        (plain,),
+        operands=(*weights, own_top),
+    )
     filtered = call(
-        filter_kernel,
+        combine_kernel,
         rows_of(2048),
-        (plain, plain, plain),
+        (plain, plain),
         smem=(0,),
-        operands=(component, *weights, tops),
+        operands=(component, terms, own_top, tops, chebyshev_nodes()),
     )
     returned = exchange(filtered, AXES, DEVICES)
-    mass_row = jnp.pad(mass.reshape(1, 3 * NODES), ((0, 0), (0, NODES)))
+    mass_row = node_rows(node_mass).reshape(1, 3 * NODES)
+    mass_row = jnp.pad(mass_row, ((0, 0), (0, NODES)))
     products = call(product_kernel, rows_of(512), operands=(returned, mass_row))
     partial = call(
         functools.partial(total_kernel, 32, 16),
@@ -600,41 +728,42 @@
         rows_of(512),
         operands=(exchange(partial, ("core", "gz"), 16),),
     )
-    subspace, projected, fields, least = call(
+    subspace, projected, force, stress_new, least = call(
         final_kernel,
         (
-            jax.ShapeDtypeStruct((3 * NODES, width), jnp.float32),
+            jax.ShapeDtypeStruct((48, 4, width), jnp.float32),
             jax.ShapeDtypeStruct((width, width), jnp.float32),
-            jax.ShapeDtypeStruct((8, 256), jnp.float32),
+            jax.ShapeDtypeStruct((24, 8), jnp.float32),
+            jax.ShapeDtypeStruct((48, 4, fibers), jnp.float32),
             rows_of(8),
         ),
         (pltpu.VMEM((2, 256, 256), jnp.float32),),
-        operands=(exchange(totals, ("cy", "gy"), 32), returned),
+        operands=(
+            exchange(totals, ("cy", "gy"), 32),
+            returned,
+            mass_row,
+            fibers_last(fiber_modulus(stiffness, yield_flags)),
+            fibers_last(stress_old),
+        ),
     )
     place = node_mass.shape[1:]
-    fields = fields[:3, : 3 * NODES].reshape((3, 3) + place)
-    subspace, projected, fields = lax.cond(
+    force = jnp.swapaxes(force.reshape(3, place[0], place[2], place[1]), -1, -2)
+    stress_new = jnp.moveaxis(stress_new.reshape((3,) + place + (fibers,)), -1, 1)
+    return lax.cond(
         least[0, 0] > LEAST_PIVOT,
-        lambda *operands: operands[:3],
-        lambda *operands: step_by_step(*operands[3:]),
+        lambda *operands: operands[:4],
+        lambda *operands: step_by_step(*operands[4:]),
         subspace.reshape(start_block.shape),
         projected,
-        fields,
+        force,
+        stress_new,
         start_block,
         node_mass,
         ground_spring,
         stiffness,
         yield_flags,
-    )
-    force = node_mass * fields[0]
-    axial = fields[1]
-    bending = jnp.roll(fields[2], -1, axis=0)
-    fibers = stress_old.shape[1]
-    heights = ((jnp.arange(fibers).astype(jnp.float32) + 0.5) / fibers - 0.5)[:, None, None, None]
-    strain = axial[:, None] + heights * bending[:, None]
-    own_stiffness = jnp.stack([stiffness[d, d] for d in range(3)])[:, None]
-    stress_new = stress_old + own_stiffness * jnp.where(yield_flags == 1, 0.05, 1.0) * strain
-    return (subspace, projected, force, stress_new)
+        stress_old,
+    )
 
 
 def solution(mesh):

time: 194 us -> 178 us (0.918)
  between operations: 14.9 us -> 1.49 us
  waiting for transfers between devices: 48.8 us -> 44.5 us
  local copies, waits for them, and re-layouts: 5.58 us -> 8.33 us
  Pallas kernels: 24.2 us -> 26.2 us
    all_to_all x3, waiting for transfers between devices: 47.1 us -> 42.8 us  [exchange(): return lax.all_to_all(blocks, axes, 0, 0, tiled=True).reshape(rows.shape)]
    unnamed x22 -> x34, local copies, waits for them, and re-layouts: 3.23 us -> 7.39 us
    pallas_call x7 -> x8, Pallas kernels: 24.2 us -> 26.2 us  [call(): pl.pallas_call(kernel, out_shape=shape, in_specs=[pl.BlockSpec(memory_spa...]
  transfers between devices with their start and end apart: 4 -> 4, of which waited for: 4 -> 3; matrix products, arithmetic and copies ran while one was open for 0% -> 0% of each run, Pallas kernels for 0% -> 4%
where the time goes in v5:
time: 178 us; the launch traced here: 176 us
  blocking collectives  72.6 us (41%)
  waiting for transfers between devices  44.5 us (25%)
  Pallas kernels  26.2 us (15%)
  starting transfers between devices  21.7 us (12%)
  local copies, waits for them, and re-layouts  8.33 us (5%)
    all_to_all x3, blocking collectives, exchange(): return lax.all_to_all(blocks, axes, 0, 0, tiled=True).reshape(rows.shape)  72.6 us
    all_to_all x3, waiting for transfers between devices, exchange(): return lax.all_to_all(blocks, axes, 0, 0, tiled=True).reshape(rows.shape)  42.8 us
    pallas_call x8, Pallas kernels, call(): pl.pallas_call(kernel, out_shape=shape, in_specs=[pl.BlockSpec(memory_spa...  26.2 us
    all_to_all x3, starting transfers between devices, exchange(): return lax.all_to_all(blocks, axes, 0, 0, tiled=True).reshape(rows.shape)  17.2 us
    unnamed x34, local copies, waits for them, and re-layouts  7.39 us
    ppermute x1, starting transfers between devices, on_device(): other = lax.ppermute(own, 'core', [(0, 1), (1, 0)])  4.49 us
  transfers between devices with their start and end apart: 4, of which 3 were waited for; matrix products, arithmetic and copies ran while one was open for 0% of the time, Pallas kernels for 4%

profile of v5, /device:TPU:1, one launch (start us, length us, event | category | flops | bytes accessed | tf_op | source)
XLA Modules:
  0.0 176.0 jit_solution(4456201668488932456)
XLA Ops:
  0.6 0.7 pad_maximum_fusion.241.node_ref
  1.4 1.3 shard_map.110
  2.6 44.4 %all_to_all.90 = f32[256,5,1,128]{3,2,1,0:T(1,128)S(1)} all-to-all(f32[256,5,1,128]{3,2,1,0:T(1,128)S(1)} %bitcast.277), channel_id=1, replica_groups=mesh['cy'=8,'core'=2,'gy'=4,'gz'=8] {'cy','gy','gz'}, dimensions={0} | all-to-all | bytes 1310720 | tf_op jit(solution)/shard_map/all_to_all | solution.py:648
  47.0 4.5 %collective-permute-start.66 = (f32[1280,128]{1,0:T(8,128)S(1)}, f32[1280,128]{1,0:T(8,128)S(1)}, u32[]{:S(2)}, u32[]{:S(2)}) collective-permute-start(f32[1280,128]{1,0:T(8,128)S(1)} %bitcast.275), channel_id=1, source_target_pairs={{0,32},{32,0},{1,33},{33,1},{2,34},{34,2},{3,35},{35,3},{4,36},{36... | collective-permute-start | bytes 1966088 | tf_op jit(solution)/shard_map/ppermute | solution.py:693
  51.5 1.7 collective-permute-done.66.other_ref
  53.2 2.3 %shard_map.111 = (f32[16,4,8,128]{3,2,1,0:T(8,128)S(1)}, f32[3,16,4,8,128]{4,3,2,1,0:T(8,128)S(1)}, f32[3,16,4,8,128]{4,3,2,1,0:T(8,128)S(1)}, f32[16,4,8,128]{3...) custom-call(s32[1]{0:T(128)} %bitcast.73.core_ref, f32[1280,128]{1,0:T(8,128)S(1)} %bitcast.276, ...), custom_call_target="tpu_custom_call" | custom-call | tf_op jit(solution)/shard_map/pallas_call | solution.py:625
  55.5 0.0 copy-start.1
  55.5 0.9 copy-done.1
  56.4 0.0 copy-start.3
  56.4 0.9 copy-done.3
  57.3 0.0 copy-start.5
  57.3 0.7 copy-done.5
  58.0 0.0 copy-start.7
  58.0 3.9 %all-to-all-start.16 = ((f32[4,8,128]{2,1,0:T(8,128)}), f32[4,8,128]{2,1,0:T(8,128)S(1)}, u32[]{:S(2)}, u32[]{:S(2)}) async-start(f32[4,8,128]{2,1,0:T(8,128)} %bitcast.85), calls=%async_computation.16 | async-start | bytes 32768 | tf_op jit(solution)/shard_map/all_to_all | solution.py:648
  61.9 0.0 copy-start.2
  61.9 1.1 copy-done.2
  63.0 0.0 copy-start.4
  63.0 1.1 copy-done.4
  64.2 0.0 copy-start.6
  64.2 0.9 copy-done.6
  65.1 6.6 %shard_map.112.terms_ref = f32[11,16,4,8,128]{4,3,2,1,0:T(8,128)S(1)} custom-call(f32[16,4,8,128]{3,2,1,0:T(8,128)S(1)} %get-tuple-element.52.vectors_ref, f32[3,16,4,8,128]{4,3,2,1,0:T(8,128)S(1)} %copy-done.2, f32[3,16,4,8,128]{4,3,2,1,0:T(8,128)S(1)} %copy-done.4, f32[16,4,8,128]{3,2,1,0:T(8,128)S(1)} %get-tuple-element.55.diagonal_ref, ...), custom_call_target="tpu_custom_call" | custom-call | tf_op jit(solution)/shard_map/pallas_call | solution.py:625
  71.7 0.0 all-to-all-done.16
  71.7 0.0 copy-done.7
  71.7 0.0 copy-start.12
  71.7 1.7 shard_map.113
  73.4 0.0 copy-start
  73.4 1.0 copy-done
  74.4 0.0 copy-start.10
  74.4 0.0 copy-start.9
  74.4 0.0 copy-start.11
  74.4 9.3 %all-to-all-start.17 = ((f32[512,4,1,128]{3,1,2,0:T(4,128)}), f32[512,4,1,128]{3,1,2,0:T(4,128)S(1)}, u32[]{:S(2)}, u32[]{:S(2)}) async-start(f32[512,4,1,128]{3,1,2,0:T(4,128)} %bitcast.274), calls=%async_computation.17 | async-start | bytes 2097152 | tf_op jit(solution)/shard_map/all_to_all | solution.py:648
  83.7 0.0 copy-start.8
  83.7 0.0 copy-start.13
  83.7 0.0 copy-done.12
  83.7 0.1 reshape_reshape.7
  83.8 32.8 %all-to-all-done.17 = f32[512,4,1,128]{3,1,2,0:T(4,128)S(1)} async-done(((f32[512,4,1,128]{3,1,2,0:T(4,128)}), f32[512,4,1,128]{3,1,2,0:T(4,128)S(1)}, u32[]{:S(2)}, u32[]{:S(2)}) %all-to-all-start.17) | async-done | bytes 1048608 | tf_op jit(solution)/shard_map/all_to_all | solution.py:648
  116.6 0.7 shard_map.114
  117.3 15.1 %all_to_all.91 = f32[32,16,128]{2,1,0:T(8,128)S(1)} all-to-all(f32[32,16,128]{2,1,0:T(8,128)S(1)} %bitcast.280), channel_id=1, replica_groups=mesh['cy'=8,'core'=2,'gy'=4,'gz'=8] {'cy','gy'}, dimensions={0} | all-to-all | bytes 524288 | tf_op jit(solution)/shard_map/all_to_all | solution.py:648
  132.5 13.1 %all_to_all.92 = f32[16,16,128]{2,1,0:T(8,128)S(1)} all-to-all(f32[16,16,128]{2,1,0:T(8,128)S(1)} %bitcast.281), channel_id=1, replica_groups=mesh['cy'=8,'core'=2,'gy'=4,'gz'=8] {'core','gz'}, dimensions={0} | all-to-all | bytes 262144 | tf_op jit(solution)/shard_map/all_to_all | solution.py:648
  145.6 0.7 shard_map.116
  146.4 4.1 %all-to-all-start.20 = ((f32[32,16,128]{2,1,0:T(8,128)}), f32[32,16,128]{2,1,0:T(8,128)S(1)}, u32[]{:S(2)}, u32[]{:S(2)}) async-start(f32[32,16,128]{2,1,0:T(8,128)} %bitcast.94), calls=%async_computation.20 | async-start | bytes 524288 | tf_op jit(solution)/shard_map/all_to_all | solution.py:648
  150.5 0.0 copy-done.10
  150.5 0.1 copy.366
  150.6 0.0 copy-done.9
  150.6 0.1 select_multiply_fusion
  150.7 10.0 %all-to-all-done.20 = f32[32,16,128]{2,1,0:T(8,128)S(1)} async-done(((f32[32,16,128]{2,1,0:T(8,128)}), f32[32,16,128]{2,1,0:T(8,128)S(1)}, u32[]{:S(2)}, u32[]{:S(2)}) %all-to-all-start.20) | async-done | bytes 262176 | tf_op jit(solution)/shard_map/all_to_all | solution.py:648
  160.8 0.0 copy-done.11
  160.8 12.8 %shard_map.117 = (f32[48,4,256]{2,1,0:T(4,128)S(1)}, f32[256,256]{1,0:T(8,128)}, f32[24,8]{1,0:T(8,128)S(1)}, f32[48,4,16]{2,1,0:T(4,128)S(1)}, f32[8,128]{1,0:T(8,128)S(1)}) custom-call(f32[512,128]{1,0:T(8,128)S(1)} %bitcast.278, f32[2048,128]{1,0:T(8,128)S(1)} %bitcast.273, f32[1,256]{1,0:T(1,128)S(1)} %pad.5.mass_ref, f32[48,4,16]{2,1,0:T(4,128)S(1)} %bitcast.283, ...), custom_call_target="tpu_custom_call" | custom-call | tf_op jit(solution)/shard_map/pallas_call | solution.py:625
  173.6 0.1 copy.367
  173.7 0.5 slice.715
  174.8 0.0 copy-done.8
  174.9 0.0 copy-done.13
  174.9 0.4 conditional.1
  175.2 0.1 copy.379
  175.3 0.0 copy-start.14
  175.3 0.0 copy-start.15
  175.3 0.0 copy-start.16
  175.3 0.6 copy-done.14
  175.9 0.1 copy-done.15
  176.0 0.0 copy-done.16
  (4 shorter events, 0.1 us)
Async XLA Ops:
  47.0 6.2 %collective-permute-start.66 = (f32[1280,128]{1,0:T(8,128)S(1)}, f32[1280,128]{1,0:T(8,128)S(1)}, u32[]{:S(2)}, u32[]{:S(2)}) collective-permute-start(f32[1280,128]{1,0:T(8,128)S(1)} %bitcast.275), channel_id=1, source_target_pairs={{0,32},{32,0},{1,33},{33,1},{2,34},{34,2},{3,35},{35,3},{4,36},{36... | collective-permute-start | bytes 1966088 | tf_op jit(solution)/shard_map/ppermute | solution.py:693
  55.5 0.9 copy-start.1
  56.4 0.9 copy-start.3
  57.3 0.7 copy-start.5
  58.0 13.7 %copy-start.7 = (f32[40,128]{1,0:T(8,128)S(1)}, f32[40,128]{1,0:T(8,128)}, u32[]{:S(2)}) copy-start(f32[40,128]{1,0:T(8,128)} %constant.132.clone.nodes_ref) | copy-start | bytes 61444
  58.0 13.7 %all-to-all-start.16 = ((f32[4,8,128]{2,1,0:T(8,128)}), f32[4,8,128]{2,1,0:T(8,128)S(1)}, u32[]{:S(2)}, u32[]{:S(2)}) async-start(f32[4,8,128]{2,1,0:T(8,128)} %bitcast.85), calls=%async_computation.16 | async-start | bytes 32768 | tf_op jit(solution)/shard_map/all_to_all | solution.py:648
  61.9 1.1 copy-start.2
  63.0 1.1 copy-start.4
  64.2 0.9 copy-start.6
  71.7 12.0 %copy-start.12 = (f32[3,2,8,4]{2,3,1,0:T(4,128)S(1)}, f32[3,2,8,4]{2,3,1,0:T(4,128)}, u32[]{:S(2)}) copy-start(f32[3,2,8,4]{2,3,1,0:T(4,128)} %param.13) | copy-start | bytes 2308
  73.4 1.0 copy-start
  74.4 76.1 %copy-start.10 = (f32[3,3,2,8,4]{3,4,2,1,0:T(4,128)S(1)}, f32[3,3,2,8,4]{3,4,2,1,0:T(4,128)}, u32[]{:S(2)}) copy-start(f32[3,3,2,8,4]{3,4,2,1,0:T(4,128)} %param.15) | copy-start | bytes 6916
  74.4 76.2 %copy-start.9 = (s32[3,16,2,8,4]{1,4,3,2,0:T(4,128)S(1)}, s32[3,16,2,8,4]{1,4,3,2,0:T(4,128)}, u32[]{:S(2)}) copy-start(s32[3,16,2,8,4]{1,4,3,2,0:T(4,128)} %param.16) | copy-start | bytes 36868
  74.4 86.4 %copy-start.11 = (f32[3,16,2,8,4]{1,4,3,2,0:T(4,128)S(1)}, f32[3,16,2,8,4]{1,4,3,2,0:T(4,128)}, u32[]{:S(2)}) copy-start(f32[3,16,2,8,4]{1,4,3,2,0:T(4,128)} %param.17) | copy-start | bytes 36868
  74.4 42.2 %all-to-all-start.17 = ((f32[512,4,1,128]{3,1,2,0:T(4,128)}), f32[512,4,1,128]{3,1,2,0:T(4,128)S(1)}, u32[]{:S(2)}, u32[]{:S(2)}) async-start(f32[512,4,1,128]{3,1,2,0:T(4,128)} %bitcast.274), calls=%async_computation.17 | async-start | bytes 2097152 | tf_op jit(solution)/shard_map/all_to_all | solution.py:648
  83.7 91.1 %copy-start.8 = (f32[3,2,8,4,256]{4,3,2,1,0:T(4,128)S(1)}, f32[3,2,8,4,256]{4,3,2,1,0:T(4,128)}, u32[]{:S(2)}) copy-start(f32[3,2,8,4,256]{4,3,2,1,0:T(4,128)} %param.12) | copy-start | bytes 589828
  83.7 91.1 %copy-start.13 = (f32[3,2,8,4]{2,3,1,0:T(4,128)S(1)}, f32[3,2,8,4]{2,3,1,0:T(4,128)}, u32[]{:S(2)}) copy-start(f32[3,2,8,4]{2,3,1,0:T(4,128)} %param.14) | copy-start | bytes 2308
  146.4 14.4 %all-to-all-start.20 = ((f32[32,16,128]{2,1,0:T(8,128)}), f32[32,16,128]{2,1,0:T(8,128)S(1)}, u32[]{:S(2)}, u32[]{:S(2)}) async-start(f32[32,16,128]{2,1,0:T(8,128)} %bitcast.94), calls=%async_computation.20 | async-start | bytes 524288 | tf_op jit(solution)/shard_map/all_to_all | solution.py:648
  175.3 0.6 copy-start.14
  175.3 0.7 copy-start.15
  175.3 0.7 copy-start.16

commit v6 on v5

--- a/solution.py
+++ b/solution.py
@@ -19,6 +19,9 @@
 NODES = 64
 DEVICES = 512
 OUT_ROWS = 5
+LEAST_PIVOT = 0.1
+BLOCK = 32
+CHUNK = 17
 LEAST_PIVOT = 0.1
 BLOCK = 32
 STIFF_LANE = 9
@@ -156,15 +159,17 @@
     return here, (turned.sides(gx), (y_up(here), y_down(here)), (z_up(here), z_down(here)))
 
 
+UP, DOWN, DIAGONAL, MASS, KINDS = 1, 4, 7, 8, 9
+
+
 def weights_kernel(
-    core_ref, own_ref, other_ref, vectors_ref, up_ref, down_ref, diagonal_ref, mass_ref, top_ref,
-    tangent_ref
+    core_ref, own_ref, other_ref, held_ref, top_ref, tangent_ref
 ):
     core = core_ref[0]
     refs = (own_ref, other_ref)
     second = []
     for gx in range(16):
-        vectors_ref[gx] = grid_row(refs, core, gx, core)
+        held_ref[gx, 0] = grid_row(refs, core, gx, core)
         first, along_y = both_halves(grid_row(refs, 2, gx, core))
         tangent_ref[gx] = first
         second.append(along_y)
@@ -187,44 +192,41 @@
         ]
         total = (ups[0] + ups[1] + ups[2]) + (downs[0] + downs[1] + downs[2])
         for direction in range(3):
-            up_ref[direction, gx] = ups[direction]
-            down_ref[direction, gx] = downs[direction]
+            held_ref[gx, UP + direction] = ups[direction]
+            held_ref[gx, DOWN + direction] = downs[direction]
         diagonal = spring + total
-        diagonal_ref[gx] = diagonal
-        mass_ref[gx] = mass
+        held_ref[gx, DIAGONAL] = diagonal
+        held_ref[gx, MASS] = mass
         best = jnp.maximum(best, (diagonal + total) / mass)
     best = jnp.max(jnp.max(best, axis=0), axis=(0, 1), keepdims=True)
     top_ref[...] = jnp.broadcast_to(best, (32, 128))
 
 
-def filter_kernel(
-    vectors_ref, up_ref, down_ref, diagonal_ref, mass_ref, top_ref, terms_ref, inverse_ref
-):
+def filter_kernel(held_ref, top_ref, terms_ref, inverse_ref):
     top = top_ref[0:1, :]
     inverse_spread = 1.0 / (top * 7.0 / 16.0)
     ratio = (top * 9.0 / 16.0) * inverse_spread
     for gx in range(16):
-        inverse_ref[gx] = inverse_spread / mass_ref[gx]
-        terms_ref[0, gx] = vectors_ref[gx]
-        terms_ref[TOTAL + 2, gx] = mass_ref[gx]
+        mass = held_ref[gx, MASS]
+        inverse_ref[gx] = inverse_spread / mass
+        terms_ref[0, gx] = held_ref[gx, 0]
+        terms_ref[TOTAL + 2, gx] = mass
     for degree in range(1, TOTAL + 2):
-        current_ref = vectors_ref if degree == 1 else terms_ref.at[degree - 1]
+        current_ref = terms_ref.at[degree - 1]
         turned = Turned(current_ref)
         for gx in range(16):
             here, sides = around(current_ref, turned, gx)
-            image = diagonal_ref[gx] * here
+            image = held_ref[gx, DIAGONAL] * here
             for direction in range(3):
-                image = image - up_ref[direction, gx] * sides[direction][0]
-                image = image - down_ref[direction, gx] * sides[direction][1]
+                image = image - held_ref[gx, UP + direction] * sides[direction][0]
+                image = image - held_ref[gx, DOWN + direction] * sides[direction][1]
             image = image * inverse_ref[gx] - ratio * here
             if degree > 1:
                 image = 2.0 * image - terms_ref[degree - 2, gx]
             terms_ref[degree, gx] = image
 
 
-def combine_kernel(
-    comp_ref, terms_ref, own_top_ref, top_ref, nodes_ref, out_ref, even_ref, image_ref
-):
+def combine_kernel(terms_ref, own_top_ref, top_ref, nodes_ref, out_ref):
     top = jnp.max(jnp.max(top_ref[...], axis=0, keepdims=True), axis=1, keepdims=True)
     own_top = own_top_ref[0:1, :]
     part = own_top / top
@@ -242,96 +244,65 @@
             if degree <= TOTAL:
                 total = total + coefficients[degree : degree + 1, :] * term
             scaled = scaled + coefficients[16 + degree : 17 + degree, :] * term
-        even_ref[gx] = total
-        image_ref[gx] = terms_ref[TOTAL + 2, gx] * (middle * total + spread * scaled)
-
-    comp = comp_ref[0]
-    turned = Turned(even_ref)
-    stiff_sum = jnp.zeros((4, 8, 128), jnp.float32)
-    mass_sum = jnp.zeros((4, 8, 128), jnp.float32)
-    for gx in range(16):
-        here, sides = around(even_ref, turned, gx)
-        axial = [0.5 * (up - down) for up, down in sides]
-        bending = [(up - 2.0 * here) + down for up, down in sides]
-        image = image_ref[gx]
-        values = [
-            here,
-            image,
-            jnp.where(comp == 0, bending[2], jnp.where(comp == 1, axial[1], axial[2])),
-            jnp.where(comp == 0, axial[0], jnp.where(comp == 1, bending[0], bending[1])),
-        ]
-        for kind in range(4):
-            out_ref[pl.ds(gx * 128 + kind, 32, stride=4), :] = values[kind].reshape(32, 128)
-        stiff_sum = stiff_sum + here * image
-        mass_sum = mass_sum + here * terms_ref[TOTAL + 2, gx]
-    lane = lax.broadcasted_iota(jnp.int32, (1, 128), 1)
-    sums = []
-    for value in (stiff_sum, mass_sum):
-        value = jnp.sum(jnp.sum(value, axis=0), axis=0, keepdims=True)
-        low = jnp.sum(jnp.where(lane < 64, value, 0.0), axis=1, keepdims=True)
-        high = jnp.sum(jnp.where(lane < 64, 0.0, value), axis=1, keepdims=True)
-        sums.append(jnp.where(lane < 64, low, high))
-    for gx in range(16):
-        rows = pl.ds(gx * 128 + 2, 32, stride=4)
-        value = jnp.where((lane & 63) == STIFF_LANE, sums[0], out_ref[rows, :])
-        out_ref[rows, :] = jnp.where((lane & 63) == MASS_LANE, sums[1], value)
+        image = terms_ref[TOTAL + 2, gx] * (middle * total + spread * scaled)
+        out_ref[pl.ds(gx * 64, 32, stride=2), :] = total.reshape(32, 128)
+        out_ref[pl.ds(gx * 64 + 1, 32, stride=2), :] = image.reshape(32, 128)
 
 
 def parts_of(rows_ref, kind):
     return [
         jnp.concatenate(
-            [rows_ref[pl.ds((gx * 4 + comp) * 32 + kind, 8, stride=4), :] for gx in range(16)],
+            [rows_ref[pl.ds((gx * 4 + comp) * 16 + kind, 8, stride=2), :] for gx in range(16)],
             axis=0,
         )
         for comp in range(3)
     ]
 
 
+def pair_rows(one, two):
+    low = lax.broadcasted_iota(jnp.int32, (128, 128), 1) < 64
+    upper = jnp.where(low, one, 0.0 if two is None else pltpu.roll(two, 64, 1))
+    lower = jnp.where(low, pltpu.roll(one, 64, 1), 0.0 if two is None else two)
+    return jnp.concatenate([upper, lower], axis=0)
+
+
 def by_vector(parts):
-    low = lax.broadcasted_iota(jnp.int32, (128, 128), 1) < 64
-    turned = [pltpu.roll(part, 64, 1) for part in parts]
-    upper = [jnp.where(low, parts[0], turned[1]), jnp.where(low, parts[2], 0.0)]
-    lower = [jnp.where(low, turned[0], parts[1]), jnp.where(low, turned[2], 0.0)]
     return jnp.concatenate(
-        [jnp.concatenate(upper, axis=1), jnp.concatenate(lower, axis=1)], axis=0
-    )
-
-
-def one_lane(part, place):
-    return jnp.concatenate(
-        [jnp.broadcast_to(part[:, at : at + 1], (128, 128)) for at in (place, 64 + place)], axis=0
-    )
-
-
-def untucked(vectors, mixed):
-    lane = lax.broadcasted_iota(jnp.int32, (128, 128), 1) & 63
-    fixed = []
-    for comp in range(3):
-        here = vectors[comp]
-        step = 1 if comp == 1 else 8
-        above = pltpu.roll(here, 128 - step, 1)
-        below = pltpu.roll(here, step, 1)
-        value = (above - 2.0 * here) + below if comp == 0 else 0.5 * (above - below)
-        held = (lane == STIFF_LANE) | (lane == MASS_LANE)
-        fixed.append(jnp.where(held, value, mixed[comp]))
-    return fixed
-
-
-def product_kernel(rows_ref, mass_ref, out_ref):
-    vectors = by_vector(parts_of(rows_ref, 0))
+        [pair_rows(parts[0], parts[1]), pair_rows(parts[2], None)], axis=1
+    )
+
+
+def product_kernel(rows_ref, mass_ref, out_ref, along_x_ref, along_y_ref, along_z_ref):
+    parts = parts_of(rows_ref, 0)
+    vectors = by_vector(parts)
+    along_x_ref[...] = vectors[:, :128]
+    along_y_ref[...] = pair_rows(parts[1], parts[2])
+    along_z_ref[...] = pair_rows(parts[2], parts[0])
     image = by_vector(parts_of(rows_ref, 1))
-    gram = dot(vectors * mass_ref[...], vectors, ((1,), (1,)))
+    weighted = vectors * mass_ref[...]
+    gram = dot(weighted, vectors, ((1,), (1,)))
     stiff = dot(vectors, image, ((1,), (1,)))
     row = lax.broadcasted_iota(jnp.int32, (256, 256), 0)
     column = lax.broadcasted_iota(jnp.int32, (256, 256), 1)
     both = jnp.where(row >= column, gram, stiff)
-    out_ref[:256, :] = both[:, :128]
-    out_ref[256:, :] = both[:, 128:]
+    diagonal = jnp.sum(vectors * image, axis=1, keepdims=True)
+    lane = lax.broadcasted_iota(jnp.int32, (256, 128), 1)
+    lateral = jnp.sum(jnp.where(lane < NODES, weighted[:, :128], 0.0), axis=1, keepdims=True)
+    further = jnp.where(lane == 0, diagonal, jnp.where(lane == 1, lateral, 0.0)).T
+    for chunk in range(32):
+        half = slice(0, 128) if chunk < 16 else slice(128, 256)
+        first = chunk % 16 * 16
+        out_ref[chunk * CHUNK : chunk * CHUNK + 16, :] = both[first : first + 16, half]
+        last = further[chunk // 2 : chunk // 2 + 1, chunk % 2 * 128 : chunk % 2 * 128 + 128]
+        out_ref[chunk * CHUNK + 16 : chunk * CHUNK + 17, :] = last
 
 
 def total_kernel(count, copies, rows_ref, out_ref):
-    total = jnp.sum(rows_ref[...].reshape(count, 16, 128), axis=0)
-    out_ref[...] = jnp.broadcast_to(total[None], (copies, 16, 128)).reshape(copies * 16, 128)
+    total = rows_ref[0:CHUNK, :]
+    for place in range(1, count):
+        total = total + rows_ref[place * CHUNK : place * CHUNK + CHUNK, :]
+    for place in range(copies):
+        out_ref[place * CHUNK : place * CHUNK + CHUNK, :] = total
 
 
 def factor_block(gram, stiff):
@@ -458,14 +429,21 @@
 
 
 def final_kernel(
-    sums_ref, rows_ref, mass_ref, modulus_ref, stress_ref, subspace_ref, projected_ref, force_ref,
+    sums_ref, rows_ref, above_x_ref, below_x_ref, above_y_ref, below_y_ref, above_z_ref,
+    below_z_ref, mass_ref, modulus_ref, stress_ref, subspace_ref, projected_ref, force_ref,
     stress_new_ref, least_ref, m_ref
 ):
-    both = jnp.concatenate([sums_ref[:256, :], sums_ref[256:, :]], axis=1)
-    mixed = parts_of(rows_ref, 2)
-    diagonal = one_lane(mixed[0] + mixed[1] + mixed[2], STIFF_LANE)
+    chunks = [sums_ref[chunk * CHUNK : chunk * CHUNK + 16, :] for chunk in range(32)]
+    both = jnp.concatenate(
+        [jnp.concatenate(chunks[:16], axis=0), jnp.concatenate(chunks[16:], axis=0)], axis=1
+    )
+    further = [
+        jnp.broadcast_to(sums_ref[chunk * CHUNK + 16 : chunk * CHUNK + 17, :], (128, 128)).T
+        for chunk in range(4)
+    ]
+    diagonal = jnp.concatenate(further[:2], axis=0)
     diagonal = jnp.concatenate([diagonal, diagonal], axis=1)
-    lateral = one_lane(mixed[0], MASS_LANE)
+    lateral = jnp.concatenate(further[2:], axis=0)
     turned = both.T
     row = lax.broadcasted_iota(jnp.int32, (256, 256), 0)
     column = lax.broadcasted_iota(jnp.int32, (256, 256), 1)
@@ -479,43 +457,57 @@
     least_ref[...] = jnp.broadcast_to(least, (8, 128))
     lower = jnp.where(row >= column, m_ref[0], 0.0)
     stiff_lower = jnp.where(row >= column, m_ref[1], 0.0)
-    parts = parts_of(rows_ref, 0)
-    vectors = by_vector(parts)
-    mixed = untucked(parts, mixed)
-    other = parts_of(rows_ref, 3)
+    vectors = by_vector(parts_of(rows_ref, 0))
     subspace = dot(vectors.T, lower, ((1,), (1,)))
     subspace = subspace * jnp.sqrt(jnp.float32(DEVICES * 3 * NODES))
     projected_ref[...] = dot(lower, dot(stiff, lower, ((1,), (1,))))
     weights = dot(stiff_lower.T, dot(stiff_lower, lateral))
     weights = jnp.concatenate([weights, weights], axis=1)
-    axial = by_vector([other[0], mixed[1], mixed[2]])
-    bending = by_vector([mixed[0], other[1], other[2]])
-    fields = [
-        jnp.sum(value * weights, axis=0, keepdims=True) for value in (vectors, axial, bending)
+    displace = jnp.sum(vectors * weights, axis=0, keepdims=True)
+    own = [displace[:, :128], pltpu.roll(displace[:, :128], 64, 1), displace[:, 128:]]
+    outside = [
+        jnp.sum(ref[...] * weights[:, :128], axis=0, keepdims=True)
+        for ref in (above_x_ref, below_x_ref, above_y_ref, below_y_ref, above_z_ref, below_z_ref)
     ]
+    lane = lax.broadcasted_iota(jnp.int32, (1, 128), 1)
+    axial = []
+    bending = []
+    for direction, (step, mask) in enumerate(((32, 32), (1, 7), (8, 24))):
+        wide = jnp.where(lane < 64, own[direction], pltpu.roll(own[(direction + 1) % 3], 64, 1))
+        above = jnp.where(
+            (lane & mask) == mask,
+            pltpu.roll(outside[2 * direction], mask, 1),
+            pltpu.roll(wide, 128 - step, 1),
+        )
+        below = jnp.where(
+            (lane & mask) == 0,
+            pltpu.roll(outside[2 * direction + 1], 128 - mask, 1),
+            pltpu.roll(wide, step, 1),
+        )
+        axial.append(0.5 * (above - below))
+        bending.append(pltpu.roll((above - 2.0 * wide) + below, 64, 1))
     lane = lax.broadcasted_iota(jnp.int32, (24, 256), 1)
     group = lax.broadcasted_iota(jnp.int32, (24, 256), 0)
-    laid = jnp.where((lane >> 3) == group, fields[0] * mass_ref[...], 0.0)
+    laid = jnp.where((lane >> 3) == group, displace * mass_ref[...], 0.0)
     column = lax.broadcasted_iota(jnp.int32, (256, 128), 0)
     place = lax.broadcasted_iota(jnp.int32, (256, 128), 1)
     force_ref[...] = dot(laid, jnp.where((column & 7) == place, 1.0, 0.0))[:, :8]
     columns = jnp.concatenate(
-        [fields[1], fields[2], jnp.zeros((126, 256), jnp.float32)], axis=0
+        axial + bending + [jnp.zeros((122, 128), jnp.float32)], axis=0
     ).T
-    axial = jnp.broadcast_to(columns[:, 0:1], (256, 16))
-    bending = jnp.broadcast_to(columns[:, 1:2], (256, 16))
+    axial = [jnp.broadcast_to(columns[:, d : d + 1], (128, 16)) for d in range(3)]
+    bending = [jnp.broadcast_to(columns[:, 3 + d : 4 + d], (128, 16)) for d in range(3)]
     fiber = lax.broadcasted_iota(jnp.int32, (8, 16), 1).astype(jnp.float32)
     heights = (fiber + 0.5) / 16.0 - 0.5
     for direction in range(3):
-        other = (direction + 1) % 3
         for x in range(2):
             for z in range(4):
                 rows = slice(direction * 16 + x * 8, direction * 16 + x * 8 + 8)
                 inner = x * 32 + z * 8
                 one = direction * NODES + inner
-                two = other * NODES + inner
                 subspace_ref[rows, z, :] = subspace[one : one + 8]
-                strain = axial[one : one + 8] + heights * bending[two : two + 8]
+                strain = axial[direction][inner : inner + 8]
+                strain = strain + heights * bending[direction][inner : inner + 8]
                 stress_new_ref[rows, z, :] = stress_ref[rows, z, :] + modulus_ref[rows, z, :] * strain
 
 
@@ -677,8 +669,7 @@
 
     grid_shape = (16, 4, 8, 128)
     plain = pltpu.VMEM(grid_shape, jnp.float32)
-    grid = jax.ShapeDtypeStruct(grid_shape, jnp.float32)
-    grids = jax.ShapeDtypeStruct((3,) + grid_shape, jnp.float32)
+    planes_shape = (16, KINDS, 4, 8, 128)
     sent = call(
         pack_kernel,
         rows_of(256 * OUT_ROWS),
@@ -692,10 +683,9 @@
     own = exchange(sent, CHIPS, 256)
     other = lax.ppermute(own, "core", [(0, 1), (1, 0)])
     core = lax.axis_index("core").astype(jnp.int32).reshape(1)
-    component = lax.axis_index("gy").astype(jnp.int32).reshape(1)
-    *weights, own_top = call(
+    planes, own_top = call(
         weights_kernel,
-        (grid, grids, grids, grid, grid, rows_of(32)),
+        (jax.ShapeDtypeStruct(planes_shape, jnp.float32), rows_of(32)),
         (plain,),
         smem=(0,),
         operands=(core, own, other),
@@ -705,29 +695,35 @@
         filter_kernel,
         jax.ShapeDtypeStruct((TOTAL + 3,) + grid_shape, jnp.float32),
         (plain,),
-        operands=(*weights, own_top),
+        operands=(planes, own_top),
     )
     filtered = call(
         combine_kernel,
-        rows_of(2048),
-        (plain, plain),
-        smem=(0,),
-        operands=(component, terms, own_top, tops, chebyshev_nodes()),
+        rows_of(1024),
+        operands=(terms, own_top, tops, chebyshev_nodes()),
     )
     returned = exchange(filtered, AXES, DEVICES)
     mass_row = node_rows(node_mass).reshape(1, 3 * NODES)
     mass_row = jnp.pad(mass_row, ((0, 0), (0, NODES)))
-    products = call(product_kernel, rows_of(512), operands=(returned, mass_row))
-    partial = call(
-        functools.partial(total_kernel, 32, 16),
-        rows_of(256),
-        operands=(exchange(products, ("cy", "gy"), 32),),
-    )
-    totals = call(
-        functools.partial(total_kernel, 16, 32),
-        rows_of(512),
-        operands=(exchange(partial, ("core", "gz"), 16),),
-    )
+    along = jax.ShapeDtypeStruct((width, 128), jnp.float32)
+    products, *along = call(
+        product_kernel,
+        (rows_of(32 * CHUNK), along, along, along),
+        operands=(returned, mass_row),
+    )
+    neighbours = []
+    for axis, mine in zip((GX, "gy", "gz"), along):
+        count = lax.axis_size(axis)
+        forward = [(i, i + 1) for i in range(count - 1)]
+        backward = [(target, source) for source, target in forward]
+        neighbours.append(lax.ppermute(mine, axis, backward))
+        neighbours.append(lax.ppermute(mine, axis, forward))
+    part = exchange(products, ("cy", "gy"), 32)
+    part, *neighbours[:4] = lax.optimization_barrier((part, *neighbours[:4]))
+    part = call(functools.partial(total_kernel, 32, 16), rows_of(16 * CHUNK), operands=(part,))
+    part = exchange(part, ("core", "gz"), 16)
+    part, *neighbours[4:] = lax.optimization_barrier((part, *neighbours[4:]))
+    totals = call(functools.partial(total_kernel, 16, 32), rows_of(32 * CHUNK), operands=(part,))
     subspace, projected, force, stress_new, least = call(
         final_kernel,
         (
@@ -741,6 +737,7 @@
         operands=(
             exchange(totals, ("cy", "gy"), 32),
             returned,
+            *neighbours,
             mass_row,
             fibers_last(fiber_modulus(stiffness, yield_flags)),
             fibers_last(stress_old),

time: 178 us -> 175 us (0.983)
  starting transfers between devices: 21.7 us -> 52.7 us
  blocking collectives: 72.6 us -> 44.4 us
  waiting for transfers between devices: 44.5 us -> 40.4 us
  local copies, waits for them, and re-layouts: 8.33 us -> 4.73 us
  Pallas kernels: 26.2 us -> 28.5 us
    all_to_all x3 -> x1, blocking collectives: 72.6 us -> 44.4 us  [exchange(): return lax.all_to_all(blocks, axes, 0, 0, tiled=True).reshape(rows.shape)]
    ppermute x0 -> x6, starting transfers between devices: none -> 17 us  [the longest x3 11.2 us: on_device(): neighbours.append(lax.ppermute(mine, axis, forward))]
    all_to_all x3 -> x5, starting transfers between devices: 17.2 us -> 31.2 us  [exchange(): return lax.all_to_all(blocks, axes, 0, 0, tiled=True).reshape(rows.shape)]
    all_to_all x3 -> x5, waiting for transfers between devices: 42.8 us -> 32.5 us  [exchange(): return lax.all_to_all(blocks, axes, 0, 0, tiled=True).reshape(rows.shape)]
    ppermute x0 -> x6, waiting for transfers between devices: none -> 6.25 us  [the longest x3 4.74 us: on_device(): neighbours.append(lax.ppermute(mine, axis, backward))]
    unnamed x34 -> x24, local copies, waits for them, and re-layouts: 7.39 us -> 3.79 us
    pallas_call x8, Pallas kernels: 26.2 us -> 28.5 us  [call(): pl.pallas_call(kernel, out_shape=shape, in_specs=[pl.BlockSpec(memory_spa...]
  transfers between devices with their start and end apart: 4 -> 12, of which waited for: 3 -> 6; matrix products, arithmetic and copies ran while one was open for 0% -> 0% of each run, Pallas kernels for 4% -> 4%
where the time goes in v6:
time: 175 us; the launch traced here: 173 us
  starting transfers between devices  52.7 us (30%)
  blocking collectives  44.4 us (25%)
  waiting for transfers between devices  40.4 us (23%)
  Pallas kernels  28.5 us (16%)
  local copies, waits for them, and re-layouts  4.73 us (3%)
    all_to_all x1, blocking collectives, exchange(): return lax.all_to_all(blocks, axes, 0, 0, tiled=True).reshape(rows.shape)  44.4 us
    all_to_all x5, waiting for transfers between devices, exchange(): return lax.all_to_all(blocks, axes, 0, 0, tiled=True).reshape(rows.shape)  32.5 us
    all_to_all x5, starting transfers between devices, exchange(): return lax.all_to_all(blocks, axes, 0, 0, tiled=True).reshape(rows.shape)  31.2 us
    pallas_call x8, Pallas kernels, call(): pl.pallas_call(kernel, out_shape=shape, in_specs=[pl.BlockSpec(memory_spa...  28.5 us
    ppermute x3, starting transfers between devices, on_device(): neighbours.append(lax.ppermute(mine, axis, forward))  11.2 us
    ppermute x3, starting transfers between devices, on_device(): neighbours.append(lax.ppermute(mine, axis, backward))  5.78 us
    ppermute x3, waiting for transfers between devices, on_device(): neighbours.append(lax.ppermute(mine, axis, backward))  4.74 us
    ppermute x1, starting transfers between devices, on_device(): other = lax.ppermute(own, 'core', [(0, 1), (1, 0)])  4.49 us
  transfers between devices with their start and end apart: 12, of which 6 were waited for; matrix products, arithmetic and copies ran while one was open for 0% of the time, Pallas kernels for 4%

profile of v6, /device:TPU:1, one launch (start us, length us, event | category | flops | bytes accessed | tf_op | source)
XLA Modules:
  0.0 173.4 jit_solution(14319080584516120692)
XLA Ops:
  0.6 0.7 pad_maximum_fusion.241.node_ref
  1.4 1.3 shard_map.110
  2.6 44.4 %all_to_all.90 = f32[256,5,1,128]{3,2,1,0:T(1,128)S(1)} all-to-all(f32[256,5,1,128]{3,2,1,0:T(1,128)S(1)} %bitcast.275), channel_id=1, replica_groups=mesh['cy'=8,'core'=2,'gy'=4,'gz'=8] {'cy','gy','gz'}, dimensions={0} | all-to-all | bytes 1310720 | tf_op jit(solution)/shard_map/all_to_all | solution.py:640
  47.0 4.5 %collective-permute-start.66 = (f32[1280,128]{1,0:T(8,128)S(1)}, f32[1280,128]{1,0:T(8,128)S(1)}, u32[]{:S(2)}, u32[]{:S(2)}) collective-permute-start(f32[1280,128]{1,0:T(8,128)S(1)} %bitcast.273), channel_id=1, source_target_pairs={{0,32},{32,0},{1,33},{33,1},{2,34},{34,2},{3,35},{35,3},{4,36},{36... | collective-permute-start | bytes 1966088 | tf_op jit(solution)/shard_map/ppermute | solution.py:684
  51.5 1.7 collective-permute-done.66.other_ref
  53.2 2.3 %shard_map.111 = (f32[16,9,4,8,128]{4,3,2,1,0:T(8,128)S(1)}, f32[32,128]{1,0:T(8,128)}) custom-call(s32[1]{0:T(128)} %bitcast.72.core_ref, f32[1280,128]{1,0:T(8,128)S(1)} %bitcast.274, f32[1280,128]{1,0:T(8,128)S(1)} %collective-permute-done.66.other_ref), custom_call_target="tpu_custom_call" | custom-call | tf_op jit(solution)/shard_map/pallas_call | solution.py:617
  55.5 0.0 copy-start
  55.5 1.4 copy-done
  56.9 0.0 copy-start.2
  56.9 3.9 %all-to-all-start.16 = ((f32[4,8,128]{2,1,0:T(8,128)}), f32[4,8,128]{2,1,0:T(8,128)S(1)}, u32[]{:S(2)}, u32[]{:S(2)}) async-start(f32[4,8,128]{2,1,0:T(8,128)} %bitcast.84), calls=%async_computation.16 | async-start | bytes 32768 | tf_op jit(solution)/shard_map/all_to_all | solution.py:640
  60.8 0.0 copy-start.1
  60.8 1.7 copy-done.1
  62.5 6.6 %shard_map.112.terms_ref = f32[11,16,4,8,128]{4,3,2,1,0:T(8,128)S(1)} custom-call(f32[16,9,4,8,128]{4,3,2,1,0:T(8,128)S(1)} %copy-done.1, f32[32,128]{1,0:T(8,128)} %get-tuple-element.61.top_ref.own_top_ref), custom_call_target="tpu_custom_call" | custom-call | tf_op jit(solution)/shard_map/pallas_call | solution.py:617
  69.0 0.0 copy-start.7
  69.1 0.0 all-to-all-done.16
  69.1 0.0 copy-done.2
  69.1 0.0 copy-start.5
  69.1 0.0 copy-start.4
  69.1 2.1 %shard_map.113 = f32[1024,128]{1,0:T(8,128)} custom-call(f32[11,16,4,8,128]{4,3,2,1,0:T(8,128)S(1)} %shard_map.112.terms_ref, f32[32,128]{1,0:T(8,128)} %get-tuple-element.61.top_ref.own_top_ref, f32[32,128]{1,0:T(8,128)S(1)} %bitcast.280, f32[40,128]{1,0:T(8,128)S(1)} %copy-done.2), custom_call_target="tpu_custom_call" | custom-call | tf_op jit(solution)/shard_map/pallas_call | solution.py:617
  71.2 0.0 copy-start.6
  71.2 0.0 copy-start.3
  71.2 0.0 copy-start.8
  71.2 9.3 %all-to-all-start.17 = ((f32[512,2,1,128]{3,1,2,0:T(2,128)}), f32[512,2,1,128]{3,1,2,0:T(2,128)S(1)}, u32[]{:S(2)}, u32[]{:S(2)}) async-start(f32[512,2,1,128]{3,1,2,0:T(2,128)} %bitcast.87), calls=%async_computation.17 | async-start | bytes 1048576 | tf_op jit(solution)/shard_map/all_to_all | solution.py:640
  80.5 0.0 copy-done.7
  80.5 0.1 reshape_reshape.7
  80.6 21.5 %all-to-all-done.17 = f32[512,2,1,128]{3,1,2,0:T(2,128)S(1)} async-done(((f32[512,2,1,128]{3,1,2,0:T(2,128)}), f32[512,2,1,128]{3,1,2,0:T(2,128)S(1)}, u32[]{:S(2)}, u32[]{:S(2)}) %all-to-all-start.17) | async-done | bytes 524320 | tf_op jit(solution)/shard_map/all_to_all | solution.py:640
  102.1 1.4 shard_map.114
  103.5 4.3 %all-to-all-start.18 = ((f32[32,17,1,128]{3,2,1,0:T(1,128)}), f32[32,17,1,128]{3,2,1,0:T(1,128)S(1)}, u32[]{:S(2)}, u32[]{:S(2)}) async-start(f32[32,17,1,128]{3,2,1,0:T(1,128)} %bitcast.89), calls=%async_computation.18 | async-start | bytes 557056 | tf_op jit(solution)/shard_map/all_to_all | solution.py:640
  107.8 3.2 %collective-permute-start.67 = (f32[256,128]{1,0:T(8,128)S(1)}, f32[256,128]{1,0:T(8,128)S(1)}, u32[]{:S(2)}, u32[]{:S(2)}) collective-permute-start(f32[256,128]{1,0:T(8,128)S(1)} %get-tuple-element.63), channel_id=1, source_target_pairs={{32,0},{64,32},{96,64},{128,96},{160,128},{192,160},{224,192},{256... | collective-permute-start | bytes 393224 | tf_op jit(solution)/shard_map/ppermute | solution.py:719
  111.0 3.2 %collective-permute-start.68 = (f32[256,128]{1,0:T(8,128)S(1)}, f32[256,128]{1,0:T(8,128)S(1)}, u32[]{:S(2)}, u32[]{:S(2)}) collective-permute-start(f32[256,128]{1,0:T(8,128)S(1)} %get-tuple-element.63), channel_id=1, source_target_pairs={{0,32},{32,64},{64,96},{96,128},{128,160},{160,192},{192,224},{224... | collective-permute-start | bytes 393224 | tf_op jit(solution)/shard_map/ppermute | solution.py:720
  114.3 1.3 collective-permute-start.69
  115.6 4.0 %collective-permute-start.70 = (f32[256,128]{1,0:T(8,128)S(1)}, f32[256,128]{1,0:T(8,128)S(1)}, u32[]{:S(2)}, u32[]{:S(2)}) collective-permute-start(f32[256,128]{1,0:T(8,128)S(1)} %get-tuple-element.64), channel_id=1, source_target_pairs={{0,8},{8,16},{16,24},{1,9},{9,17},{17,25},{2,10},{10,18},{18,26},{... | collective-permute-start | bytes 393224 | tf_op jit(solution)/shard_map/ppermute | solution.py:720
  119.6 0.0 collective-permute-done.67.above_x_ref
  119.6 0.0 collective-permute-done.68.below_x_ref
  119.6 1.8 %collective-permute-done.69.above_y_ref = f32[256,128]{1,0:T(8,128)S(1)} collective-permute-done((f32[256,128]{1,0:T(8,128)S(1)}, f32[256,128]{1,0:T(8,128)S(1)}, u32[]{:S(2)}, u32[]{:S(2)}) %collective-permute-start.69) | collective-permute-done | bytes 131104 | tf_op jit(solution)/shard_map/ppermute | solution.py:719
  121.4 1.5 collective-permute-done.70.below_y_ref
  122.9 0.0 all-to-all-done.18
  122.9 0.7 shard_map.115
  123.6 3.6 %all-to-all-start.19 = ((f32[16,17,1,128]{3,2,1,0:T(1,128)}), f32[16,17,1,128]{3,2,1,0:T(1,128)S(1)}, u32[]{:S(2)}, u32[]{:S(2)}) async-start(f32[16,17,1,128]{3,2,1,0:T(1,128)} %bitcast.91), calls=%async_computation.19 | async-start | bytes 278528 | tf_op jit(solution)/shard_map/all_to_all | solution.py:640
  127.2 1.3 collective-permute-start.71
  128.5 4.0 %collective-permute-start.72 = (f32[256,128]{1,0:T(8,128)S(1)}, f32[256,128]{1,0:T(8,128)S(1)}, u32[]{:S(2)}, u32[]{:S(2)}) collective-permute-start(f32[256,128]{1,0:T(8,128)S(1)} %get-tuple-element.66), channel_id=1, source_target_pairs={{0,1},{1,2},{2,3},{3,4},{4,5},{5,6},{6,7},{8,9},{9,10},{10,11},{11... | collective-permute-start | bytes 393224 | tf_op jit(solution)/shard_map/ppermute | solution.py:720
  132.5 3.0 %collective-permute-done.71.above_z_ref = f32[256,128]{1,0:T(8,128)S(1)} collective-permute-done((f32[256,128]{1,0:T(8,128)S(1)}, f32[256,128]{1,0:T(8,128)S(1)}, u32[]{:S(2)}, u32[]{:S(2)}) %collective-permute-start.71) | collective-permute-done | bytes 131104 | tf_op jit(solution)/shard_map/ppermute | solution.py:719
  135.5 0.0 collective-permute-done.72.below_z_ref
  135.5 0.0 all-to-all-done.19
  135.5 0.7 shard_map.116
  136.2 10.2 %all-to-all-start.20 = ((f32[32,17,1,128]{3,2,1,0:T(1,128)}), f32[32,17,1,128]{3,2,1,0:T(1,128)S(1)}, u32[]{:S(2)}, u32[]{:S(2)}) async-start(f32[32,17,1,128]{3,2,1,0:T(1,128)} %bitcast.93), calls=%async_computation.20 | async-start | bytes 557056 | tf_op jit(solution)/shard_map/all_to_all | solution.py:640
  146.4 0.0 copy-done.5
  146.5 0.1 copy.378
  146.6 0.0 copy-done.4
  146.6 0.1 select_multiply_fusion
  146.7 11.0 %all-to-all-done.20 = f32[32,17,1,128]{3,2,1,0:T(1,128)S(1)} async-done(((f32[32,17,1,128]{3,2,1,0:T(1,128)}), f32[32,17,1,128]{3,2,1,0:T(1,128)S(1)}, u32[]{:S(2)}, u32[]{:S(2)}) %all-to-all-start.20) | async-done | bytes 278560 | tf_op jit(solution)/shard_map/all_to_all | solution.py:640
  157.7 0.0 copy-done.6
  157.7 13.3 %shard_map.117 = (f32[48,4,256]{2,1,0:T(4,128)S(1)}, f32[256,256]{1,0:T(8,128)}, f32[24,8]{1,0:T(8,128)S(1)}, f32[48,4,16]{2,1,0:T(4,128)S(1)}, f32[8,128]{1,0:T(8,128)S(1)}) custom-call(f32[544,128]{1,0:T(8,128)S(1)} %bitcast.277, f32[1024,128]{1,0:T(8,128)S(1)} %bitcast.272, f32[256,128]{1,0:T(8,128)S(1)} %collective-permute-done.67.above_x_ref, ...), custom_call_target="tpu_custom_call" | custom-call | tf_op jit(solution)/shard_map/pallas_call | solution.py:617
  170.9 0.1 copy.379
  171.1 0.5 slice.715
  172.2 0.0 copy-done.3
  172.2 0.0 copy-done.8
  172.2 0.4 conditional.1
  172.6 0.1 copy.391
  172.7 0.0 copy-start.9
  172.7 0.0 copy-start.11
  172.7 0.6 copy-done.9
  173.3 0.1 copy-done.10
  173.4 0.0 copy-done.11
  (4 shorter events, 0.0 us)
Async XLA Ops:
  47.0 6.2 %collective-permute-start.66 = (f32[1280,128]{1,0:T(8,128)S(1)}, f32[1280,128]{1,0:T(8,128)S(1)}, u32[]{:S(2)}, u32[]{:S(2)}) collective-permute-start(f32[1280,128]{1,0:T(8,128)S(1)} %bitcast.273), channel_id=1, source_target_pairs={{0,32},{32,0},{1,33},{33,1},{2,34},{34,2},{3,35},{35,3},{4,36},{36... | collective-permute-start | bytes 1966088 | tf_op jit(solution)/shard_map/ppermute | solution.py:684
  55.5 1.4 copy-start
  56.9 12.1 %copy-start.2 = (f32[40,128]{1,0:T(8,128)S(1)}, f32[40,128]{1,0:T(8,128)}, u32[]{:S(2)}) copy-start(f32[40,128]{1,0:T(8,128)} %constant.127.clone.nodes_ref) | copy-start | bytes 61444
  56.9 12.1 %all-to-all-start.16 = ((f32[4,8,128]{2,1,0:T(8,128)}), f32[4,8,128]{2,1,0:T(8,128)S(1)}, u32[]{:S(2)}, u32[]{:S(2)}) async-start(f32[4,8,128]{2,1,0:T(8,128)} %bitcast.84), calls=%async_computation.16 | async-start | bytes 32768 | tf_op jit(solution)/shard_map/all_to_all | solution.py:640
  60.8 1.7 copy-start.1
  69.0 11.4 %copy-start.7 = (f32[3,2,8,4]{2,3,1,0:T(4,128)S(1)}, f32[3,2,8,4]{2,3,1,0:T(4,128)}, u32[]{:S(2)}) copy-start(f32[3,2,8,4]{2,3,1,0:T(4,128)} %param.13) | copy-start | bytes 2308
  69.1 77.3 %copy-start.5 = (f32[3,3,2,8,4]{3,4,2,1,0:T(4,128)S(1)}, f32[3,3,2,8,4]{3,4,2,1,0:T(4,128)}, u32[]{:S(2)}) copy-start(f32[3,3,2,8,4]{3,4,2,1,0:T(4,128)} %param.15) | copy-start | bytes 6916
  69.1 77.5 %copy-start.4 = (s32[3,16,2,8,4]{1,4,3,2,0:T(4,128)S(1)}, s32[3,16,2,8,4]{1,4,3,2,0:T(4,128)}, u32[]{:S(2)}) copy-start(s32[3,16,2,8,4]{1,4,3,2,0:T(4,128)} %param.16) | copy-start | bytes 36868
  71.2 86.5 %copy-start.6 = (f32[3,16,2,8,4]{1,4,3,2,0:T(4,128)S(1)}, f32[3,16,2,8,4]{1,4,3,2,0:T(4,128)}, u32[]{:S(2)}) copy-start(f32[3,16,2,8,4]{1,4,3,2,0:T(4,128)} %param.17) | copy-start | bytes 36868
  71.2 101.0 %copy-start.3 = (f32[3,2,8,4,256]{4,3,2,1,0:T(4,128)S(1)}, f32[3,2,8,4,256]{4,3,2,1,0:T(4,128)}, u32[]{:S(2)}) copy-start(f32[3,2,8,4,256]{4,3,2,1,0:T(4,128)} %param.12) | copy-start | bytes 589828
  71.2 101.0 %copy-start.8 = (f32[3,2,8,4]{2,3,1,0:T(4,128)S(1)}, f32[3,2,8,4]{2,3,1,0:T(4,128)}, u32[]{:S(2)}) copy-start(f32[3,2,8,4]{2,3,1,0:T(4,128)} %param.14) | copy-start | bytes 2308
  71.2 30.9 %all-to-all-start.17 = ((f32[512,2,1,128]{3,1,2,0:T(2,128)}), f32[512,2,1,128]{3,1,2,0:T(2,128)S(1)}, u32[]{:S(2)}, u32[]{:S(2)}) async-start(f32[512,2,1,128]{3,1,2,0:T(2,128)} %bitcast.87), calls=%async_computation.17 | async-start | bytes 1048576 | tf_op jit(solution)/shard_map/all_to_all | solution.py:640
  103.5 19.3 %all-to-all-start.18 = ((f32[32,17,1,128]{3,2,1,0:T(1,128)}), f32[32,17,1,128]{3,2,1,0:T(1,128)S(1)}, u32[]{:S(2)}, u32[]{:S(2)}) async-start(f32[32,17,1,128]{3,2,1,0:T(1,128)} %bitcast.89), calls=%async_computation.18 | async-start | bytes 557056 | tf_op jit(solution)/shard_map/all_to_all | solution.py:640
  107.8 11.8 %collective-permute-start.67 = (f32[256,128]{1,0:T(8,128)S(1)}, f32[256,128]{1,0:T(8,128)S(1)}, u32[]{:S(2)}, u32[]{:S(2)}) collective-permute-start(f32[256,128]{1,0:T(8,128)S(1)} %get-tuple-element.63), channel_id=1, source_target_pairs={{32,0},{64,32},{96,64},{128,96},{160,128},{192,160},{224,192},{256... | collective-permute-start | bytes 393224 | tf_op jit(solution)/shard_map/ppermute | solution.py:719
  111.0 8.5 %collective-permute-start.68 = (f32[256,128]{1,0:T(8,128)S(1)}, f32[256,128]{1,0:T(8,128)S(1)}, u32[]{:S(2)}, u32[]{:S(2)}) collective-permute-start(f32[256,128]{1,0:T(8,128)S(1)} %get-tuple-element.63), channel_id=1, source_target_pairs={{0,32},{32,64},{64,96},{96,128},{128,160},{160,192},{192,224},{224... | collective-permute-start | bytes 393224 | tf_op jit(solution)/shard_map/ppermute | solution.py:720
  114.3 7.1 %collective-permute-start.69 = (f32[256,128]{1,0:T(8,128)S(1)}, f32[256,128]{1,0:T(8,128)S(1)}, u32[]{:S(2)}, u32[]{:S(2)}) collective-permute-start(f32[256,128]{1,0:T(8,128)S(1)} %get-tuple-element.64), channel_id=1, source_target_pairs={{8,0},{16,8},{24,16},{9,1},{17,9},{25,17},{10,2},{18,10},{26,18},{... | collective-permute-start | bytes 393224 | tf_op jit(solution)/shard_map/ppermute | solution.py:719
  115.6 7.3 %collective-permute-start.70 = (f32[256,128]{1,0:T(8,128)S(1)}, f32[256,128]{1,0:T(8,128)S(1)}, u32[]{:S(2)}, u32[]{:S(2)}) collective-permute-start(f32[256,128]{1,0:T(8,128)S(1)} %get-tuple-element.64), channel_id=1, source_target_pairs={{0,8},{8,16},{16,24},{1,9},{9,17},{17,25},{2,10},{10,18},{18,26},{... | collective-permute-start | bytes 393224 | tf_op jit(solution)/shard_map/ppermute | solution.py:720
  123.6 11.9 %all-to-all-start.19 = ((f32[16,17,1,128]{3,2,1,0:T(1,128)}), f32[16,17,1,128]{3,2,1,0:T(1,128)S(1)}, u32[]{:S(2)}, u32[]{:S(2)}) async-start(f32[16,17,1,128]{3,2,1,0:T(1,128)} %bitcast.91), calls=%async_computation.19 | async-start | bytes 278528 | tf_op jit(solution)/shard_map/all_to_all | solution.py:640
  127.2 8.3 %collective-permute-start.71 = (f32[256,128]{1,0:T(8,128)S(1)}, f32[256,128]{1,0:T(8,128)S(1)}, u32[]{:S(2)}, u32[]{:S(2)}) collective-permute-start(f32[256,128]{1,0:T(8,128)S(1)} %get-tuple-element.66), channel_id=1, source_target_pairs={{1,0},{2,1},{3,2},{4,3},{5,4},{6,5},{7,6},{9,8},{10,9},{11,10},{12... | collective-permute-start | bytes 393224 | tf_op jit(solution)/shard_map/ppermute | solution.py:719
  128.5 7.0 %collective-permute-start.72 = (f32[256,128]{1,0:T(8,128)S(1)}, f32[256,128]{1,0:T(8,128)S(1)}, u32[]{:S(2)}, u32[]{:S(2)}) collective-permute-start(f32[256,128]{1,0:T(8,128)S(1)} %get-tuple-element.66), channel_id=1, source_target_pairs={{0,1},{1,2},{2,3},{3,4},{4,5},{5,6},{6,7},{8,9},{9,10},{10,11},{11... | collective-permute-start | bytes 393224 | tf_op jit(solution)/shard_map/ppermute | solution.py:720
  136.2 21.4 %all-to-all-start.20 = ((f32[32,17,1,128]{3,2,1,0:T(1,128)}), f32[32,17,1,128]{3,2,1,0:T(1,128)S(1)}, u32[]{:S(2)}, u32[]{:S(2)}) async-start(f32[32,17,1,128]{3,2,1,0:T(1,128)} %bitcast.93), calls=%async_computation.20 | async-start | bytes 557056 | tf_op jit(solution)/shard_map/all_to_all | solution.py:640
  172.7 0.6 copy-start.9
  172.7 0.7 copy-start.10
  172.7 0.7 copy-start.11

commit v7 on v6

--- a/solution.py
+++ b/solution.py
@@ -359,8 +359,9 @@
 
 
 def four_copies(value):
-    value = value + pltpu.roll(value, 32, 1)
-    return value + pltpu.roll(value, 64, 1)
+    return (value + pltpu.roll(value, 32, 1)) + (
+        pltpu.roll(value, 64, 1) + pltpu.roll(value, 96, 1)
+    )
 
 
 def left_groups(first, second):
@@ -711,19 +712,25 @@
         (rows_of(32 * CHUNK), along, along, along),
         operands=(returned, mass_row),
     )
-    neighbours = []
-    for axis, mine in zip((GX, "gy", "gz"), along):
+
+    def from_neighbours(mine, axis, senses):
         count = lax.axis_size(axis)
-        forward = [(i, i + 1) for i in range(count - 1)]
-        backward = [(target, source) for source, target in forward]
-        neighbours.append(lax.ppermute(mine, axis, backward))
-        neighbours.append(lax.ppermute(mine, axis, forward))
+        pairs = [(i, i + 1) for i in range(count - 1)]
+        return [
+            lax.ppermute(mine, axis, [(b, a) for a, b in pairs] if sense > 0 else pairs)
+            for sense in senses
+        ]
+
+    near = from_neighbours(along[0], GX, (1, -1)) + from_neighbours(along[1], "gy", (1,))
     part = exchange(products, ("cy", "gy"), 32)
-    part, *neighbours[:4] = lax.optimization_barrier((part, *neighbours[:4]))
+    part, *near = lax.optimization_barrier((part, *near))
     part = call(functools.partial(total_kernel, 32, 16), rows_of(16 * CHUNK), operands=(part,))
     part = exchange(part, ("core", "gz"), 16)
-    part, *neighbours[4:] = lax.optimization_barrier((part, *neighbours[4:]))
-    totals = call(functools.partial(total_kernel, 16, 32), rows_of(32 * CHUNK), operands=(part,))
+    part = call(functools.partial(total_kernel, 16, 32), rows_of(32 * CHUNK), operands=(part,))
+    part, *along[1:] = lax.optimization_barrier((part, *along[1:]))
+    far = from_neighbours(along[1], "gy", (-1,)) + from_neighbours(along[2], "gz", (1, -1))
+    part = exchange(part, ("cy", "gy"), 32)
+    part, *far = lax.optimization_barrier((part, *far))
     subspace, projected, force, stress_new, least = call(
         final_kernel,
         (
@@ -735,9 +742,10 @@
         ),
         (pltpu.VMEM((2, 256, 256), jnp.float32),),
         operands=(
-            exchange(totals, ("cy", "gy"), 32),
+            part,
             returned,
-            *neighbours,
+            *near,
+            *far,
             mass_row,
             fibers_last(fiber_modulus(stiffness, yield_flags)),
             fibers_last(stress_old),

time: 175 us -> 172 us (0.983)
  the two profiles are of different devices: /device:TPU:1 before, /device:TPU:2 now
where the time goes in v7:
time: 172 us; the launch traced here: 171 us
  blocking collectives  57.2 us (33%)
  starting transfers between devices  45.7 us (27%)
  waiting for transfers between devices  33 us (19%)
  Pallas kernels  27.3 us (16%)
  local copies, waits for them, and re-layouts  4.72 us (3%)
    all_to_all x2, blocking collectives, exchange(): return lax.all_to_all(blocks, axes, 0, 0, tiled=True).reshape(rows.shape)  57.2 us
    all_to_all x4, starting transfers between devices, exchange(): return lax.all_to_all(blocks, axes, 0, 0, tiled=True).reshape(rows.shape)  27.7 us
    pallas_call x8, Pallas kernels, call(): pl.pallas_call(kernel, out_shape=shape, in_specs=[pl.BlockSpec(memory_spa...  27.3 us
    all_to_all x4, waiting for transfers between devices, exchange(): return lax.all_to_all(blocks, axes, 0, 0, tiled=True).reshape(rows.shape)  21.7 us
    ppermute x6, starting transfers between devices, from_neighbours(): lax.ppermute(mine, axis, [(b, a) for a, b in pairs] if sense > 0 else pairs)  16 us
    ppermute x6, waiting for transfers between devices, from_neighbours(): lax.ppermute(mine, axis, [(b, a) for a, b in pairs] if sense > 0 else pairs)  9.24 us
    unnamed x24, local copies, waits for them, and re-layouts  3.78 us
  transfers between devices with their start and end apart: 11, of which 4 were waited for; matrix products, arithmetic and copies ran while one was open for 0% of the time, Pallas kernels for 4%

profile of v7, /device:TPU:2, one launch (start us, length us, event | category | flops | bytes accessed | tf_op | source)
XLA Modules:
  0.0 170.6 jit_solution(14162291046044143792)
XLA Ops:
  0.6 0.7 pad_maximum_fusion.241.node_ref
  1.4 1.3 shard_map.110
  2.6 45.5 %all_to_all.90 = f32[256,5,1,128]{3,2,1,0:T(1,128)S(1)} all-to-all(f32[256,5,1,128]{3,2,1,0:T(1,128)S(1)} %bitcast.275), channel_id=1, replica_groups=mesh['cy'=8,'core'=2,'gy'=4,'gz'=8] {'cy','gy','gz'}, dimensions={0} | all-to-all | bytes 1310720 | tf_op jit(solution)/shard_map/all_to_all | solution.py:641
  48.2 1.9 %collective-permute-start.66 = (f32[1280,128]{1,0:T(8,128)S(1)}, f32[1280,128]{1,0:T(8,128)S(1)}, u32[]{:S(2)}, u32[]{:S(2)}) collective-permute-start(f32[1280,128]{1,0:T(8,128)S(1)} %bitcast.273), channel_id=1, source_target_pairs={{0,32},{32,0},{1,33},{33,1},{2,34},{34,2},{3,35},{35,3},{4,36},{36... | collective-permute-start | bytes 1966088 | tf_op jit(solution)/shard_map/ppermute | solution.py:685
  50.1 2.1 %collective-permute-done.66.other_ref = f32[1280,128]{1,0:T(8,128)S(1)} collective-permute-done((f32[1280,128]{1,0:T(8,128)S(1)}, f32[1280,128]{1,0:T(8,128)S(1)}, u32[]{:S(2)}, u32[]{:S(2)}) %collective-permute-start.66) | collective-permute-done | bytes 655392 | tf_op jit(solution)/shard_map/ppermute | solution.py:685
  52.1 2.3 %shard_map.111 = (f32[16,9,4,8,128]{4,3,2,1,0:T(8,128)S(1)}, f32[32,128]{1,0:T(8,128)}) custom-call(s32[1]{0:T(128)} %bitcast.72.core_ref, f32[1280,128]{1,0:T(8,128)S(1)} %bitcast.274, f32[1280,128]{1,0:T(8,128)S(1)} %collective-permute-done.66.other_ref), custom_call_target="tpu_custom_call" | custom-call | tf_op jit(solution)/shard_map/pallas_call | solution.py:618
  54.5 0.0 copy-start
  54.5 1.4 copy-done
  55.9 0.0 copy-start.2
  55.9 4.6 %all-to-all-start.16 = ((f32[4,8,128]{2,1,0:T(8,128)}), f32[4,8,128]{2,1,0:T(8,128)S(1)}, u32[]{:S(2)}, u32[]{:S(2)}) async-start(f32[4,8,128]{2,1,0:T(8,128)} %bitcast.84), calls=%async_computation.16 | async-start | bytes 32768 | tf_op jit(solution)/shard_map/all_to_all | solution.py:641
  60.5 0.0 copy-start.1
  60.5 1.7 copy-done.1
  62.1 6.6 %shard_map.112.terms_ref = f32[11,16,4,8,128]{4,3,2,1,0:T(8,128)S(1)} custom-call(f32[16,9,4,8,128]{4,3,2,1,0:T(8,128)S(1)} %copy-done.1, f32[32,128]{1,0:T(8,128)} %get-tuple-element.64.top_ref.own_top_ref), custom_call_target="tpu_custom_call" | custom-call | tf_op jit(solution)/shard_map/pallas_call | solution.py:618
  68.7 0.0 copy-start.7
  68.7 0.0 all-to-all-done.16
  68.7 0.0 copy-done.2
  68.8 0.0 copy-start.5
  68.8 0.0 copy-start.4
  68.8 2.1 %shard_map.113 = f32[1024,128]{1,0:T(8,128)} custom-call(f32[11,16,4,8,128]{4,3,2,1,0:T(8,128)S(1)} %shard_map.112.terms_ref, f32[32,128]{1,0:T(8,128)} %get-tuple-element.64.top_ref.own_top_ref, f32[32,128]{1,0:T(8,128)S(1)} %bitcast.281, f32[40,128]{1,0:T(8,128)S(1)} %copy-done.2), custom_call_target="tpu_custom_call" | custom-call | tf_op jit(solution)/shard_map/pallas_call | solution.py:618
  70.9 0.0 copy-start.6
  70.9 0.0 copy-start.3
  70.9 0.0 copy-start.8
  70.9 8.7 %all-to-all-start.17 = ((f32[512,2,1,128]{3,1,2,0:T(2,128)}), f32[512,2,1,128]{3,1,2,0:T(2,128)S(1)}, u32[]{:S(2)}, u32[]{:S(2)}) async-start(f32[512,2,1,128]{3,1,2,0:T(2,128)} %bitcast.87), calls=%async_computation.17 | async-start | bytes 1048576 | tf_op jit(solution)/shard_map/all_to_all | solution.py:641
  79.5 0.0 copy-done.7
  79.5 0.1 reshape_reshape.7
  79.6 21.7 %all-to-all-done.17 = f32[512,2,1,128]{3,1,2,0:T(2,128)S(1)} async-done(((f32[512,2,1,128]{3,1,2,0:T(2,128)}), f32[512,2,1,128]{3,1,2,0:T(2,128)S(1)}, u32[]{:S(2)}, u32[]{:S(2)}) %all-to-all-start.17) | async-done | bytes 524320 | tf_op jit(solution)/shard_map/all_to_all | solution.py:641
  101.3 1.5 shard_map.114
  102.8 5.0 %all-to-all-start.18 = ((f32[32,17,1,128]{3,2,1,0:T(1,128)}), f32[32,17,1,128]{3,2,1,0:T(1,128)S(1)}, u32[]{:S(2)}, u32[]{:S(2)}) async-start(f32[32,17,1,128]{3,2,1,0:T(1,128)} %bitcast.89), calls=%async_computation.18 | async-start | bytes 557056 | tf_op jit(solution)/shard_map/all_to_all | solution.py:641
  107.8 1.3 collective-permute-start.67
  109.1 3.0 %collective-permute-start.68 = (f32[256,128]{1,0:T(8,128)S(1)}, f32[256,128]{1,0:T(8,128)S(1)}, u32[]{:S(2)}, u32[]{:S(2)}) collective-permute-start(f32[256,128]{1,0:T(8,128)S(1)} %get-tuple-element.66), channel_id=1, source_target_pairs={{0,32},{32,64},{64,96},{96,128},{128,160},{160,192},{192,224},{224... | collective-permute-start | bytes 393224 | tf_op jit(solution)/shard_map/ppermute | solution.py:720
  112.1 2.3 %collective-permute-start.69 = (f32[256,128]{1,0:T(8,128)S(1)}, f32[256,128]{1,0:T(8,128)S(1)}, u32[]{:S(2)}, u32[]{:S(2)}) collective-permute-start(f32[256,128]{1,0:T(8,128)S(1)} %get-tuple-element.71), channel_id=1, source_target_pairs={{8,0},{16,8},{24,16},{9,1},{17,9},{25,17},{10,2},{18,10},{26,18},{... | collective-permute-start | bytes 393224 | tf_op jit(solution)/shard_map/ppermute | solution.py:720
  114.4 0.0 collective-permute-done.67.above_x_ref
  114.4 0.0 collective-permute-done.68.below_x_ref
  114.4 6.1 %collective-permute-done.69.above_y_ref = f32[256,128]{1,0:T(8,128)S(1)} collective-permute-done((f32[256,128]{1,0:T(8,128)S(1)}, f32[256,128]{1,0:T(8,128)S(1)}, u32[]{:S(2)}, u32[]{:S(2)}) %collective-permute-start.69) | collective-permute-done | bytes 131104 | tf_op jit(solution)/shard_map/ppermute | solution.py:720
  120.5 0.0 all-to-all-done.18
  120.6 11.7 %all_to_all.91 = f32[16,17,1,128]{3,2,1,0:T(1,128)S(1)} all-to-all(f32[16,17,1,128]{3,2,1,0:T(1,128)S(1)} %bitcast.278), channel_id=1, replica_groups=mesh['cy'=8,'core'=2,'gy'=4,'gz'=8] {'core','gz'}, dimensions={0} | all-to-all | bytes 278528 | tf_op jit(solution)/shard_map/all_to_all | solution.py:641
  132.3 0.8 shard_map.116
  133.0 9.4 %all-to-all-start.20 = ((f32[32,17,1,128]{3,2,1,0:T(1,128)}), f32[32,17,1,128]{3,2,1,0:T(1,128)S(1)}, u32[]{:S(2)}, u32[]{:S(2)}) async-start(f32[32,17,1,128]{3,2,1,0:T(1,128)} %bitcast.93), calls=%async_computation.20 | async-start | bytes 557056 | tf_op jit(solution)/shard_map/all_to_all | solution.py:641
  142.5 0.0 copy-done.5
  142.5 0.1 copy.378
  142.6 1.3 collective-permute-start.71
  143.9 4.6 %collective-permute-start.72 = (f32[256,128]{1,0:T(8,128)S(1)}, f32[256,128]{1,0:T(8,128)S(1)}, u32[]{:S(2)}, u32[]{:S(2)}) collective-permute-start(f32[256,128]{1,0:T(8,128)S(1)} %get-tuple-element.72), channel_id=1, source_target_pairs={{0,1},{1,2},{2,3},{3,4},{4,5},{5,6},{6,7},{8,9},{9,10},{10,11},{11... | collective-permute-start | bytes 393224 | tf_op jit(solution)/shard_map/ppermute | solution.py:720
  148.5 3.6 %collective-permute-start.70 = (f32[256,128]{1,0:T(8,128)S(1)}, f32[256,128]{1,0:T(8,128)S(1)}, u32[]{:S(2)}, u32[]{:S(2)}) collective-permute-start(f32[256,128]{1,0:T(8,128)S(1)} %get-tuple-element.71), channel_id=1, source_target_pairs={{0,8},{8,16},{16,24},{1,9},{9,17},{17,25},{2,10},{10,18},{18,26},{... | collective-permute-start | bytes 393224 | tf_op jit(solution)/shard_map/ppermute | solution.py:720
  152.1 0.0 copy-done.4
  152.1 0.1 select_multiply_fusion
  152.2 3.1 %collective-permute-done.70.below_y_ref = f32[256,128]{1,0:T(8,128)S(1)} collective-permute-done((f32[256,128]{1,0:T(8,128)S(1)}, f32[256,128]{1,0:T(8,128)S(1)}, u32[]{:S(2)}, u32[]{:S(2)}) %collective-permute-start.70) | collective-permute-done | bytes 131104 | tf_op jit(solution)/shard_map/ppermute | solution.py:720
  155.3 0.0 collective-permute-done.71.above_z_ref
  155.3 0.0 collective-permute-done.72.below_z_ref
  155.3 0.0 all-to-all-done.20
  155.3 0.0 copy-done.6
  155.4 12.8 %shard_map.117 = (f32[48,4,256]{2,1,0:T(4,128)S(1)}, f32[256,256]{1,0:T(8,128)}, f32[24,8]{1,0:T(8,128)S(1)}, f32[48,4,16]{2,1,0:T(4,128)S(1)}, f32[8,128]{1,0:T(8,128)S(1)}) custom-call(f32[544,128]{1,0:T(8,128)S(1)} %bitcast.276, f32[1024,128]{1,0:T(8,128)S(1)} %bitcast.272, f32[256,128]{1,0:T(8,128)S(1)} %collective-permute-done.67.above_x_ref, ...), custom_call_target="tpu_custom_call" | custom-call | tf_op jit(solution)/shard_map/pallas_call | solution.py:618
  168.1 0.1 copy.379
  168.2 0.5 slice.715
  169.4 0.0 copy-done.3
  169.4 0.0 copy-done.8
  169.4 0.4 conditional.1
  169.7 0.1 copy.391
  169.8 0.0 copy-start.9
  169.9 0.0 copy-start.10
  169.9 0.0 copy-start.11
  169.9 0.6 copy-done.9
  170.5 0.1 copy-done.10
  170.5 0.0 copy-done.11
  (4 shorter events, 0.1 us)
Async XLA Ops:
  48.2 4.0 %collective-permute-start.66 = (f32[1280,128]{1,0:T(8,128)S(1)}, f32[1280,128]{1,0:T(8,128)S(1)}, u32[]{:S(2)}, u32[]{:S(2)}) collective-permute-start(f32[1280,128]{1,0:T(8,128)S(1)} %bitcast.273), channel_id=1, source_target_pairs={{0,32},{32,0},{1,33},{33,1},{2,34},{34,2},{3,35},{35,3},{4,36},{36... | collective-permute-start | bytes 1966088 | tf_op jit(solution)/shard_map/ppermute | solution.py:685
  54.5 1.4 copy-start
  55.9 12.9 %copy-start.2 = (f32[40,128]{1,0:T(8,128)S(1)}, f32[40,128]{1,0:T(8,128)}, u32[]{:S(2)}) copy-start(f32[40,128]{1,0:T(8,128)} %constant.127.clone.nodes_ref) | copy-start | bytes 61444
  55.9 12.9 %all-to-all-start.16 = ((f32[4,8,128]{2,1,0:T(8,128)}), f32[4,8,128]{2,1,0:T(8,128)S(1)}, u32[]{:S(2)}, u32[]{:S(2)}) async-start(f32[4,8,128]{2,1,0:T(8,128)} %bitcast.84), calls=%async_computation.16 | async-start | bytes 32768 | tf_op jit(solution)/shard_map/all_to_all | solution.py:641
  60.5 1.7 copy-start.1
  68.7 10.8 %copy-start.7 = (f32[3,2,8,4]{2,3,1,0:T(4,128)S(1)}, f32[3,2,8,4]{2,3,1,0:T(4,128)}, u32[]{:S(2)}) copy-start(f32[3,2,8,4]{2,3,1,0:T(4,128)} %param.13) | copy-start | bytes 2308
  68.8 73.7 %copy-start.5 = (f32[3,3,2,8,4]{3,4,2,1,0:T(4,128)S(1)}, f32[3,3,2,8,4]{3,4,2,1,0:T(4,128)}, u32[]{:S(2)}) copy-start(f32[3,3,2,8,4]{3,4,2,1,0:T(4,128)} %param.15) | copy-start | bytes 6916
  68.8 83.3 %copy-start.4 = (s32[3,16,2,8,4]{1,4,3,2,0:T(4,128)S(1)}, s32[3,16,2,8,4]{1,4,3,2,0:T(4,128)}, u32[]{:S(2)}) copy-start(s32[3,16,2,8,4]{1,4,3,2,0:T(4,128)} %param.16) | copy-start | bytes 36868
  70.9 84.5 %copy-start.6 = (f32[3,16,2,8,4]{1,4,3,2,0:T(4,128)S(1)}, f32[3,16,2,8,4]{1,4,3,2,0:T(4,128)}, u32[]{:S(2)}) copy-start(f32[3,16,2,8,4]{1,4,3,2,0:T(4,128)} %param.17) | copy-start | bytes 36868
  70.9 98.5 %copy-start.3 = (f32[3,2,8,4,256]{4,3,2,1,0:T(4,128)S(1)}, f32[3,2,8,4,256]{4,3,2,1,0:T(4,128)}, u32[]{:S(2)}) copy-start(f32[3,2,8,4,256]{4,3,2,1,0:T(4,128)} %param.12) | copy-start | bytes 589828
  70.9 98.6 %copy-start.8 = (f32[3,2,8,4]{2,3,1,0:T(4,128)S(1)}, f32[3,2,8,4]{2,3,1,0:T(4,128)}, u32[]{:S(2)}) copy-start(f32[3,2,8,4]{2,3,1,0:T(4,128)} %param.14) | copy-start | bytes 2308
  70.9 30.5 %all-to-all-start.17 = ((f32[512,2,1,128]{3,1,2,0:T(2,128)}), f32[512,2,1,128]{3,1,2,0:T(2,128)S(1)}, u32[]{:S(2)}, u32[]{:S(2)}) async-start(f32[512,2,1,128]{3,1,2,0:T(2,128)} %bitcast.87), calls=%async_computation.17 | async-start | bytes 1048576 | tf_op jit(solution)/shard_map/all_to_all | solution.py:641
  102.8 17.8 %all-to-all-start.18 = ((f32[32,17,1,128]{3,2,1,0:T(1,128)}), f32[32,17,1,128]{3,2,1,0:T(1,128)S(1)}, u32[]{:S(2)}, u32[]{:S(2)}) async-start(f32[32,17,1,128]{3,2,1,0:T(1,128)} %bitcast.89), calls=%async_computation.18 | async-start | bytes 557056 | tf_op jit(solution)/shard_map/all_to_all | solution.py:641
  107.8 6.6 %collective-permute-start.67 = (f32[256,128]{1,0:T(8,128)S(1)}, f32[256,128]{1,0:T(8,128)S(1)}, u32[]{:S(2)}, u32[]{:S(2)}) collective-permute-start(f32[256,128]{1,0:T(8,128)S(1)} %get-tuple-element.66), channel_id=1, source_target_pairs={{32,0},{64,32},{96,64},{128,96},{160,128},{192,160},{224,192},{256... | collective-permute-start | bytes 393224 | tf_op jit(solution)/shard_map/ppermute | solution.py:720
  109.1 5.3 %collective-permute-start.68 = (f32[256,128]{1,0:T(8,128)S(1)}, f32[256,128]{1,0:T(8,128)S(1)}, u32[]{:S(2)}, u32[]{:S(2)}) collective-permute-start(f32[256,128]{1,0:T(8,128)S(1)} %get-tuple-element.66), channel_id=1, source_target_pairs={{0,32},{32,64},{64,96},{96,128},{128,160},{160,192},{192,224},{224... | collective-permute-start | bytes 393224 | tf_op jit(solution)/shard_map/ppermute | solution.py:720
  112.1 8.4 %collective-permute-start.69 = (f32[256,128]{1,0:T(8,128)S(1)}, f32[256,128]{1,0:T(8,128)S(1)}, u32[]{:S(2)}, u32[]{:S(2)}) collective-permute-start(f32[256,128]{1,0:T(8,128)S(1)} %get-tuple-element.71), channel_id=1, source_target_pairs={{8,0},{16,8},{24,16},{9,1},{17,9},{25,17},{10,2},{18,10},{26,18},{... | collective-permute-start | bytes 393224 | tf_op jit(solution)/shard_map/ppermute | solution.py:720
  133.0 22.3 %all-to-all-start.20 = ((f32[32,17,1,128]{3,2,1,0:T(1,128)}), f32[32,17,1,128]{3,2,1,0:T(1,128)S(1)}, u32[]{:S(2)}, u32[]{:S(2)}) async-start(f32[32,17,1,128]{3,2,1,0:T(1,128)} %bitcast.93), calls=%async_computation.20 | async-start | bytes 557056 | tf_op jit(solution)/shard_map/all_to_all | solution.py:641
  142.6 12.7 %collective-permute-start.71 = (f32[256,128]{1,0:T(8,128)S(1)}, f32[256,128]{1,0:T(8,128)S(1)}, u32[]{:S(2)}, u32[]{:S(2)}) collective-permute-start(f32[256,128]{1,0:T(8,128)S(1)} %get-tuple-element.72), channel_id=1, source_target_pairs={{1,0},{2,1},{3,2},{4,3},{5,4},{6,5},{7,6},{9,8},{10,9},{11,10},{12... | collective-permute-start | bytes 393224 | tf_op jit(solution)/shard_map/ppermute | solution.py:720
  143.9 11.4 %collective-permute-start.72 = (f32[256,128]{1,0:T(8,128)S(1)}, f32[256,128]{1,0:T(8,128)S(1)}, u32[]{:S(2)}, u32[]{:S(2)}) collective-permute-start(f32[256,128]{1,0:T(8,128)S(1)} %get-tuple-element.72), channel_id=1, source_target_pairs={{0,1},{1,2},{2,3},{3,4},{4,5},{5,6},{6,7},{8,9},{9,10},{10,11},{11... | collective-permute-start | bytes 393224 | tf_op jit(solution)/shard_map/ppermute | solution.py:720
  148.5 6.9 %collective-permute-start.70 = (f32[256,128]{1,0:T(8,128)S(1)}, f32[256,128]{1,0:T(8,128)S(1)}, u32[]{:S(2)}, u32[]{:S(2)}) collective-permute-start(f32[256,128]{1,0:T(8,128)S(1)} %get-tuple-element.71), channel_id=1, source_target_pairs={{0,8},{8,16},{16,24},{1,9},{9,17},{17,25},{2,10},{10,18},{18,26},{... | collective-permute-start | bytes 393224 | tf_op jit(solution)/shard_map/ppermute | solution.py:720
  169.8 0.6 copy-start.9
  169.9 0.7 copy-start.10
  169.9 0.7 copy-start.11

commit v8 on v7

--- a/solution.py
+++ b/solution.py
@@ -39,13 +39,14 @@
     return jnp.sum(groups, axis=1)
 
 
-def pack_kernel(start_ref, stiffness_ref, node_ref, flags_ref, out_ref):
+def pack_kernel(start_ref, stiffness_ref, mass_ref, spring_ref, flags_ref, out_ref):
     lane = lax.broadcasted_iota(jnp.int32, (8, 128), 1)
     place = lax.broadcasted_iota(jnp.int32, (8, 128), 0)
     repeated = jnp.where((lane & 7) == place, 1.0, 0.0)
     keep = ((lane >> 3) & 7) == place
     stiffness = spread_nodes(dot(stiffness_ref[...], repeated), keep)
-    nodes = spread_nodes(dot(node_ref[...], repeated), keep)
+    masses = spread_nodes(dot(mass_ref[...], repeated), keep)
+    springs = spread_nodes(dot(spring_ref[...], repeated), keep)
     counts = jnp.dot(
         flags_ref[...].astype(jnp.bfloat16),
         jnp.ones((16, 128), jnp.bfloat16),
@@ -74,8 +75,8 @@
             stiffness[3 * d + source : 3 * d + source + 1, :] * softening[d : d + 1, :]
             for d in range(3)
         ]
-        mass = nodes[source : source + 1, :]
-        spring = nodes[3 + source : 4 + source, :]
+        mass = masses[source : source + 1, :]
+        spring = springs[source : source + 1, :]
         rows = [
             jnp.broadcast_to(row, (8, 128))
             for row in (
@@ -432,7 +433,7 @@
 def final_kernel(
     sums_ref, rows_ref, above_x_ref, below_x_ref, above_y_ref, below_y_ref, above_z_ref,
     below_z_ref, mass_ref, modulus_ref, stress_ref, subspace_ref, projected_ref, force_ref,
-    stress_new_ref, least_ref, m_ref
+    stress_new_ref, apart_ref, m_ref
 ):
     chunks = [sums_ref[chunk * CHUNK : chunk * CHUNK + 16, :] for chunk in range(32)]
     both = jnp.concatenate(
@@ -455,7 +456,7 @@
     half = lax.broadcasted_iota(jnp.int32, (256, 128), 1) < 64
     gram_diagonal = jnp.sum(jnp.where(row == column, gram, 0.0), axis=1, keepdims=True)
     least = invert_factors(m_ref, jnp.where(half, gram_diagonal, diagonal[:, :128]))
-    least_ref[...] = jnp.broadcast_to(least, (8, 128))
+    apart_ref[0, 0] = jnp.where(least[0, 0] > LEAST_PIVOT, 1, 0)
     lower = jnp.where(row >= column, m_ref[0], 0.0)
     stiff_lower = jnp.where(row >= column, m_ref[1], 0.0)
     vectors = by_vector(parts_of(rows_ref, 0))
@@ -614,7 +615,12 @@
     return subspace, projected, node_mass * displace, stress_new
 
 
-def call(kernel, shape, scratch=(), smem=(), operands=()):
+def call(kernel, shape, scratch=(), smem=(), operands=(), smem_out=()):
+    results = len(shape) if isinstance(shape, tuple) else 1
+    out_specs = tuple(
+        pl.BlockSpec(memory_space=pltpu.SMEM if place in smem_out else pltpu.VMEM)
+        for place in range(results)
+    )
     return pl.pallas_call(
         kernel,
         out_shape=shape,
@@ -622,7 +628,7 @@
             pl.BlockSpec(memory_space=pltpu.SMEM if place in smem else pltpu.VMEM)
             for place in range(len(operands))
         ],
-        out_specs=jax.tree.map(lambda _: pl.BlockSpec(memory_space=pltpu.VMEM), shape),
+        out_specs=out_specs if isinstance(shape, tuple) else out_specs[0],
         scratch_shapes=list(scratch),
         compiler_params=pltpu.CompilerParams(vmem_limit_bytes=40 * 1024 * 1024),
     )(*operands)
@@ -677,7 +683,8 @@
         operands=(
             start_block.reshape(48, 4, width),
             node_rows(stiffness),
-            jnp.concatenate([node_rows(node_mass), node_rows(ground_spring)], axis=0),
+            node_rows(node_mass),
+            node_rows(ground_spring),
             fibers_last(yield_flags).reshape(3 * NODES, fibers),
         ),
     )
@@ -725,20 +732,23 @@
     part = exchange(products, ("cy", "gy"), 32)
     part, *near = lax.optimization_barrier((part, *near))
     part = call(functools.partial(total_kernel, 32, 16), rows_of(16 * CHUNK), operands=(part,))
+    part, along[1] = lax.optimization_barrier((part, along[1]))
+    near += from_neighbours(along[1], "gy", (-1,))
     part = exchange(part, ("core", "gz"), 16)
+    part, *near = lax.optimization_barrier((part, *near))
     part = call(functools.partial(total_kernel, 16, 32), rows_of(32 * CHUNK), operands=(part,))
-    part, *along[1:] = lax.optimization_barrier((part, *along[1:]))
-    far = from_neighbours(along[1], "gy", (-1,)) + from_neighbours(along[2], "gz", (1, -1))
+    part, along[2] = lax.optimization_barrier((part, along[2]))
+    far = from_neighbours(along[2], "gz", (1, -1))
     part = exchange(part, ("cy", "gy"), 32)
     part, *far = lax.optimization_barrier((part, *far))
-    subspace, projected, force, stress_new, least = call(
+    subspace, projected, force, stress_new, apart = call(
         final_kernel,
         (
             jax.ShapeDtypeStruct((48, 4, width), jnp.float32),
             jax.ShapeDtypeStruct((width, width), jnp.float32),
             jax.ShapeDtypeStruct((24, 8), jnp.float32),
             jax.ShapeDtypeStruct((48, 4, fibers), jnp.float32),
-            rows_of(8),
+            jax.ShapeDtypeStruct((1, 1), jnp.int32),
         ),
         (pltpu.VMEM((2, 256, 256), jnp.float32),),
         operands=(
@@ -750,14 +760,14 @@
             fibers_last(fiber_modulus(stiffness, yield_flags)),
             fibers_last(stress_old),
         ),
+        smem_out=(4,),
     )
     place = node_mass.shape[1:]
     force = jnp.swapaxes(force.reshape(3, place[0], place[2], place[1]), -1, -2)
     stress_new = jnp.moveaxis(stress_new.reshape((3,) + place + (fibers,)), -1, 1)
-    return lax.cond(
-        least[0, 0] > LEAST_PIVOT,
-        lambda *operands: operands[:4],
-        lambda *operands: step_by_step(*operands[4:]),
+    return lax.switch(
+        apart[0, 0],
+        (lambda *operands: step_by_step(*operands[4:]), lambda *operands: operands[:4]),
         subspace.reshape(start_block.shape),
         projected,
         force,

time: 172 us -> 170 us (0.988)
  the two profiles are of different devices: /device:TPU:2 before, /device:TPU:1 now
where the time goes in v8:
time: 170 us; the launch traced here: 168 us
  starting transfers between devices  50.7 us (30%)
  blocking collectives  44.3 us (26%)
  waiting for transfers between devices  38.5 us (23%)
  Pallas kernels  28 us (16%)
  local copies, waits for them, and re-layouts  4.22 us (2%)
    all_to_all x1, blocking collectives, exchange(): return lax.all_to_all(blocks, axes, 0, 0, tiled=True).reshape(rows.shape)  44.3 us
    all_to_all x5, starting transfers between devices, exchange(): return lax.all_to_all(blocks, axes, 0, 0, tiled=True).reshape(rows.shape)  30.3 us
    pallas_call x8, Pallas kernels, call(): pl.pallas_call(kernel, out_shape=shape, in_specs=[pl.BlockSpec(memory_spa...  28 us
    all_to_all x5, waiting for transfers between devices, exchange(): return lax.all_to_all(blocks, axes, 0, 0, tiled=True).reshape(rows.shape)  26.8 us
    ppermute x6, starting transfers between devices, from_neighbours(): lax.ppermute(mine, axis, [(b, a) for a, b in pairs] if sense > 0 else pairs)  15.8 us
    ppermute x6, waiting for transfers between devices, from_neighbours(): lax.ppermute(mine, axis, [(b, a) for a, b in pairs] if sense > 0 else pairs)  10.1 us
    ppermute x1, starting transfers between devices, on_device(): other = lax.ppermute(own, 'core', [(0, 1), (1, 0)])  4.57 us
    unnamed x24, local copies, waits for them, and re-layouts  3.79 us
  transfers between devices with their start and end apart: 12, of which 9 were waited for; matrix products, arithmetic and copies ran while one was open for 0% of the time, Pallas kernels for 4%

profile of v8, /device:TPU:1, one launch (start us, length us, event | category | flops | bytes accessed | tf_op | source)
XLA Modules:
  0.0 167.7 jit_solution(4516148522329427334)
XLA Ops:
  0.6 1.3 shard_map.110
  2.0 44.3 %all_to_all.90 = f32[256,5,1,128]{3,2,1,0:T(1,128)S(1)} all-to-all(f32[256,5,1,128]{3,2,1,0:T(1,128)S(1)} %bitcast.275), channel_id=1, replica_groups=mesh['cy'=8,'core'=2,'gy'=4,'gz'=8] {'cy','gy','gz'}, dimensions={0} | all-to-all | bytes 1310720 | tf_op jit(solution)/shard_map/all_to_all | solution.py:647
  46.2 4.6 %collective-permute-start.66 = (f32[1280,128]{1,0:T(8,128)S(1)}, f32[1280,128]{1,0:T(8,128)S(1)}, u32[]{:S(2)}, u32[]{:S(2)}) collective-permute-start(f32[1280,128]{1,0:T(8,128)S(1)} %bitcast.273), channel_id=1, source_target_pairs={{0,32},{32,0},{1,33},{33,1},{2,34},{34,2},{3,35},{35,3},{4,36},{36... | collective-permute-start | bytes 1966088 | tf_op jit(solution)/shard_map/ppermute | solution.py:692
  50.8 1.7 %collective-permute-done.66.other_ref = f32[1280,128]{1,0:T(8,128)S(1)} collective-permute-done((f32[1280,128]{1,0:T(8,128)S(1)}, f32[1280,128]{1,0:T(8,128)S(1)}, u32[]{:S(2)}, u32[]{:S(2)}) %collective-permute-start.66) | collective-permute-done | bytes 655392 | tf_op jit(solution)/shard_map/ppermute | solution.py:692
  52.5 2.3 %shard_map.111 = (f32[16,9,4,8,128]{4,3,2,1,0:T(8,128)S(1)}, f32[32,128]{1,0:T(8,128)}) custom-call(s32[1]{0:T(128)} %bitcast.72.core_ref, f32[1280,128]{1,0:T(8,128)S(1)} %bitcast.274, f32[1280,128]{1,0:T(8,128)S(1)} %collective-permute-done.66.other_ref), custom_call_target="tpu_custom_call" | custom-call | tf_op jit(solution)/shard_map/pallas_call | solution.py:624
  54.9 0.0 copy-start
  54.9 1.4 copy-done
  56.2 0.0 copy-start.2
  56.2 3.9 %all-to-all-start.16 = ((f32[4,8,128]{2,1,0:T(8,128)}), f32[4,8,128]{2,1,0:T(8,128)S(1)}, u32[]{:S(2)}, u32[]{:S(2)}) async-start(f32[4,8,128]{2,1,0:T(8,128)} %bitcast.84), calls=%async_computation.16 | async-start | bytes 32768 | tf_op jit(solution)/shard_map/all_to_all | solution.py:647
  60.1 0.0 copy-start.1
  60.1 1.7 copy-done.1
  61.8 6.6 %shard_map.112.terms_ref = f32[11,16,4,8,128]{4,3,2,1,0:T(8,128)S(1)} custom-call(f32[16,9,4,8,128]{4,3,2,1,0:T(8,128)S(1)} %copy-done.1, f32[32,128]{1,0:T(8,128)} %get-tuple-element.69.top_ref.own_top_ref), custom_call_target="tpu_custom_call" | custom-call | tf_op jit(solution)/shard_map/pallas_call | solution.py:624
  68.4 0.0 copy-start.7
  68.4 0.0 all-to-all-done.16
  68.4 0.0 copy-done.2
  68.4 0.0 copy-start.5
  68.4 0.0 copy-start.4
  68.4 2.1 %shard_map.113 = f32[1024,128]{1,0:T(8,128)} custom-call(f32[11,16,4,8,128]{4,3,2,1,0:T(8,128)S(1)} %shard_map.112.terms_ref, f32[32,128]{1,0:T(8,128)} %get-tuple-element.69.top_ref.own_top_ref, f32[32,128]{1,0:T(8,128)S(1)} %bitcast.280, f32[40,128]{1,0:T(8,128)S(1)} %copy-done.2), custom_call_target="tpu_custom_call" | custom-call | tf_op jit(solution)/shard_map/pallas_call | solution.py:624
  70.5 0.0 copy-start.6
  70.5 0.0 copy-start.3
  70.5 0.0 copy-start.8
  70.5 9.3 %all-to-all-start.17 = ((f32[512,2,1,128]{3,1,2,0:T(2,128)}), f32[512,2,1,128]{3,1,2,0:T(2,128)S(1)}, u32[]{:S(2)}, u32[]{:S(2)}) async-start(f32[512,2,1,128]{3,1,2,0:T(2,128)} %bitcast.87), calls=%async_computation.17 | async-start | bytes 1048576 | tf_op jit(solution)/shard_map/all_to_all | solution.py:647
  79.8 0.0 copy-done.7
  79.8 0.1 reshape_reshape.7
  79.9 21.5 %all-to-all-done.17 = f32[512,2,1,128]{3,1,2,0:T(2,128)S(1)} async-done(((f32[512,2,1,128]{3,1,2,0:T(2,128)}), f32[512,2,1,128]{3,1,2,0:T(2,128)S(1)}, u32[]{:S(2)}, u32[]{:S(2)}) %all-to-all-start.17) | async-done | bytes 524320 | tf_op jit(solution)/shard_map/all_to_all | solution.py:647
  101.4 1.4 shard_map.114
  102.9 4.3 %all-to-all-start.18 = ((f32[32,17,1,128]{3,2,1,0:T(1,128)}), f32[32,17,1,128]{3,2,1,0:T(1,128)S(1)}, u32[]{:S(2)}, u32[]{:S(2)}) async-start(f32[32,17,1,128]{3,2,1,0:T(1,128)} %bitcast.89), calls=%async_computation.18 | async-start | bytes 557056 | tf_op jit(solution)/shard_map/all_to_all | solution.py:647
  107.2 3.2 %collective-permute-start.67 = (f32[256,128]{1,0:T(8,128)S(1)}, f32[256,128]{1,0:T(8,128)S(1)}, u32[]{:S(2)}, u32[]{:S(2)}) collective-permute-start(f32[256,128]{1,0:T(8,128)S(1)} %get-tuple-element.71), channel_id=1, source_target_pairs={{32,0},{64,32},{96,64},{128,96},{160,128},{192,160},{224,192},{256... | collective-permute-start | bytes 393224 | tf_op jit(solution)/shard_map/ppermute | solution.py:727
  110.4 3.2 %collective-permute-start.68 = (f32[256,128]{1,0:T(8,128)S(1)}, f32[256,128]{1,0:T(8,128)S(1)}, u32[]{:S(2)}, u32[]{:S(2)}) collective-permute-start(f32[256,128]{1,0:T(8,128)S(1)} %get-tuple-element.71), channel_id=1, source_target_pairs={{0,32},{32,64},{64,96},{96,128},{128,160},{160,192},{192,224},{224... | collective-permute-start | bytes 393224 | tf_op jit(solution)/shard_map/ppermute | solution.py:727
  113.6 1.3 collective-permute-start.69
  114.9 2.2 %collective-permute-done.67.above_x_ref = f32[256,128]{1,0:T(8,128)S(1)} collective-permute-done((f32[256,128]{1,0:T(8,128)S(1)}, f32[256,128]{1,0:T(8,128)S(1)}, u32[]{:S(2)}, u32[]{:S(2)}) %collective-permute-start.67) | collective-permute-done | bytes 131104 | tf_op jit(solution)/shard_map/ppermute | solution.py:727
  117.1 0.0 collective-permute-done.68.below_x_ref
  117.1 3.6 %collective-permute-done.69.above_y_ref = f32[256,128]{1,0:T(8,128)S(1)} collective-permute-done((f32[256,128]{1,0:T(8,128)S(1)}, f32[256,128]{1,0:T(8,128)S(1)}, u32[]{:S(2)}, u32[]{:S(2)}) %collective-permute-start.69) | collective-permute-done | bytes 131104 | tf_op jit(solution)/shard_map/ppermute | solution.py:727
  120.7 0.0 all-to-all-done.18
  120.7 0.7 shard_map.115
  121.4 4.7 %all-to-all-start.19 = ((f32[16,17,1,128]{3,2,1,0:T(1,128)}), f32[16,17,1,128]{3,2,1,0:T(1,128)S(1)}, u32[]{:S(2)}, u32[]{:S(2)}) async-start(f32[16,17,1,128]{3,2,1,0:T(1,128)} %bitcast.91), calls=%async_computation.19 | async-start | bytes 278528 | tf_op jit(solution)/shard_map/all_to_all | solution.py:647
  126.0 2.5 %collective-permute-start.70 = (f32[256,128]{1,0:T(8,128)S(1)}, f32[256,128]{1,0:T(8,128)S(1)}, u32[]{:S(2)}, u32[]{:S(2)}) collective-permute-start(f32[256,128]{1,0:T(8,128)S(1)} %get-tuple-element.78), channel_id=1, source_target_pairs={{0,8},{8,16},{16,24},{1,9},{9,17},{17,25},{2,10},{10,18},{18,26},{... | collective-permute-start | bytes 393224 | tf_op jit(solution)/shard_map/ppermute | solution.py:727
  128.5 2.7 %collective-permute-done.70.below_y_ref = f32[256,128]{1,0:T(8,128)S(1)} collective-permute-done((f32[256,128]{1,0:T(8,128)S(1)}, f32[256,128]{1,0:T(8,128)S(1)}, u32[]{:S(2)}, u32[]{:S(2)}) %collective-permute-start.70) | collective-permute-done | bytes 131104 | tf_op jit(solution)/shard_map/ppermute | solution.py:727
  131.2 2.2 %all-to-all-done.19 = f32[16,17,1,128]{3,2,1,0:T(1,128)S(1)} async-done(((f32[16,17,1,128]{3,2,1,0:T(1,128)}), f32[16,17,1,128]{3,2,1,0:T(1,128)S(1)}, u32[]{:S(2)}, u32[]{:S(2)}) %all-to-all-start.19) | async-done | bytes 139296 | tf_op jit(solution)/shard_map/all_to_all | solution.py:647
  133.4 0.7 shard_map.116
  134.2 8.2 %all-to-all-start.20 = ((f32[32,17,1,128]{3,2,1,0:T(1,128)}), f32[32,17,1,128]{3,2,1,0:T(1,128)S(1)}, u32[]{:S(2)}, u32[]{:S(2)}) async-start(f32[32,17,1,128]{3,2,1,0:T(1,128)} %bitcast.93), calls=%async_computation.20 | async-start | bytes 557056 | tf_op jit(solution)/shard_map/all_to_all | solution.py:647
  142.4 0.0 copy-done.5
  142.4 0.1 copy.303
  142.5 1.3 collective-permute-start.71
  143.8 4.3 %collective-permute-start.72 = (f32[256,128]{1,0:T(8,128)S(1)}, f32[256,128]{1,0:T(8,128)S(1)}, u32[]{:S(2)}, u32[]{:S(2)}) collective-permute-start(f32[256,128]{1,0:T(8,128)S(1)} %get-tuple-element.82), channel_id=1, source_target_pairs={{0,1},{1,2},{2,3},{3,4},{4,5},{5,6},{6,7},{8,9},{9,10},{10,11},{11... | collective-permute-start | bytes 393224 | tf_op jit(solution)/shard_map/ppermute | solution.py:727
  148.2 0.0 copy-done.4
  148.2 0.1 select_multiply_fusion
  148.3 0.4 collective-permute-done.71.above_z_ref
  148.6 1.2 collective-permute-done.72.below_z_ref
  149.9 3.1 %all-to-all-done.20 = f32[32,17,1,128]{3,2,1,0:T(1,128)S(1)} async-done(((f32[32,17,1,128]{3,2,1,0:T(1,128)}), f32[32,17,1,128]{3,2,1,0:T(1,128)S(1)}, u32[]{:S(2)}, u32[]{:S(2)}) %all-to-all-start.20) | async-done | bytes 278560 | tf_op jit(solution)/shard_map/all_to_all | solution.py:647
  153.0 0.0 copy-done.6
  153.0 12.8 %shard_map.117 = (f32[48,4,256]{2,1,0:T(4,128)S(1)}, f32[256,256]{1,0:T(8,128)}, f32[24,8]{1,0:T(8,128)S(1)}, f32[48,4,16]{2,1,0:T(4,128)S(1)}, s32[1,1]{1,0:T(1,128)}) custom-call(f32[544,128]{1,0:T(8,128)S(1)} %bitcast.276, f32[1024,128]{1,0:T(8,128)S(1)} %bitcast.272, f32[256,128]{1,0:T(8,128)S(1)} %collective-permute-done.67.above_x_ref, ...), custom_call_target="tpu_custom_call" | custom-call | tf_op jit(solution)/shard_map/pallas_call | solution.py:624
  165.8 0.1 copy.304
  166.6 0.0 copy-done.3
  166.6 0.0 copy-done.8
  166.6 0.4 conditional.1
  166.9 0.1 copy.316
  167.0 0.0 copy-start.9
  167.0 0.0 copy-start.10
  167.0 0.0 copy-start.11
  167.0 0.6 copy-done.9
  167.6 0.1 copy-done.10
  167.7 0.0 copy-done.11
  (3 shorter events, 0.0 us)
Async XLA Ops:
  46.2 6.3 %collective-permute-start.66 = (f32[1280,128]{1,0:T(8,128)S(1)}, f32[1280,128]{1,0:T(8,128)S(1)}, u32[]{:S(2)}, u32[]{:S(2)}) collective-permute-start(f32[1280,128]{1,0:T(8,128)S(1)} %bitcast.273), channel_id=1, source_target_pairs={{0,32},{32,0},{1,33},{33,1},{2,34},{34,2},{3,35},{35,3},{4,36},{36... | collective-permute-start | bytes 1966088 | tf_op jit(solution)/shard_map/ppermute | solution.py:692
  54.9 1.4 copy-start
  56.2 12.1 %copy-start.2 = (f32[40,128]{1,0:T(8,128)S(1)}, f32[40,128]{1,0:T(8,128)}, u32[]{:S(2)}) copy-start(f32[40,128]{1,0:T(8,128)} %constant.129.clone.nodes_ref) | copy-start | bytes 61444
  56.2 12.1 %all-to-all-start.16 = ((f32[4,8,128]{2,1,0:T(8,128)}), f32[4,8,128]{2,1,0:T(8,128)S(1)}, u32[]{:S(2)}, u32[]{:S(2)}) async-start(f32[4,8,128]{2,1,0:T(8,128)} %bitcast.84), calls=%async_computation.16 | async-start | bytes 32768 | tf_op jit(solution)/shard_map/all_to_all | solution.py:647
  60.1 1.7 copy-start.1
  68.4 11.4 %copy-start.7 = (f32[3,2,8,4]{2,3,1,0:T(4,128)S(1)}, f32[3,2,8,4]{2,3,1,0:T(4,128)}, u32[]{:S(2)}) copy-start(f32[3,2,8,4]{2,3,1,0:T(4,128)} %param.13) | copy-start | bytes 2308
  68.4 74.0 %copy-start.5 = (f32[3,3,2,8,4]{3,4,2,1,0:T(4,128)S(1)}, f32[3,3,2,8,4]{3,4,2,1,0:T(4,128)}, u32[]{:S(2)}) copy-start(f32[3,3,2,8,4]{3,4,2,1,0:T(4,128)} %param.15) | copy-start | bytes 6916
  68.4 79.8 %copy-start.4 = (s32[3,16,2,8,4]{1,4,3,2,0:T(4,128)S(1)}, s32[3,16,2,8,4]{1,4,3,2,0:T(4,128)}, u32[]{:S(2)}) copy-start(s32[3,16,2,8,4]{1,4,3,2,0:T(4,128)} %param.16) | copy-start | bytes 36868
  70.5 82.4 %copy-start.6 = (f32[3,16,2,8,4]{1,4,3,2,0:T(4,128)S(1)}, f32[3,16,2,8,4]{1,4,3,2,0:T(4,128)}, u32[]{:S(2)}) copy-start(f32[3,16,2,8,4]{1,4,3,2,0:T(4,128)} %param.17) | copy-start | bytes 36868
  70.5 96.0 %copy-start.3 = (f32[3,2,8,4,256]{4,3,2,1,0:T(4,128)S(1)}, f32[3,2,8,4,256]{4,3,2,1,0:T(4,128)}, u32[]{:S(2)}) copy-start(f32[3,2,8,4,256]{4,3,2,1,0:T(4,128)} %param.12) | copy-start | bytes 589828
  70.5 96.0 %copy-start.8 = (f32[3,2,8,4]{2,3,1,0:T(4,128)S(1)}, f32[3,2,8,4]{2,3,1,0:T(4,128)}, u32[]{:S(2)}) copy-start(f32[3,2,8,4]{2,3,1,0:T(4,128)} %param.14) | copy-start | bytes 2308
  70.5 30.9 %all-to-all-start.17 = ((f32[512,2,1,128]{3,1,2,0:T(2,128)}), f32[512,2,1,128]{3,1,2,0:T(2,128)S(1)}, u32[]{:S(2)}, u32[]{:S(2)}) async-start(f32[512,2,1,128]{3,1,2,0:T(2,128)} %bitcast.87), calls=%async_computation.17 | async-start | bytes 1048576 | tf_op jit(solution)/shard_map/all_to_all | solution.py:647
  102.9 17.8 %all-to-all-start.18 = ((f32[32,17,1,128]{3,2,1,0:T(1,128)}), f32[32,17,1,128]{3,2,1,0:T(1,128)S(1)}, u32[]{:S(2)}, u32[]{:S(2)}) async-start(f32[32,17,1,128]{3,2,1,0:T(1,128)} %bitcast.89), calls=%async_computation.18 | async-start | bytes 557056 | tf_op jit(solution)/shard_map/all_to_all | solution.py:647
  107.2 9.9 %collective-permute-start.67 = (f32[256,128]{1,0:T(8,128)S(1)}, f32[256,128]{1,0:T(8,128)S(1)}, u32[]{:S(2)}, u32[]{:S(2)}) collective-permute-start(f32[256,128]{1,0:T(8,128)S(1)} %get-tuple-element.71), channel_id=1, source_target_pairs={{32,0},{64,32},{96,64},{128,96},{160,128},{192,160},{224,192},{256... | collective-permute-start | bytes 393224 | tf_op jit(solution)/shard_map/ppermute | solution.py:727
  110.4 6.7 %collective-permute-start.68 = (f32[256,128]{1,0:T(8,128)S(1)}, f32[256,128]{1,0:T(8,128)S(1)}, u32[]{:S(2)}, u32[]{:S(2)}) collective-permute-start(f32[256,128]{1,0:T(8,128)S(1)} %get-tuple-element.71), channel_id=1, source_target_pairs={{0,32},{32,64},{64,96},{96,128},{128,160},{160,192},{192,224},{224... | collective-permute-start | bytes 393224 | tf_op jit(solution)/shard_map/ppermute | solution.py:727
  113.6 7.1 %collective-permute-start.69 = (f32[256,128]{1,0:T(8,128)S(1)}, f32[256,128]{1,0:T(8,128)S(1)}, u32[]{:S(2)}, u32[]{:S(2)}) collective-permute-start(f32[256,128]{1,0:T(8,128)S(1)} %get-tuple-element.78), channel_id=1, source_target_pairs={{8,0},{16,8},{24,16},{9,1},{17,9},{25,17},{10,2},{18,10},{26,18},{... | collective-permute-start | bytes 393224 | tf_op jit(solution)/shard_map/ppermute | solution.py:727
  121.4 12.0 %all-to-all-start.19 = ((f32[16,17,1,128]{3,2,1,0:T(1,128)}), f32[16,17,1,128]{3,2,1,0:T(1,128)S(1)}, u32[]{:S(2)}, u32[]{:S(2)}) async-start(f32[16,17,1,128]{3,2,1,0:T(1,128)} %bitcast.91), calls=%async_computation.19 | async-start | bytes 278528 | tf_op jit(solution)/shard_map/all_to_all | solution.py:647
  126.0 5.2 %collective-permute-start.70 = (f32[256,128]{1,0:T(8,128)S(1)}, f32[256,128]{1,0:T(8,128)S(1)}, u32[]{:S(2)}, u32[]{:S(2)}) collective-permute-start(f32[256,128]{1,0:T(8,128)S(1)} %get-tuple-element.78), channel_id=1, source_target_pairs={{0,8},{8,16},{16,24},{1,9},{9,17},{17,25},{2,10},{10,18},{18,26},{... | collective-permute-start | bytes 393224 | tf_op jit(solution)/shard_map/ppermute | solution.py:727
  134.2 18.8 %all-to-all-start.20 = ((f32[32,17,1,128]{3,2,1,0:T(1,128)}), f32[32,17,1,128]{3,2,1,0:T(1,128)S(1)}, u32[]{:S(2)}, u32[]{:S(2)}) async-start(f32[32,17,1,128]{3,2,1,0:T(1,128)} %bitcast.93), calls=%async_computation.20 | async-start | bytes 557056 | tf_op jit(solution)/shard_map/all_to_all | solution.py:647
  142.5 6.1 %collective-permute-start.71 = (f32[256,128]{1,0:T(8,128)S(1)}, f32[256,128]{1,0:T(8,128)S(1)}, u32[]{:S(2)}, u32[]{:S(2)}) collective-permute-start(f32[256,128]{1,0:T(8,128)S(1)} %get-tuple-element.82), channel_id=1, source_target_pairs={{1,0},{2,1},{3,2},{4,3},{5,4},{6,5},{7,6},{9,8},{10,9},{11,10},{12... | collective-permute-start | bytes 393224 | tf_op jit(solution)/shard_map/ppermute | solution.py:727
  143.8 6.1 %collective-permute-start.72 = (f32[256,128]{1,0:T(8,128)S(1)}, f32[256,128]{1,0:T(8,128)S(1)}, u32[]{:S(2)}, u32[]{:S(2)}) collective-permute-start(f32[256,128]{1,0:T(8,128)S(1)} %get-tuple-element.82), channel_id=1, source_target_pairs={{0,1},{1,2},{2,3},{3,4},{4,5},{5,6},{6,7},{8,9},{9,10},{10,11},{11... | collective-permute-start | bytes 393224 | tf_op jit(solution)/shard_map/ppermute | solution.py:727
  167.0 0.6 copy-start.9
  167.0 0.7 copy-start.10
  167.0 0.7 copy-start.11

commit v9 on v8

--- a/solution.py
+++ b/solution.py
@@ -728,17 +728,18 @@
             for sense in senses
         ]
 
-    near = from_neighbours(along[0], GX, (1, -1)) + from_neighbours(along[1], "gy", (1,))
+    along_x, along_y, along_z = along
+    near = from_neighbours(along_z, "gz", (1, -1)) + from_neighbours(along_y, "gy", (1,))
     part = exchange(products, ("cy", "gy"), 32)
     part, *near = lax.optimization_barrier((part, *near))
     part = call(functools.partial(total_kernel, 32, 16), rows_of(16 * CHUNK), operands=(part,))
-    part, along[1] = lax.optimization_barrier((part, along[1]))
-    near += from_neighbours(along[1], "gy", (-1,))
+    part, along_y = lax.optimization_barrier((part, along_y))
+    near += from_neighbours(along_y, "gy", (-1,))
     part = exchange(part, ("core", "gz"), 16)
     part, *near = lax.optimization_barrier((part, *near))
     part = call(functools.partial(total_kernel, 16, 32), rows_of(32 * CHUNK), operands=(part,))
-    part, along[2] = lax.optimization_barrier((part, along[2]))
-    far = from_neighbours(along[2], "gz", (1, -1))
+    part, along_x = lax.optimization_barrier((part, along_x))
+    far = from_neighbours(along_x, GX, (1, -1))
     part = exchange(part, ("cy", "gy"), 32)
     part, *far = lax.optimization_barrier((part, *far))
     subspace, projected, force, stress_new, apart = call(
@@ -754,8 +755,9 @@
         operands=(
             part,
             returned,
-            *near,
             *far,
+            *near[2:],
+            *near[:2],
             mass_row,
             fibers_last(fiber_modulus(stiffness, yield_flags)),
             fibers_last(stress_old),

time: 170 us -> 172 us (1.012)
  starting transfers between devices: 50.7 us -> 55.5 us
  waiting for transfers between devices: 38.5 us -> 35.3 us
    all_to_all x5, starting transfers between devices: 30.3 us -> 34.1 us  [exchange(): return lax.all_to_all(blocks, axes, 0, 0, tiled=True).reshape(rows.shape)]
    all_to_all x5, waiting for transfers between devices: 26.8 us -> 23.4 us  [exchange(): return lax.all_to_all(blocks, axes, 0, 0, tiled=True).reshape(rows.shape)]
  transfers between devices with their start and end apart: 12 -> 12, of which waited for: 9 -> 8; matrix products, arithmetic and copies ran while one was open for 0% -> 0% of each run, Pallas kernels for 4% -> 4%
where the time goes in v9:
time: 172 us; the launch traced here: 169 us
  starting transfers between devices  55.5 us (32%)
  blocking collectives  44.3 us (26%)
  waiting for transfers between devices  35.3 us (21%)
  Pallas kernels  28 us (16%)
  local copies, waits for them, and re-layouts  4.22 us (2%)
    all_to_all x1, blocking collectives, exchange(): return lax.all_to_all(blocks, axes, 0, 0, tiled=True).reshape(rows.shape)  44.3 us
    all_to_all x5, starting transfers between devices, exchange(): return lax.all_to_all(blocks, axes, 0, 0, tiled=True).reshape(rows.shape)  34.1 us
    pallas_call x8, Pallas kernels, call(): pl.pallas_call(kernel, out_shape=shape, in_specs=[pl.BlockSpec(memory_spa...  28 us
    all_to_all x5, waiting for transfers between devices, exchange(): return lax.all_to_all(blocks, axes, 0, 0, tiled=True).reshape(rows.shape)  23.4 us
    ppermute x6, starting transfers between devices, from_neighbours(): lax.ppermute(mine, axis, [(b, a) for a, b in pairs] if sense > 0 else pairs)  16.8 us
    ppermute x6, waiting for transfers between devices, from_neighbours(): lax.ppermute(mine, axis, [(b, a) for a, b in pairs] if sense > 0 else pairs)  10.3 us
    ppermute x1, starting transfers between devices, on_device(): other = lax.ppermute(own, 'core', [(0, 1), (1, 0)])  4.57 us
    unnamed x24, local copies, waits for them, and re-layouts  3.79 us
  transfers between devices with their start and end apart: 12, of which 8 were waited for; matrix products, arithmetic and copies ran while one was open for 0% of the time, Pallas kernels for 4%

profile of v9, /device:TPU:1, one launch (start us, length us, event | category | flops | bytes accessed | tf_op | source)
XLA Modules:
  0.0 169.3 jit_solution(15661030681600308431)
XLA Ops:
  0.6 1.3 shard_map.110
  2.0 44.3 %all_to_all.90 = f32[256,5,1,128]{3,2,1,0:T(1,128)S(1)} all-to-all(f32[256,5,1,128]{3,2,1,0:T(1,128)S(1)} %bitcast.275), channel_id=1, replica_groups=mesh['cy'=8,'core'=2,'gy'=4,'gz'=8] {'cy','gy','gz'}, dimensions={0} | all-to-all | bytes 1310720 | tf_op jit(solution)/shard_map/all_to_all | solution.py:647
  46.2 4.6 %collective-permute-start.66 = (f32[1280,128]{1,0:T(8,128)S(1)}, f32[1280,128]{1,0:T(8,128)S(1)}, u32[]{:S(2)}, u32[]{:S(2)}) collective-permute-start(f32[1280,128]{1,0:T(8,128)S(1)} %bitcast.273), channel_id=1, source_target_pairs={{0,32},{32,0},{1,33},{33,1},{2,34},{34,2},{3,35},{35,3},{4,36},{36... | collective-permute-start | bytes 1966088 | tf_op jit(solution)/shard_map/ppermute | solution.py:692
  50.8 1.7 %collective-permute-done.66.other_ref = f32[1280,128]{1,0:T(8,128)S(1)} collective-permute-done((f32[1280,128]{1,0:T(8,128)S(1)}, f32[1280,128]{1,0:T(8,128)S(1)}, u32[]{:S(2)}, u32[]{:S(2)}) %collective-permute-start.66) | collective-permute-done | bytes 655392 | tf_op jit(solution)/shard_map/ppermute | solution.py:692
  52.5 2.3 %shard_map.111 = (f32[16,9,4,8,128]{4,3,2,1,0:T(8,128)S(1)}, f32[32,128]{1,0:T(8,128)}) custom-call(s32[1]{0:T(128)} %bitcast.72.core_ref, f32[1280,128]{1,0:T(8,128)S(1)} %bitcast.274, f32[1280,128]{1,0:T(8,128)S(1)} %collective-permute-done.66.other_ref), custom_call_target="tpu_custom_call" | custom-call | tf_op jit(solution)/shard_map/pallas_call | solution.py:624
  54.9 0.0 copy-start
  54.9 1.4 copy-done
  56.2 0.0 copy-start.2
  56.2 3.9 %all-to-all-start.16 = ((f32[4,8,128]{2,1,0:T(8,128)}), f32[4,8,128]{2,1,0:T(8,128)S(1)}, u32[]{:S(2)}, u32[]{:S(2)}) async-start(f32[4,8,128]{2,1,0:T(8,128)} %bitcast.84), calls=%async_computation.16 | async-start | bytes 32768 | tf_op jit(solution)/shard_map/all_to_all | solution.py:647
  60.1 0.0 copy-start.1
  60.1 1.7 copy-done.1
  61.8 6.6 %shard_map.112.terms_ref = f32[11,16,4,8,128]{4,3,2,1,0:T(8,128)S(1)} custom-call(f32[16,9,4,8,128]{4,3,2,1,0:T(8,128)S(1)} %copy-done.1, f32[32,128]{1,0:T(8,128)} %get-tuple-element.69.top_ref.own_top_ref), custom_call_target="tpu_custom_call" | custom-call | tf_op jit(solution)/shard_map/pallas_call | solution.py:624
  68.4 0.0 copy-start.7
  68.4 0.0 all-to-all-done.16
  68.4 0.0 copy-done.2
  68.4 0.0 copy-start.5
  68.4 0.0 copy-start.4
  68.4 2.1 %shard_map.113 = f32[1024,128]{1,0:T(8,128)} custom-call(f32[11,16,4,8,128]{4,3,2,1,0:T(8,128)S(1)} %shard_map.112.terms_ref, f32[32,128]{1,0:T(8,128)} %get-tuple-element.69.top_ref.own_top_ref, f32[32,128]{1,0:T(8,128)S(1)} %bitcast.280, f32[40,128]{1,0:T(8,128)S(1)} %copy-done.2), custom_call_target="tpu_custom_call" | custom-call | tf_op jit(solution)/shard_map/pallas_call | solution.py:624
  70.5 0.0 copy-start.6
  70.5 0.0 copy-start.3
  70.5 0.0 copy-start.8
  70.5 9.3 %all-to-all-start.17 = ((f32[512,2,1,128]{3,1,2,0:T(2,128)}), f32[512,2,1,128]{3,1,2,0:T(2,128)S(1)}, u32[]{:S(2)}, u32[]{:S(2)}) async-start(f32[512,2,1,128]{3,1,2,0:T(2,128)} %bitcast.87), calls=%async_computation.17 | async-start | bytes 1048576 | tf_op jit(solution)/shard_map/all_to_all | solution.py:647
  79.8 0.0 copy-done.7
  79.8 0.1 reshape_reshape.7
  79.9 21.5 %all-to-all-done.17 = f32[512,2,1,128]{3,1,2,0:T(2,128)S(1)} async-done(((f32[512,2,1,128]{3,1,2,0:T(2,128)}), f32[512,2,1,128]{3,1,2,0:T(2,128)S(1)}, u32[]{:S(2)}, u32[]{:S(2)}) %all-to-all-start.17) | async-done | bytes 524320 | tf_op jit(solution)/shard_map/all_to_all | solution.py:647
  101.4 1.4 shard_map.114
  102.9 4.3 %all-to-all-start.18 = ((f32[32,17,1,128]{3,2,1,0:T(1,128)}), f32[32,17,1,128]{3,2,1,0:T(1,128)S(1)}, u32[]{:S(2)}, u32[]{:S(2)}) async-start(f32[32,17,1,128]{3,2,1,0:T(1,128)} %bitcast.89), calls=%async_computation.18 | async-start | bytes 557056 | tf_op jit(solution)/shard_map/all_to_all | solution.py:647
  107.2 1.3 collective-permute-start.67
  108.5 4.0 %collective-permute-start.68 = (f32[256,128]{1,0:T(8,128)S(1)}, f32[256,128]{1,0:T(8,128)S(1)}, u32[]{:S(2)}, u32[]{:S(2)}) collective-permute-start(f32[256,128]{1,0:T(8,128)S(1)} %get-tuple-element.71), channel_id=1, source_target_pairs={{0,1},{1,2},{2,3},{3,4},{4,5},{5,6},{6,7},{8,9},{9,10},{10,11},{11... | collective-permute-start | bytes 393224 | tf_op jit(solution)/shard_map/ppermute | solution.py:727
  112.5 1.3 collective-permute-start.69
  113.8 0.0 collective-permute-done.67.above_z_ref
  113.8 0.6 collective-permute-done.68.below_z_ref
  114.4 4.1 %collective-permute-done.69.above_y_ref = f32[256,128]{1,0:T(8,128)S(1)} collective-permute-done((f32[256,128]{1,0:T(8,128)S(1)}, f32[256,128]{1,0:T(8,128)S(1)}, u32[]{:S(2)}, u32[]{:S(2)}) %collective-permute-start.69) | collective-permute-done | bytes 131104 | tf_op jit(solution)/shard_map/ppermute | solution.py:727
  118.5 0.0 all-to-all-done.18
  118.5 0.7 shard_map.115
  119.2 7.2 %all-to-all-start.19 = ((f32[16,17,1,128]{3,2,1,0:T(1,128)}), f32[16,17,1,128]{3,2,1,0:T(1,128)S(1)}, u32[]{:S(2)}, u32[]{:S(2)}) async-start(f32[16,17,1,128]{3,2,1,0:T(1,128)} %bitcast.91), calls=%async_computation.19 | async-start | bytes 278528 | tf_op jit(solution)/shard_map/all_to_all | solution.py:647
  126.4 3.3 %collective-permute-start.70 = (f32[256,128]{1,0:T(8,128)S(1)}, f32[256,128]{1,0:T(8,128)S(1)}, u32[]{:S(2)}, u32[]{:S(2)}) collective-permute-start(f32[256,128]{1,0:T(8,128)S(1)} %get-tuple-element.78), channel_id=1, source_target_pairs={{0,8},{8,16},{16,24},{1,9},{9,17},{17,25},{2,10},{10,18},{18,26},{... | collective-permute-start | bytes 393224 | tf_op jit(solution)/shard_map/ppermute | solution.py:727
  129.7 2.8 %collective-permute-done.70.below_y_ref = f32[256,128]{1,0:T(8,128)S(1)} collective-permute-done((f32[256,128]{1,0:T(8,128)S(1)}, f32[256,128]{1,0:T(8,128)S(1)}, u32[]{:S(2)}, u32[]{:S(2)}) %collective-permute-start.70) | collective-permute-done | bytes 131104 | tf_op jit(solution)/shard_map/ppermute | solution.py:727
  132.5 1.2 all-to-all-done.19
  133.8 0.7 shard_map.116
  134.5 9.5 %all-to-all-start.20 = ((f32[32,17,1,128]{3,2,1,0:T(1,128)}), f32[32,17,1,128]{3,2,1,0:T(1,128)S(1)}, u32[]{:S(2)}, u32[]{:S(2)}) async-start(f32[32,17,1,128]{3,2,1,0:T(1,128)} %bitcast.93), calls=%async_computation.20 | async-start | bytes 557056 | tf_op jit(solution)/shard_map/all_to_all | solution.py:647
  144.0 0.0 copy-done.5
  144.0 0.1 copy.303
  144.1 3.4 %collective-permute-start.71 = (f32[256,128]{1,0:T(8,128)S(1)}, f32[256,128]{1,0:T(8,128)S(1)}, u32[]{:S(2)}, u32[]{:S(2)}) collective-permute-start(f32[256,128]{1,0:T(8,128)S(1)} %get-tuple-element.82), channel_id=1, source_target_pairs={{32,0},{64,32},{96,64},{128,96},{160,128},{192,160},{224,192},{256... | collective-permute-start | bytes 393224 | tf_op jit(solution)/shard_map/ppermute | solution.py:727
  147.5 3.5 %collective-permute-start.72 = (f32[256,128]{1,0:T(8,128)S(1)}, f32[256,128]{1,0:T(8,128)S(1)}, u32[]{:S(2)}, u32[]{:S(2)}) collective-permute-start(f32[256,128]{1,0:T(8,128)S(1)} %get-tuple-element.82), channel_id=1, source_target_pairs={{0,32},{32,64},{64,96},{96,128},{128,160},{160,192},{192,224},{224... | collective-permute-start | bytes 393224 | tf_op jit(solution)/shard_map/ppermute | solution.py:727
  151.1 0.0 copy-done.4
  151.1 0.1 select_multiply_fusion
  151.2 2.7 %collective-permute-done.71.above_x_ref = f32[256,128]{1,0:T(8,128)S(1)} collective-permute-done((f32[256,128]{1,0:T(8,128)S(1)}, f32[256,128]{1,0:T(8,128)S(1)}, u32[]{:S(2)}, u32[]{:S(2)}) %collective-permute-start.71) | collective-permute-done | bytes 131104 | tf_op jit(solution)/shard_map/ppermute | solution.py:727
  153.9 0.0 collective-permute-done.72.below_x_ref
  153.9 0.7 all-to-all-done.20
  154.6 0.0 copy-done.6
  154.6 12.8 %shard_map.117 = (f32[48,4,256]{2,1,0:T(4,128)S(1)}, f32[256,256]{1,0:T(8,128)}, f32[24,8]{1,0:T(8,128)S(1)}, f32[48,4,16]{2,1,0:T(4,128)S(1)}, s32[1,1]{1,0:T(1,128)}) custom-call(f32[544,128]{1,0:T(8,128)S(1)} %bitcast.276, f32[1024,128]{1,0:T(8,128)S(1)} %bitcast.272, f32[256,128]{1,0:T(8,128)S(1)} %collective-permute-done.71.above_x_ref, ...), custom_call_target="tpu_custom_call" | custom-call | tf_op jit(solution)/shard_map/pallas_call | solution.py:624
  167.4 0.1 copy.304
  168.2 0.0 copy-done.3
  168.2 0.0 copy-done.8
  168.2 0.4 conditional.1
  168.5 0.1 copy.316
  168.6 0.0 copy-start.9
  168.6 0.0 copy-start.10
  168.6 0.0 copy-start.11
  168.6 0.6 copy-done.9
  169.2 0.1 copy-done.10
  169.3 0.0 copy-done.11
  (3 shorter events, 0.0 us)
Async XLA Ops:
  46.2 6.3 %collective-permute-start.66 = (f32[1280,128]{1,0:T(8,128)S(1)}, f32[1280,128]{1,0:T(8,128)S(1)}, u32[]{:S(2)}, u32[]{:S(2)}) collective-permute-start(f32[1280,128]{1,0:T(8,128)S(1)} %bitcast.273), channel_id=1, source_target_pairs={{0,32},{32,0},{1,33},{33,1},{2,34},{34,2},{3,35},{35,3},{4,36},{36... | collective-permute-start | bytes 1966088 | tf_op jit(solution)/shard_map/ppermute | solution.py:692
  54.9 1.4 copy-start
  56.2 12.1 %copy-start.2 = (f32[40,128]{1,0:T(8,128)S(1)}, f32[40,128]{1,0:T(8,128)}, u32[]{:S(2)}) copy-start(f32[40,128]{1,0:T(8,128)} %constant.129.clone.nodes_ref) | copy-start | bytes 61444
  56.2 12.1 %all-to-all-start.16 = ((f32[4,8,128]{2,1,0:T(8,128)}), f32[4,8,128]{2,1,0:T(8,128)S(1)}, u32[]{:S(2)}, u32[]{:S(2)}) async-start(f32[4,8,128]{2,1,0:T(8,128)} %bitcast.84), calls=%async_computation.16 | async-start | bytes 32768 | tf_op jit(solution)/shard_map/all_to_all | solution.py:647
  60.1 1.7 copy-start.1
  68.4 11.4 %copy-start.7 = (f32[3,2,8,4]{2,3,1,0:T(4,128)S(1)}, f32[3,2,8,4]{2,3,1,0:T(4,128)}, u32[]{:S(2)}) copy-start(f32[3,2,8,4]{2,3,1,0:T(4,128)} %param.13) | copy-start | bytes 2308
  68.4 75.6 %copy-start.5 = (f32[3,3,2,8,4]{3,4,2,1,0:T(4,128)S(1)}, f32[3,3,2,8,4]{3,4,2,1,0:T(4,128)}, u32[]{:S(2)}) copy-start(f32[3,3,2,8,4]{3,4,2,1,0:T(4,128)} %param.15) | copy-start | bytes 6916
  68.4 82.7 %copy-start.4 = (s32[3,16,2,8,4]{1,4,3,2,0:T(4,128)S(1)}, s32[3,16,2,8,4]{1,4,3,2,0:T(4,128)}, u32[]{:S(2)}) copy-start(s32[3,16,2,8,4]{1,4,3,2,0:T(4,128)} %param.16) | copy-start | bytes 36868
  70.5 84.1 %copy-start.6 = (f32[3,16,2,8,4]{1,4,3,2,0:T(4,128)S(1)}, f32[3,16,2,8,4]{1,4,3,2,0:T(4,128)}, u32[]{:S(2)}) copy-start(f32[3,16,2,8,4]{1,4,3,2,0:T(4,128)} %param.17) | copy-start | bytes 36868
  70.5 97.7 %copy-start.3 = (f32[3,2,8,4,256]{4,3,2,1,0:T(4,128)S(1)}, f32[3,2,8,4,256]{4,3,2,1,0:T(4,128)}, u32[]{:S(2)}) copy-start(f32[3,2,8,4,256]{4,3,2,1,0:T(4,128)} %param.12) | copy-start | bytes 589828
  70.5 97.7 %copy-start.8 = (f32[3,2,8,4]{2,3,1,0:T(4,128)S(1)}, f32[3,2,8,4]{2,3,1,0:T(4,128)}, u32[]{:S(2)}) copy-start(f32[3,2,8,4]{2,3,1,0:T(4,128)} %param.14) | copy-start | bytes 2308
  70.5 30.9 %all-to-all-start.17 = ((f32[512,2,1,128]{3,1,2,0:T(2,128)}), f32[512,2,1,128]{3,1,2,0:T(2,128)S(1)}, u32[]{:S(2)}, u32[]{:S(2)}) async-start(f32[512,2,1,128]{3,1,2,0:T(2,128)} %bitcast.87), calls=%async_computation.17 | async-start | bytes 1048576 | tf_op jit(solution)/shard_map/all_to_all | solution.py:647
  102.9 15.6 %all-to-all-start.18 = ((f32[32,17,1,128]{3,2,1,0:T(1,128)}), f32[32,17,1,128]{3,2,1,0:T(1,128)S(1)}, u32[]{:S(2)}, u32[]{:S(2)}) async-start(f32[32,17,1,128]{3,2,1,0:T(1,128)} %bitcast.89), calls=%async_computation.18 | async-start | bytes 557056 | tf_op jit(solution)/shard_map/all_to_all | solution.py:647
  107.2 6.6 %collective-permute-start.67 = (f32[256,128]{1,0:T(8,128)S(1)}, f32[256,128]{1,0:T(8,128)S(1)}, u32[]{:S(2)}, u32[]{:S(2)}) collective-permute-start(f32[256,128]{1,0:T(8,128)S(1)} %get-tuple-element.71), channel_id=1, source_target_pairs={{1,0},{2,1},{3,2},{4,3},{5,4},{6,5},{7,6},{9,8},{10,9},{11,10},{12... | collective-permute-start | bytes 393224 | tf_op jit(solution)/shard_map/ppermute | solution.py:727
  108.5 5.9 %collective-permute-start.68 = (f32[256,128]{1,0:T(8,128)S(1)}, f32[256,128]{1,0:T(8,128)S(1)}, u32[]{:S(2)}, u32[]{:S(2)}) collective-permute-start(f32[256,128]{1,0:T(8,128)S(1)} %get-tuple-element.71), channel_id=1, source_target_pairs={{0,1},{1,2},{2,3},{3,4},{4,5},{5,6},{6,7},{8,9},{9,10},{10,11},{11... | collective-permute-start | bytes 393224 | tf_op jit(solution)/shard_map/ppermute | solution.py:727
  112.5 6.0 %collective-permute-start.69 = (f32[256,128]{1,0:T(8,128)S(1)}, f32[256,128]{1,0:T(8,128)S(1)}, u32[]{:S(2)}, u32[]{:S(2)}) collective-permute-start(f32[256,128]{1,0:T(8,128)S(1)} %get-tuple-element.78), channel_id=1, source_target_pairs={{8,0},{16,8},{24,16},{9,1},{17,9},{25,17},{10,2},{18,10},{26,18},{... | collective-permute-start | bytes 393224 | tf_op jit(solution)/shard_map/ppermute | solution.py:727
  119.2 14.6 %all-to-all-start.19 = ((f32[16,17,1,128]{3,2,1,0:T(1,128)}), f32[16,17,1,128]{3,2,1,0:T(1,128)S(1)}, u32[]{:S(2)}, u32[]{:S(2)}) async-start(f32[16,17,1,128]{3,2,1,0:T(1,128)} %bitcast.91), calls=%async_computation.19 | async-start | bytes 278528 | tf_op jit(solution)/shard_map/all_to_all | solution.py:647
  126.4 6.1 %collective-permute-start.70 = (f32[256,128]{1,0:T(8,128)S(1)}, f32[256,128]{1,0:T(8,128)S(1)}, u32[]{:S(2)}, u32[]{:S(2)}) collective-permute-start(f32[256,128]{1,0:T(8,128)S(1)} %get-tuple-element.78), channel_id=1, source_target_pairs={{0,8},{8,16},{16,24},{1,9},{9,17},{17,25},{2,10},{10,18},{18,26},{... | collective-permute-start | bytes 393224 | tf_op jit(solution)/shard_map/ppermute | solution.py:727
  134.5 20.1 %all-to-all-start.20 = ((f32[32,17,1,128]{3,2,1,0:T(1,128)}), f32[32,17,1,128]{3,2,1,0:T(1,128)S(1)}, u32[]{:S(2)}, u32[]{:S(2)}) async-start(f32[32,17,1,128]{3,2,1,0:T(1,128)} %bitcast.93), calls=%async_computation.20 | async-start | bytes 557056 | tf_op jit(solution)/shard_map/all_to_all | solution.py:647
  144.1 9.8 %collective-permute-start.71 = (f32[256,128]{1,0:T(8,128)S(1)}, f32[256,128]{1,0:T(8,128)S(1)}, u32[]{:S(2)}, u32[]{:S(2)}) collective-permute-start(f32[256,128]{1,0:T(8,128)S(1)} %get-tuple-element.82), channel_id=1, source_target_pairs={{32,0},{64,32},{96,64},{128,96},{160,128},{192,160},{224,192},{256... | collective-permute-start | bytes 393224 | tf_op jit(solution)/shard_map/ppermute | solution.py:727
  147.5 6.4 %collective-permute-start.72 = (f32[256,128]{1,0:T(8,128)S(1)}, f32[256,128]{1,0:T(8,128)S(1)}, u32[]{:S(2)}, u32[]{:S(2)}) collective-permute-start(f32[256,128]{1,0:T(8,128)S(1)} %get-tuple-element.82), channel_id=1, source_target_pairs={{0,32},{32,64},{64,96},{96,128},{128,160},{160,192},{192,224},{224... | collective-permute-start | bytes 393224 | tf_op jit(solution)/shard_map/ppermute | solution.py:727
  168.6 0.6 copy-start.9
  168.6 0.7 copy-start.10
  168.6 0.7 copy-start.11

commit v10 on v8

--- a/solution.py
+++ b/solution.py
@@ -728,17 +728,17 @@
             for sense in senses
         ]
 
-    near = from_neighbours(along[0], GX, (1, -1)) + from_neighbours(along[1], "gy", (1,))
+    near = from_neighbours(along[0], GX, (1, -1))
     part = exchange(products, ("cy", "gy"), 32)
     part, *near = lax.optimization_barrier((part, *near))
     part = call(functools.partial(total_kernel, 32, 16), rows_of(16 * CHUNK), operands=(part,))
     part, along[1] = lax.optimization_barrier((part, along[1]))
-    near += from_neighbours(along[1], "gy", (-1,))
+    near += from_neighbours(along[1], "gy", (1,))
     part = exchange(part, ("core", "gz"), 16)
     part, *near = lax.optimization_barrier((part, *near))
     part = call(functools.partial(total_kernel, 16, 32), rows_of(32 * CHUNK), operands=(part,))
-    part, along[2] = lax.optimization_barrier((part, along[2]))
-    far = from_neighbours(along[2], "gz", (1, -1))
+    part, *along[1:] = lax.optimization_barrier((part, *along[1:]))
+    far = from_neighbours(along[1], "gy", (-1,)) + from_neighbours(along[2], "gz", (1, -1))
     part = exchange(part, ("cy", "gy"), 32)
     part, *far = lax.optimization_barrier((part, *far))
     subspace, projected, force, stress_new, apart = call(

time: 170 us -> 168 us (0.988)
  waiting for transfers between devices: 38.5 us -> 35.3 us
    all_to_all x5, waiting for transfers between devices: 26.8 us -> 22.8 us  [exchange(): return lax.all_to_all(blocks, axes, 0, 0, tiled=True).reshape(rows.shape)]
  transfers between devices with their start and end apart: 12 -> 12, of which waited for: 9 -> 7; matrix products, arithmetic and copies ran while one was open for 0% -> 0% of each run, Pallas kernels for 4% -> 4%
where the time goes in v10:
time: 168 us; the launch traced here: 165 us
  starting transfers between devices  51.3 us (31%)
  blocking collectives  44.3 us (26%)
  waiting for transfers between devices  35.3 us (21%)
  Pallas kernels  28 us (17%)
  local copies, waits for them, and re-layouts  4.22 us (3%)
    all_to_all x1, blocking collectives, exchange(): return lax.all_to_all(blocks, axes, 0, 0, tiled=True).reshape(rows.shape)  44.3 us
    all_to_all x5, starting transfers between devices, exchange(): return lax.all_to_all(blocks, axes, 0, 0, tiled=True).reshape(rows.shape)  30.2 us
    pallas_call x8, Pallas kernels, call(): pl.pallas_call(kernel, out_shape=shape, in_specs=[pl.BlockSpec(memory_spa...  28 us
    all_to_all x5, waiting for transfers between devices, exchange(): return lax.all_to_all(blocks, axes, 0, 0, tiled=True).reshape(rows.shape)  22.8 us
    ppermute x6, starting transfers between devices, from_neighbours(): lax.ppermute(mine, axis, [(b, a) for a, b in pairs] if sense > 0 else pairs)  16.5 us
    ppermute x6, waiting for transfers between devices, from_neighbours(): lax.ppermute(mine, axis, [(b, a) for a, b in pairs] if sense > 0 else pairs)  10.8 us
    ppermute x1, starting transfers between devices, on_device(): other = lax.ppermute(own, 'core', [(0, 1), (1, 0)])  4.57 us
    unnamed x24, local copies, waits for them, and re-layouts  3.79 us
  transfers between devices with their start and end apart: 12, of which 7 were waited for; matrix products, arithmetic and copies ran while one was open for 0% of the time, Pallas kernels for 4%

profile of v10, /device:TPU:1, one launch (start us, length us, event | category | flops | bytes accessed | tf_op | source)
XLA Modules:
  0.0 165.1 jit_solution(17409383718244124293)
XLA Ops:
  0.6 1.3 shard_map.110
  2.0 44.3 %all_to_all.90 = f32[256,5,1,128]{3,2,1,0:T(1,128)S(1)} all-to-all(f32[256,5,1,128]{3,2,1,0:T(1,128)S(1)} %bitcast.275), channel_id=1, replica_groups=mesh['cy'=8,'core'=2,'gy'=4,'gz'=8] {'cy','gy','gz'}, dimensions={0} | all-to-all | bytes 1310720 | tf_op jit(solution)/shard_map/all_to_all | solution.py:647
  46.2 4.6 %collective-permute-start.66 = (f32[1280,128]{1,0:T(8,128)S(1)}, f32[1280,128]{1,0:T(8,128)S(1)}, u32[]{:S(2)}, u32[]{:S(2)}) collective-permute-start(f32[1280,128]{1,0:T(8,128)S(1)} %bitcast.273), channel_id=1, source_target_pairs={{0,32},{32,0},{1,33},{33,1},{2,34},{34,2},{3,35},{35,3},{4,36},{36... | collective-permute-start | bytes 1966088 | tf_op jit(solution)/shard_map/ppermute | solution.py:692
  50.8 1.7 %collective-permute-done.66.other_ref = f32[1280,128]{1,0:T(8,128)S(1)} collective-permute-done((f32[1280,128]{1,0:T(8,128)S(1)}, f32[1280,128]{1,0:T(8,128)S(1)}, u32[]{:S(2)}, u32[]{:S(2)}) %collective-permute-start.66) | collective-permute-done | bytes 655392 | tf_op jit(solution)/shard_map/ppermute | solution.py:692
  52.5 2.3 %shard_map.111 = (f32[16,9,4,8,128]{4,3,2,1,0:T(8,128)S(1)}, f32[32,128]{1,0:T(8,128)}) custom-call(s32[1]{0:T(128)} %bitcast.72.core_ref, f32[1280,128]{1,0:T(8,128)S(1)} %bitcast.274, f32[1280,128]{1,0:T(8,128)S(1)} %collective-permute-done.66.other_ref), custom_call_target="tpu_custom_call" | custom-call | tf_op jit(solution)/shard_map/pallas_call | solution.py:624
  54.9 0.0 copy-start
  54.9 1.4 copy-done
  56.2 0.0 copy-start.2
  56.2 3.9 %all-to-all-start.16 = ((f32[4,8,128]{2,1,0:T(8,128)}), f32[4,8,128]{2,1,0:T(8,128)S(1)}, u32[]{:S(2)}, u32[]{:S(2)}) async-start(f32[4,8,128]{2,1,0:T(8,128)} %bitcast.84), calls=%async_computation.16 | async-start | bytes 32768 | tf_op jit(solution)/shard_map/all_to_all | solution.py:647
  60.1 0.0 copy-start.1
  60.1 1.7 %copy-done.1 = f32[16,9,4,8,128]{4,3,2,1,0:T(8,128)S(1)} copy-done((f32[16,9,4,8,128]{4,3,2,1,0:T(8,128)S(1)}, f32[16,9,4,8,128]{4,3,2,1,0:T(8,128)}, u32[]{:S(2)}) %copy-start.1) | copy-done | bytes 2359320
  61.8 6.6 %shard_map.112.terms_ref = f32[11,16,4,8,128]{4,3,2,1,0:T(8,128)S(1)} custom-call(f32[16,9,4,8,128]{4,3,2,1,0:T(8,128)S(1)} %copy-done.1, f32[32,128]{1,0:T(8,128)} %get-tuple-element.69.top_ref.own_top_ref), custom_call_target="tpu_custom_call" | custom-call | tf_op jit(solution)/shard_map/pallas_call | solution.py:624
  68.4 0.0 copy-start.7
  68.4 0.0 all-to-all-done.16
  68.4 0.0 copy-done.2
  68.4 0.0 copy-start.5
  68.4 0.0 copy-start.4
  68.4 2.1 %shard_map.113 = f32[1024,128]{1,0:T(8,128)} custom-call(f32[11,16,4,8,128]{4,3,2,1,0:T(8,128)S(1)} %shard_map.112.terms_ref, f32[32,128]{1,0:T(8,128)} %get-tuple-element.69.top_ref.own_top_ref, f32[32,128]{1,0:T(8,128)S(1)} %bitcast.280, f32[40,128]{1,0:T(8,128)S(1)} %copy-done.2), custom_call_target="tpu_custom_call" | custom-call | tf_op jit(solution)/shard_map/pallas_call | solution.py:624
  70.5 0.0 copy-start.6
  70.5 0.0 copy-start.3
  70.5 0.0 copy-start.8
  70.5 9.3 %all-to-all-start.17 = ((f32[512,2,1,128]{3,1,2,0:T(2,128)}), f32[512,2,1,128]{3,1,2,0:T(2,128)S(1)}, u32[]{:S(2)}, u32[]{:S(2)}) async-start(f32[512,2,1,128]{3,1,2,0:T(2,128)} %bitcast.87), calls=%async_computation.17 | async-start | bytes 1048576 | tf_op jit(solution)/shard_map/all_to_all | solution.py:647
  79.8 0.0 copy-done.7
  79.8 0.1 reshape_reshape.7
  79.9 21.5 %all-to-all-done.17 = f32[512,2,1,128]{3,1,2,0:T(2,128)S(1)} async-done(((f32[512,2,1,128]{3,1,2,0:T(2,128)}), f32[512,2,1,128]{3,1,2,0:T(2,128)S(1)}, u32[]{:S(2)}, u32[]{:S(2)}) %all-to-all-start.17) | async-done | bytes 524320 | tf_op jit(solution)/shard_map/all_to_all | solution.py:647
  101.4 1.4 shard_map.114
  102.9 4.3 %all-to-all-start.18 = ((f32[32,17,1,128]{3,2,1,0:T(1,128)}), f32[32,17,1,128]{3,2,1,0:T(1,128)S(1)}, u32[]{:S(2)}, u32[]{:S(2)}) async-start(f32[32,17,1,128]{3,2,1,0:T(1,128)} %bitcast.89), calls=%async_computation.18 | async-start | bytes 557056 | tf_op jit(solution)/shard_map/all_to_all | solution.py:647
  107.2 3.2 %collective-permute-start.67 = (f32[256,128]{1,0:T(8,128)S(1)}, f32[256,128]{1,0:T(8,128)S(1)}, u32[]{:S(2)}, u32[]{:S(2)}) collective-permute-start(f32[256,128]{1,0:T(8,128)S(1)} %get-tuple-element.71), channel_id=1, source_target_pairs={{32,0},{64,32},{96,64},{128,96},{160,128},{192,160},{224,192},{256... | collective-permute-start | bytes 393224 | tf_op jit(solution)/shard_map/ppermute | solution.py:727
  110.4 3.2 %collective-permute-start.68 = (f32[256,128]{1,0:T(8,128)S(1)}, f32[256,128]{1,0:T(8,128)S(1)}, u32[]{:S(2)}, u32[]{:S(2)}) collective-permute-start(f32[256,128]{1,0:T(8,128)S(1)} %get-tuple-element.71), channel_id=1, source_target_pairs={{0,32},{32,64},{64,96},{96,128},{128,160},{160,192},{192,224},{224... | collective-permute-start | bytes 393224 | tf_op jit(solution)/shard_map/ppermute | solution.py:727
  113.6 3.5 %collective-permute-done.67.above_x_ref = f32[256,128]{1,0:T(8,128)S(1)} collective-permute-done((f32[256,128]{1,0:T(8,128)S(1)}, f32[256,128]{1,0:T(8,128)S(1)}, u32[]{:S(2)}, u32[]{:S(2)}) %collective-permute-start.67) | collective-permute-done | bytes 131104 | tf_op jit(solution)/shard_map/ppermute | solution.py:727
  117.1 0.0 collective-permute-done.68.below_x_ref
  117.1 0.9 all-to-all-done.18
  118.0 0.7 shard_map.115
  118.7 7.3 %all-to-all-start.19 = ((f32[16,17,1,128]{3,2,1,0:T(1,128)}), f32[16,17,1,128]{3,2,1,0:T(1,128)S(1)}, u32[]{:S(2)}, u32[]{:S(2)}) async-start(f32[16,17,1,128]{3,2,1,0:T(1,128)} %bitcast.91), calls=%async_computation.19 | async-start | bytes 278528 | tf_op jit(solution)/shard_map/all_to_all | solution.py:647
  126.0 1.3 collective-permute-start.69
  127.3 5.7 %collective-permute-done.69.above_y_ref = f32[256,128]{1,0:T(8,128)S(1)} collective-permute-done((f32[256,128]{1,0:T(8,128)S(1)}, f32[256,128]{1,0:T(8,128)S(1)}, u32[]{:S(2)}, u32[]{:S(2)}) %collective-permute-start.69) | collective-permute-done | bytes 131104 | tf_op jit(solution)/shard_map/ppermute | solution.py:727
  133.0 0.4 all-to-all-done.19
  133.4 0.7 shard_map.116
  134.2 5.5 %all-to-all-start.20 = ((f32[32,17,1,128]{3,2,1,0:T(1,128)}), f32[32,17,1,128]{3,2,1,0:T(1,128)S(1)}, u32[]{:S(2)}, u32[]{:S(2)}) async-start(f32[32,17,1,128]{3,2,1,0:T(1,128)} %bitcast.93), calls=%async_computation.20 | async-start | bytes 557056 | tf_op jit(solution)/shard_map/all_to_all | solution.py:647
  139.6 0.0 copy-done.5
  139.7 0.1 copy.303
  139.8 1.3 collective-permute-start.71
  141.1 4.1 %collective-permute-start.72 = (f32[256,128]{1,0:T(8,128)S(1)}, f32[256,128]{1,0:T(8,128)S(1)}, u32[]{:S(2)}, u32[]{:S(2)}) collective-permute-start(f32[256,128]{1,0:T(8,128)S(1)} %get-tuple-element.82), channel_id=1, source_target_pairs={{0,1},{1,2},{2,3},{3,4},{4,5},{5,6},{6,7},{8,9},{9,10},{10,11},{11... | collective-permute-start | bytes 393224 | tf_op jit(solution)/shard_map/ppermute | solution.py:727
  145.2 3.4 %collective-permute-start.70 = (f32[256,128]{1,0:T(8,128)S(1)}, f32[256,128]{1,0:T(8,128)S(1)}, u32[]{:S(2)}, u32[]{:S(2)}) collective-permute-start(f32[256,128]{1,0:T(8,128)S(1)} %get-tuple-element.81), channel_id=1, source_target_pairs={{0,8},{8,16},{16,24},{1,9},{9,17},{17,25},{2,10},{10,18},{18,26},{... | collective-permute-start | bytes 393224 | tf_op jit(solution)/shard_map/ppermute | solution.py:727
  148.6 0.0 copy-done.4
  148.6 0.1 select_multiply_fusion
  148.7 1.6 collective-permute-done.70.below_y_ref
  150.3 0.0 collective-permute-done.71.above_z_ref
  150.3 0.0 collective-permute-done.72.below_z_ref
  150.3 0.0 all-to-all-done.20
  150.4 0.0 copy-done.6
  150.4 12.8 %shard_map.117 = (f32[48,4,256]{2,1,0:T(4,128)S(1)}, f32[256,256]{1,0:T(8,128)}, f32[24,8]{1,0:T(8,128)S(1)}, f32[48,4,16]{2,1,0:T(4,128)S(1)}, s32[1,1]{1,0:T(1,128)}) custom-call(f32[544,128]{1,0:T(8,128)S(1)} %bitcast.276, f32[1024,128]{1,0:T(8,128)S(1)} %bitcast.272, f32[256,128]{1,0:T(8,128)S(1)} %collective-permute-done.67.above_x_ref, ...), custom_call_target="tpu_custom_call" | custom-call | tf_op jit(solution)/shard_map/pallas_call | solution.py:624
  163.2 0.1 copy.304
  164.0 0.0 copy-done.3
  164.0 0.0 copy-done.8
  164.0 0.4 conditional.1
  164.3 0.1 copy.316
  164.4 0.0 copy-start.9
  164.4 0.0 copy-start.10
  164.4 0.0 copy-start.11
  164.4 0.6 copy-done.9
  165.0 0.1 copy-done.10
  165.1 0.0 copy-done.11
  (3 shorter events, 0.0 us)
Async XLA Ops:
  46.2 6.3 %collective-permute-start.66 = (f32[1280,128]{1,0:T(8,128)S(1)}, f32[1280,128]{1,0:T(8,128)S(1)}, u32[]{:S(2)}, u32[]{:S(2)}) collective-permute-start(f32[1280,128]{1,0:T(8,128)S(1)} %bitcast.273), channel_id=1, source_target_pairs={{0,32},{32,0},{1,33},{33,1},{2,34},{34,2},{3,35},{35,3},{4,36},{36... | collective-permute-start | bytes 1966088 | tf_op jit(solution)/shard_map/ppermute | solution.py:692
  54.9 1.4 copy-start
  56.2 12.1 %copy-start.2 = (f32[40,128]{1,0:T(8,128)S(1)}, f32[40,128]{1,0:T(8,128)}, u32[]{:S(2)}) copy-start(f32[40,128]{1,0:T(8,128)} %constant.129.clone.nodes_ref) | copy-start | bytes 61444
  56.2 12.1 %all-to-all-start.16 = ((f32[4,8,128]{2,1,0:T(8,128)}), f32[4,8,128]{2,1,0:T(8,128)S(1)}, u32[]{:S(2)}, u32[]{:S(2)}) async-start(f32[4,8,128]{2,1,0:T(8,128)} %bitcast.84), calls=%async_computation.16 | async-start | bytes 32768 | tf_op jit(solution)/shard_map/all_to_all | solution.py:647
  60.1 1.7 %copy-start.1 = (f32[16,9,4,8,128]{4,3,2,1,0:T(8,128)S(1)}, f32[16,9,4,8,128]{4,3,2,1,0:T(8,128)}, u32[]{:S(2)}) copy-start(f32[16,9,4,8,128]{4,3,2,1,0:T(8,128)} %copy-done) | copy-start | bytes 7077892
  68.4 11.4 %copy-start.7 = (f32[3,2,8,4]{2,3,1,0:T(4,128)S(1)}, f32[3,2,8,4]{2,3,1,0:T(4,128)}, u32[]{:S(2)}) copy-start(f32[3,2,8,4]{2,3,1,0:T(4,128)} %param.13) | copy-start | bytes 2308
  68.4 71.2 %copy-start.5 = (f32[3,3,2,8,4]{3,4,2,1,0:T(4,128)S(1)}, f32[3,3,2,8,4]{3,4,2,1,0:T(4,128)}, u32[]{:S(2)}) copy-start(f32[3,3,2,8,4]{3,4,2,1,0:T(4,128)} %param.15) | copy-start | bytes 6916
  68.4 80.2 %copy-start.4 = (s32[3,16,2,8,4]{1,4,3,2,0:T(4,128)S(1)}, s32[3,16,2,8,4]{1,4,3,2,0:T(4,128)}, u32[]{:S(2)}) copy-start(s32[3,16,2,8,4]{1,4,3,2,0:T(4,128)} %param.16) | copy-start | bytes 36868
  70.5 79.8 %copy-start.6 = (f32[3,16,2,8,4]{1,4,3,2,0:T(4,128)S(1)}, f32[3,16,2,8,4]{1,4,3,2,0:T(4,128)}, u32[]{:S(2)}) copy-start(f32[3,16,2,8,4]{1,4,3,2,0:T(4,128)} %param.17) | copy-start | bytes 36868
  70.5 93.4 %copy-start.3 = (f32[3,2,8,4,256]{4,3,2,1,0:T(4,128)S(1)}, f32[3,2,8,4,256]{4,3,2,1,0:T(4,128)}, u32[]{:S(2)}) copy-start(f32[3,2,8,4,256]{4,3,2,1,0:T(4,128)} %param.12) | copy-start | bytes 589828
  70.5 93.4 %copy-start.8 = (f32[3,2,8,4]{2,3,1,0:T(4,128)S(1)}, f32[3,2,8,4]{2,3,1,0:T(4,128)}, u32[]{:S(2)}) copy-start(f32[3,2,8,4]{2,3,1,0:T(4,128)} %param.14) | copy-start | bytes 2308
  70.5 30.9 %all-to-all-start.17 = ((f32[512,2,1,128]{3,1,2,0:T(2,128)}), f32[512,2,1,128]{3,1,2,0:T(2,128)S(1)}, u32[]{:S(2)}, u32[]{:S(2)}) async-start(f32[512,2,1,128]{3,1,2,0:T(2,128)} %bitcast.87), calls=%async_computation.17 | async-start | bytes 1048576 | tf_op jit(solution)/shard_map/all_to_all | solution.py:647
  102.9 15.2 %all-to-all-start.18 = ((f32[32,17,1,128]{3,2,1,0:T(1,128)}), f32[32,17,1,128]{3,2,1,0:T(1,128)S(1)}, u32[]{:S(2)}, u32[]{:S(2)}) async-start(f32[32,17,1,128]{3,2,1,0:T(1,128)} %bitcast.89), calls=%async_computation.18 | async-start | bytes 557056 | tf_op jit(solution)/shard_map/all_to_all | solution.py:647
  107.2 9.9 %collective-permute-start.67 = (f32[256,128]{1,0:T(8,128)S(1)}, f32[256,128]{1,0:T(8,128)S(1)}, u32[]{:S(2)}, u32[]{:S(2)}) collective-permute-start(f32[256,128]{1,0:T(8,128)S(1)} %get-tuple-element.71), channel_id=1, source_target_pairs={{32,0},{64,32},{96,64},{128,96},{160,128},{192,160},{224,192},{256... | collective-permute-start | bytes 393224 | tf_op jit(solution)/shard_map/ppermute | solution.py:727
  110.4 6.7 %collective-permute-start.68 = (f32[256,128]{1,0:T(8,128)S(1)}, f32[256,128]{1,0:T(8,128)S(1)}, u32[]{:S(2)}, u32[]{:S(2)}) collective-permute-start(f32[256,128]{1,0:T(8,128)S(1)} %get-tuple-element.71), channel_id=1, source_target_pairs={{0,32},{32,64},{64,96},{96,128},{128,160},{160,192},{192,224},{224... | collective-permute-start | bytes 393224 | tf_op jit(solution)/shard_map/ppermute | solution.py:727
  118.7 14.7 %all-to-all-start.19 = ((f32[16,17,1,128]{3,2,1,0:T(1,128)}), f32[16,17,1,128]{3,2,1,0:T(1,128)S(1)}, u32[]{:S(2)}, u32[]{:S(2)}) async-start(f32[16,17,1,128]{3,2,1,0:T(1,128)} %bitcast.91), calls=%async_computation.19 | async-start | bytes 278528 | tf_op jit(solution)/shard_map/all_to_all | solution.py:647
  126.0 6.9 %collective-permute-start.69 = (f32[256,128]{1,0:T(8,128)S(1)}, f32[256,128]{1,0:T(8,128)S(1)}, u32[]{:S(2)}, u32[]{:S(2)}) collective-permute-start(f32[256,128]{1,0:T(8,128)S(1)} %get-tuple-element.81), channel_id=1, source_target_pairs={{8,0},{16,8},{24,16},{9,1},{17,9},{25,17},{10,2},{18,10},{26,18},{... | collective-permute-start | bytes 393224 | tf_op jit(solution)/shard_map/ppermute | solution.py:727
  134.2 16.2 %all-to-all-start.20 = ((f32[32,17,1,128]{3,2,1,0:T(1,128)}), f32[32,17,1,128]{3,2,1,0:T(1,128)S(1)}, u32[]{:S(2)}, u32[]{:S(2)}) async-start(f32[32,17,1,128]{3,2,1,0:T(1,128)} %bitcast.93), calls=%async_computation.20 | async-start | bytes 557056 | tf_op jit(solution)/shard_map/all_to_all | solution.py:647
  139.8 10.6 %collective-permute-start.71 = (f32[256,128]{1,0:T(8,128)S(1)}, f32[256,128]{1,0:T(8,128)S(1)}, u32[]{:S(2)}, u32[]{:S(2)}) collective-permute-start(f32[256,128]{1,0:T(8,128)S(1)} %get-tuple-element.82), channel_id=1, source_target_pairs={{1,0},{2,1},{3,2},{4,3},{5,4},{6,5},{7,6},{9,8},{10,9},{11,10},{12... | collective-permute-start | bytes 393224 | tf_op jit(solution)/shard_map/ppermute | solution.py:727
  141.1 9.3 %collective-permute-start.72 = (f32[256,128]{1,0:T(8,128)S(1)}, f32[256,128]{1,0:T(8,128)S(1)}, u32[]{:S(2)}, u32[]{:S(2)}) collective-permute-start(f32[256,128]{1,0:T(8,128)S(1)} %get-tuple-element.82), channel_id=1, source_target_pairs={{0,1},{1,2},{2,3},{3,4},{4,5},{5,6},{6,7},{8,9},{9,10},{10,11},{11... | collective-permute-start | bytes 393224 | tf_op jit(solution)/shard_map/ppermute | solution.py:727
  145.2 5.1 %collective-permute-start.70 = (f32[256,128]{1,0:T(8,128)S(1)}, f32[256,128]{1,0:T(8,128)S(1)}, u32[]{:S(2)}, u32[]{:S(2)}) collective-permute-start(f32[256,128]{1,0:T(8,128)S(1)} %get-tuple-element.81), channel_id=1, source_target_pairs={{0,8},{8,16},{16,24},{1,9},{9,17},{17,25},{2,10},{10,18},{18,26},{... | collective-permute-start | bytes 393224 | tf_op jit(solution)/shard_map/ppermute | solution.py:727
  164.4 0.6 copy-start.9
  164.4 0.7 copy-start.10
  164.4 0.7 copy-start.11

commit v11 on v10

--- a/solution.py
+++ b/solution.py
@@ -170,7 +170,9 @@
     refs = (own_ref, other_ref)
     second = []
     for gx in range(16):
-        held_ref[gx, 0] = grid_row(refs, core, gx, core)
+        held_ref[gx, 0] = jnp.where(
+            core == 0, grid_row(refs, 0, gx, core), grid_row(refs, 1, gx, core)
+        )
         first, along_y = both_halves(grid_row(refs, 2, gx, core))
         tangent_ref[gx] = first
         second.append(along_y)

time: 168 us -> 168 us (level)
  no operation moved by 1% of the time
where the time goes in v11:
time: 168 us; the launch traced here: 165 us
  starting transfers between devices  51.3 us (31%)
  blocking collectives  44.3 us (26%)
  waiting for transfers between devices  35.3 us (21%)
  Pallas kernels  28 us (17%)
  local copies, waits for them, and re-layouts  4.22 us (3%)
    all_to_all x1, blocking collectives, exchange(): return lax.all_to_all(blocks, axes, 0, 0, tiled=True).reshape(rows.shape)  44.3 us
    all_to_all x5, starting transfers between devices, exchange(): return lax.all_to_all(blocks, axes, 0, 0, tiled=True).reshape(rows.shape)  30.2 us
    pallas_call x8, Pallas kernels, call(): pl.pallas_call(kernel, out_shape=shape, in_specs=[pl.BlockSpec(memory_spa...  28 us
    all_to_all x5, waiting for transfers between devices, exchange(): return lax.all_to_all(blocks, axes, 0, 0, tiled=True).reshape(rows.shape)  22.8 us
    ppermute x6, starting transfers between devices, from_neighbours(): lax.ppermute(mine, axis, [(b, a) for a, b in pairs] if sense > 0 else pairs)  16.5 us
    ppermute x6, waiting for transfers between devices, from_neighbours(): lax.ppermute(mine, axis, [(b, a) for a, b in pairs] if sense > 0 else pairs)  10.8 us
    ppermute x1, starting transfers between devices, on_device(): other = lax.ppermute(own, 'core', [(0, 1), (1, 0)])  4.57 us
    unnamed x24, local copies, waits for them, and re-layouts  3.79 us
  transfers between devices with their start and end apart: 12, of which 7 were waited for; matrix products, arithmetic and copies ran while one was open for 0% of the time, Pallas kernels for 4%

profile of v11, /device:TPU:1, one launch (start us, length us, event | category | flops | bytes accessed | tf_op | source)
XLA Modules:
  0.0 165.1 jit_solution(15162647293807223455)
XLA Ops:
  0.6 1.3 shard_map.110
  2.0 44.3 %all_to_all.90 = f32[256,5,1,128]{3,2,1,0:T(1,128)S(1)} all-to-all(f32[256,5,1,128]{3,2,1,0:T(1,128)S(1)} %bitcast.275), channel_id=1, replica_groups=mesh['cy'=8,'core'=2,'gy'=4,'gz'=8] {'cy','gy','gz'}, dimensions={0} | all-to-all | bytes 1310720 | tf_op jit(solution)/shard_map/all_to_all | solution.py:649
  46.2 4.6 %collective-permute-start.66 = (f32[1280,128]{1,0:T(8,128)S(1)}, f32[1280,128]{1,0:T(8,128)S(1)}, u32[]{:S(2)}, u32[]{:S(2)}) collective-permute-start(f32[1280,128]{1,0:T(8,128)S(1)} %bitcast.273), channel_id=1, source_target_pairs={{0,32},{32,0},{1,33},{33,1},{2,34},{34,2},{3,35},{35,3},{4,36},{36... | collective-permute-start | bytes 1966088 | tf_op jit(solution)/shard_map/ppermute | solution.py:694
  50.8 1.7 %collective-permute-done.66.other_ref = f32[1280,128]{1,0:T(8,128)S(1)} collective-permute-done((f32[1280,128]{1,0:T(8,128)S(1)}, f32[1280,128]{1,0:T(8,128)S(1)}, u32[]{:S(2)}, u32[]{:S(2)}) %collective-permute-start.66) | collective-permute-done | bytes 655392 | tf_op jit(solution)/shard_map/ppermute | solution.py:694
  52.5 2.3 %shard_map.111 = (f32[16,9,4,8,128]{4,3,2,1,0:T(8,128)S(1)}, f32[32,128]{1,0:T(8,128)}) custom-call(s32[1]{0:T(128)} %bitcast.72.core_ref, f32[1280,128]{1,0:T(8,128)S(1)} %bitcast.274, f32[1280,128]{1,0:T(8,128)S(1)} %collective-permute-done.66.other_ref), custom_call_target="tpu_custom_call" | custom-call | tf_op jit(solution)/shard_map/pallas_call | solution.py:626
  54.9 0.0 copy-start
  54.9 1.4 copy-done
  56.2 0.0 copy-start.2
  56.2 3.9 %all-to-all-start.16 = ((f32[4,8,128]{2,1,0:T(8,128)}), f32[4,8,128]{2,1,0:T(8,128)S(1)}, u32[]{:S(2)}, u32[]{:S(2)}) async-start(f32[4,8,128]{2,1,0:T(8,128)} %bitcast.84), calls=%async_computation.16 | async-start | bytes 32768 | tf_op jit(solution)/shard_map/all_to_all | solution.py:649
  60.1 0.0 copy-start.1
  60.1 1.7 %copy-done.1 = f32[16,9,4,8,128]{4,3,2,1,0:T(8,128)S(1)} copy-done((f32[16,9,4,8,128]{4,3,2,1,0:T(8,128)S(1)}, f32[16,9,4,8,128]{4,3,2,1,0:T(8,128)}, u32[]{:S(2)}) %copy-start.1) | copy-done | bytes 2359320
  61.8 6.6 %shard_map.112.terms_ref = f32[11,16,4,8,128]{4,3,2,1,0:T(8,128)S(1)} custom-call(f32[16,9,4,8,128]{4,3,2,1,0:T(8,128)S(1)} %copy-done.1, f32[32,128]{1,0:T(8,128)} %get-tuple-element.69.top_ref.own_top_ref), custom_call_target="tpu_custom_call" | custom-call | tf_op jit(solution)/shard_map/pallas_call | solution.py:626
  68.4 0.0 copy-start.7
  68.4 0.0 all-to-all-done.16
  68.4 0.0 copy-done.2
  68.4 0.0 copy-start.5
  68.4 0.0 copy-start.4
  68.4 2.1 %shard_map.113 = f32[1024,128]{1,0:T(8,128)} custom-call(f32[11,16,4,8,128]{4,3,2,1,0:T(8,128)S(1)} %shard_map.112.terms_ref, f32[32,128]{1,0:T(8,128)} %get-tuple-element.69.top_ref.own_top_ref, f32[32,128]{1,0:T(8,128)S(1)} %bitcast.280, f32[40,128]{1,0:T(8,128)S(1)} %copy-done.2), custom_call_target="tpu_custom_call" | custom-call | tf_op jit(solution)/shard_map/pallas_call | solution.py:626
  70.5 0.0 copy-start.6
  70.5 0.0 copy-start.3
  70.5 0.0 copy-start.8
  70.5 9.3 %all-to-all-start.17 = ((f32[512,2,1,128]{3,1,2,0:T(2,128)}), f32[512,2,1,128]{3,1,2,0:T(2,128)S(1)}, u32[]{:S(2)}, u32[]{:S(2)}) async-start(f32[512,2,1,128]{3,1,2,0:T(2,128)} %bitcast.87), calls=%async_computation.17 | async-start | bytes 1048576 | tf_op jit(solution)/shard_map/all_to_all | solution.py:649
  79.8 0.0 copy-done.7
  79.8 0.1 reshape_reshape.7
  79.9 21.5 %all-to-all-done.17 = f32[512,2,1,128]{3,1,2,0:T(2,128)S(1)} async-done(((f32[512,2,1,128]{3,1,2,0:T(2,128)}), f32[512,2,1,128]{3,1,2,0:T(2,128)S(1)}, u32[]{:S(2)}, u32[]{:S(2)}) %all-to-all-start.17) | async-done | bytes 524320 | tf_op jit(solution)/shard_map/all_to_all | solution.py:649
  101.4 1.4 shard_map.114
  102.9 4.3 %all-to-all-start.18 = ((f32[32,17,1,128]{3,2,1,0:T(1,128)}), f32[32,17,1,128]{3,2,1,0:T(1,128)S(1)}, u32[]{:S(2)}, u32[]{:S(2)}) async-start(f32[32,17,1,128]{3,2,1,0:T(1,128)} %bitcast.89), calls=%async_computation.18 | async-start | bytes 557056 | tf_op jit(solution)/shard_map/all_to_all | solution.py:649
  107.2 3.2 %collective-permute-start.67 = (f32[256,128]{1,0:T(8,128)S(1)}, f32[256,128]{1,0:T(8,128)S(1)}, u32[]{:S(2)}, u32[]{:S(2)}) collective-permute-start(f32[256,128]{1,0:T(8,128)S(1)} %get-tuple-element.71), channel_id=1, source_target_pairs={{32,0},{64,32},{96,64},{128,96},{160,128},{192,160},{224,192},{256... | collective-permute-start | bytes 393224 | tf_op jit(solution)/shard_map/ppermute | solution.py:729
  110.4 3.2 %collective-permute-start.68 = (f32[256,128]{1,0:T(8,128)S(1)}, f32[256,128]{1,0:T(8,128)S(1)}, u32[]{:S(2)}, u32[]{:S(2)}) collective-permute-start(f32[256,128]{1,0:T(8,128)S(1)} %get-tuple-element.71), channel_id=1, source_target_pairs={{0,32},{32,64},{64,96},{96,128},{128,160},{160,192},{192,224},{224... | collective-permute-start | bytes 393224 | tf_op jit(solution)/shard_map/ppermute | solution.py:729
  113.6 3.5 %collective-permute-done.67.above_x_ref = f32[256,128]{1,0:T(8,128)S(1)} collective-permute-done((f32[256,128]{1,0:T(8,128)S(1)}, f32[256,128]{1,0:T(8,128)S(1)}, u32[]{:S(2)}, u32[]{:S(2)}) %collective-permute-start.67) | collective-permute-done | bytes 131104 | tf_op jit(solution)/shard_map/ppermute | solution.py:729
  117.1 0.0 collective-permute-done.68.below_x_ref
  117.1 0.9 all-to-all-done.18
  118.0 0.7 shard_map.115
  118.7 7.3 %all-to-all-start.19 = ((f32[16,17,1,128]{3,2,1,0:T(1,128)}), f32[16,17,1,128]{3,2,1,0:T(1,128)S(1)}, u32[]{:S(2)}, u32[]{:S(2)}) async-start(f32[16,17,1,128]{3,2,1,0:T(1,128)} %bitcast.91), calls=%async_computation.19 | async-start | bytes 278528 | tf_op jit(solution)/shard_map/all_to_all | solution.py:649
  126.0 1.3 collective-permute-start.69
  127.3 5.7 %collective-permute-done.69.above_y_ref = f32[256,128]{1,0:T(8,128)S(1)} collective-permute-done((f32[256,128]{1,0:T(8,128)S(1)}, f32[256,128]{1,0:T(8,128)S(1)}, u32[]{:S(2)}, u32[]{:S(2)}) %collective-permute-start.69) | collective-permute-done | bytes 131104 | tf_op jit(solution)/shard_map/ppermute | solution.py:729
  133.0 0.4 all-to-all-done.19
  133.4 0.7 shard_map.116
  134.2 5.5 %all-to-all-start.20 = ((f32[32,17,1,128]{3,2,1,0:T(1,128)}), f32[32,17,1,128]{3,2,1,0:T(1,128)S(1)}, u32[]{:S(2)}, u32[]{:S(2)}) async-start(f32[32,17,1,128]{3,2,1,0:T(1,128)} %bitcast.93), calls=%async_computation.20 | async-start | bytes 557056 | tf_op jit(solution)/shard_map/all_to_all | solution.py:649
  139.6 0.0 copy-done.5
  139.7 0.1 copy.303
  139.8 1.3 collective-permute-start.71
  141.1 4.1 %collective-permute-start.72 = (f32[256,128]{1,0:T(8,128)S(1)}, f32[256,128]{1,0:T(8,128)S(1)}, u32[]{:S(2)}, u32[]{:S(2)}) collective-permute-start(f32[256,128]{1,0:T(8,128)S(1)} %get-tuple-element.82), channel_id=1, source_target_pairs={{0,1},{1,2},{2,3},{3,4},{4,5},{5,6},{6,7},{8,9},{9,10},{10,11},{11... | collective-permute-start | bytes 393224 | tf_op jit(solution)/shard_map/ppermute | solution.py:729
  145.2 3.4 %collective-permute-start.70 = (f32[256,128]{1,0:T(8,128)S(1)}, f32[256,128]{1,0:T(8,128)S(1)}, u32[]{:S(2)}, u32[]{:S(2)}) collective-permute-start(f32[256,128]{1,0:T(8,128)S(1)} %get-tuple-element.81), channel_id=1, source_target_pairs={{0,8},{8,16},{16,24},{1,9},{9,17},{17,25},{2,10},{10,18},{18,26},{... | collective-permute-start | bytes 393224 | tf_op jit(solution)/shard_map/ppermute | solution.py:729
  148.6 0.0 copy-done.4
  148.6 0.1 select_multiply_fusion
  148.7 1.6 collective-permute-done.70.below_y_ref
  150.3 0.0 collective-permute-done.71.above_z_ref
  150.3 0.0 collective-permute-done.72.below_z_ref
  150.3 0.0 all-to-all-done.20
  150.4 0.0 copy-done.6
  150.4 12.8 %shard_map.117 = (f32[48,4,256]{2,1,0:T(4,128)S(1)}, f32[256,256]{1,0:T(8,128)}, f32[24,8]{1,0:T(8,128)S(1)}, f32[48,4,16]{2,1,0:T(4,128)S(1)}, s32[1,1]{1,0:T(1,128)}) custom-call(f32[544,128]{1,0:T(8,128)S(1)} %bitcast.276, f32[1024,128]{1,0:T(8,128)S(1)} %bitcast.272, f32[256,128]{1,0:T(8,128)S(1)} %collective-permute-done.67.above_x_ref, ...), custom_call_target="tpu_custom_call" | custom-call | tf_op jit(solution)/shard_map/pallas_call | solution.py:626
  163.2 0.1 copy.304
  164.0 0.0 copy-done.3
  164.0 0.0 copy-done.8
  164.0 0.4 conditional.1
  164.3 0.1 copy.316
  164.4 0.0 copy-start.9
  164.4 0.0 copy-start.10
  164.4 0.0 copy-start.11
  164.4 0.6 copy-done.9
  165.0 0.1 copy-done.10
  165.1 0.0 copy-done.11
  (3 shorter events, 0.0 us)
Async XLA Ops:
  46.2 6.3 %collective-permute-start.66 = (f32[1280,128]{1,0:T(8,128)S(1)}, f32[1280,128]{1,0:T(8,128)S(1)}, u32[]{:S(2)}, u32[]{:S(2)}) collective-permute-start(f32[1280,128]{1,0:T(8,128)S(1)} %bitcast.273), channel_id=1, source_target_pairs={{0,32},{32,0},{1,33},{33,1},{2,34},{34,2},{3,35},{35,3},{4,36},{36... | collective-permute-start | bytes 1966088 | tf_op jit(solution)/shard_map/ppermute | solution.py:694
  54.9 1.4 copy-start
  56.2 12.1 %copy-start.2 = (f32[40,128]{1,0:T(8,128)S(1)}, f32[40,128]{1,0:T(8,128)}, u32[]{:S(2)}) copy-start(f32[40,128]{1,0:T(8,128)} %constant.129.clone.nodes_ref) | copy-start | bytes 61444
  56.2 12.1 %all-to-all-start.16 = ((f32[4,8,128]{2,1,0:T(8,128)}), f32[4,8,128]{2,1,0:T(8,128)S(1)}, u32[]{:S(2)}, u32[]{:S(2)}) async-start(f32[4,8,128]{2,1,0:T(8,128)} %bitcast.84), calls=%async_computation.16 | async-start | bytes 32768 | tf_op jit(solution)/shard_map/all_to_all | solution.py:649
  60.1 1.7 %copy-start.1 = (f32[16,9,4,8,128]{4,3,2,1,0:T(8,128)S(1)}, f32[16,9,4,8,128]{4,3,2,1,0:T(8,128)}, u32[]{:S(2)}) copy-start(f32[16,9,4,8,128]{4,3,2,1,0:T(8,128)} %copy-done) | copy-start | bytes 7077892
  68.4 11.4 %copy-start.7 = (f32[3,2,8,4]{2,3,1,0:T(4,128)S(1)}, f32[3,2,8,4]{2,3,1,0:T(4,128)}, u32[]{:S(2)}) copy-start(f32[3,2,8,4]{2,3,1,0:T(4,128)} %param.13) | copy-start | bytes 2308
  68.4 71.2 %copy-start.5 = (f32[3,3,2,8,4]{3,4,2,1,0:T(4,128)S(1)}, f32[3,3,2,8,4]{3,4,2,1,0:T(4,128)}, u32[]{:S(2)}) copy-start(f32[3,3,2,8,4]{3,4,2,1,0:T(4,128)} %param.15) | copy-start | bytes 6916
  68.4 80.2 %copy-start.4 = (s32[3,16,2,8,4]{1,4,3,2,0:T(4,128)S(1)}, s32[3,16,2,8,4]{1,4,3,2,0:T(4,128)}, u32[]{:S(2)}) copy-start(s32[3,16,2,8,4]{1,4,3,2,0:T(4,128)} %param.16) | copy-start | bytes 36868
  70.5 79.8 %copy-start.6 = (f32[3,16,2,8,4]{1,4,3,2,0:T(4,128)S(1)}, f32[3,16,2,8,4]{1,4,3,2,0:T(4,128)}, u32[]{:S(2)}) copy-start(f32[3,16,2,8,4]{1,4,3,2,0:T(4,128)} %param.17) | copy-start | bytes 36868
  70.5 93.4 %copy-start.3 = (f32[3,2,8,4,256]{4,3,2,1,0:T(4,128)S(1)}, f32[3,2,8,4,256]{4,3,2,1,0:T(4,128)}, u32[]{:S(2)}) copy-start(f32[3,2,8,4,256]{4,3,2,1,0:T(4,128)} %param.12) | copy-start | bytes 589828
  70.5 93.4 %copy-start.8 = (f32[3,2,8,4]{2,3,1,0:T(4,128)S(1)}, f32[3,2,8,4]{2,3,1,0:T(4,128)}, u32[]{:S(2)}) copy-start(f32[3,2,8,4]{2,3,1,0:T(4,128)} %param.14) | copy-start | bytes 2308
  70.5 30.9 %all-to-all-start.17 = ((f32[512,2,1,128]{3,1,2,0:T(2,128)}), f32[512,2,1,128]{3,1,2,0:T(2,128)S(1)}, u32[]{:S(2)}, u32[]{:S(2)}) async-start(f32[512,2,1,128]{3,1,2,0:T(2,128)} %bitcast.87), calls=%async_computation.17 | async-start | bytes 1048576 | tf_op jit(solution)/shard_map/all_to_all | solution.py:649
  102.9 15.2 %all-to-all-start.18 = ((f32[32,17,1,128]{3,2,1,0:T(1,128)}), f32[32,17,1,128]{3,2,1,0:T(1,128)S(1)}, u32[]{:S(2)}, u32[]{:S(2)}) async-start(f32[32,17,1,128]{3,2,1,0:T(1,128)} %bitcast.89), calls=%async_computation.18 | async-start | bytes 557056 | tf_op jit(solution)/shard_map/all_to_all | solution.py:649
  107.2 9.9 %collective-permute-start.67 = (f32[256,128]{1,0:T(8,128)S(1)}, f32[256,128]{1,0:T(8,128)S(1)}, u32[]{:S(2)}, u32[]{:S(2)}) collective-permute-start(f32[256,128]{1,0:T(8,128)S(1)} %get-tuple-element.71), channel_id=1, source_target_pairs={{32,0},{64,32},{96,64},{128,96},{160,128},{192,160},{224,192},{256... | collective-permute-start | bytes 393224 | tf_op jit(solution)/shard_map/ppermute | solution.py:729
  110.4 6.7 %collective-permute-start.68 = (f32[256,128]{1,0:T(8,128)S(1)}, f32[256,128]{1,0:T(8,128)S(1)}, u32[]{:S(2)}, u32[]{:S(2)}) collective-permute-start(f32[256,128]{1,0:T(8,128)S(1)} %get-tuple-element.71), channel_id=1, source_target_pairs={{0,32},{32,64},{64,96},{96,128},{128,160},{160,192},{192,224},{224... | collective-permute-start | bytes 393224 | tf_op jit(solution)/shard_map/ppermute | solution.py:729
  118.7 14.7 %all-to-all-start.19 = ((f32[16,17,1,128]{3,2,1,0:T(1,128)}), f32[16,17,1,128]{3,2,1,0:T(1,128)S(1)}, u32[]{:S(2)}, u32[]{:S(2)}) async-start(f32[16,17,1,128]{3,2,1,0:T(1,128)} %bitcast.91), calls=%async_computation.19 | async-start | bytes 278528 | tf_op jit(solution)/shard_map/all_to_all | solution.py:649
  126.0 6.9 %collective-permute-start.69 = (f32[256,128]{1,0:T(8,128)S(1)}, f32[256,128]{1,0:T(8,128)S(1)}, u32[]{:S(2)}, u32[]{:S(2)}) collective-permute-start(f32[256,128]{1,0:T(8,128)S(1)} %get-tuple-element.81), channel_id=1, source_target_pairs={{8,0},{16,8},{24,16},{9,1},{17,9},{25,17},{10,2},{18,10},{26,18},{... | collective-permute-start | bytes 393224 | tf_op jit(solution)/shard_map/ppermute | solution.py:729
  134.2 16.2 %all-to-all-start.20 = ((f32[32,17,1,128]{3,2,1,0:T(1,128)}), f32[32,17,1,128]{3,2,1,0:T(1,128)S(1)}, u32[]{:S(2)}, u32[]{:S(2)}) async-start(f32[32,17,1,128]{3,2,1,0:T(1,128)} %bitcast.93), calls=%async_computation.20 | async-start | bytes 557056 | tf_op jit(solution)/shard_map/all_to_all | solution.py:649
  139.8 10.6 %collective-permute-start.71 = (f32[256,128]{1,0:T(8,128)S(1)}, f32[256,128]{1,0:T(8,128)S(1)}, u32[]{:S(2)}, u32[]{:S(2)}) collective-permute-start(f32[256,128]{1,0:T(8,128)S(1)} %get-tuple-element.82), channel_id=1, source_target_pairs={{1,0},{2,1},{3,2},{4,3},{5,4},{6,5},{7,6},{9,8},{10,9},{11,10},{12... | collective-permute-start | bytes 393224 | tf_op jit(solution)/shard_map/ppermute | solution.py:729
  141.1 9.3 %collective-permute-start.72 = (f32[256,128]{1,0:T(8,128)S(1)}, f32[256,128]{1,0:T(8,128)S(1)}, u32[]{:S(2)}, u32[]{:S(2)}) collective-permute-start(f32[256,128]{1,0:T(8,128)S(1)} %get-tuple-element.82), channel_id=1, source_target_pairs={{0,1},{1,2},{2,3},{3,4},{4,5},{5,6},{6,7},{8,9},{9,10},{10,11},{11... | collective-permute-start | bytes 393224 | tf_op jit(solution)/shard_map/ppermute | solution.py:729
  145.2 5.1 %collective-permute-start.70 = (f32[256,128]{1,0:T(8,128)S(1)}, f32[256,128]{1,0:T(8,128)S(1)}, u32[]{:S(2)}, u32[]{:S(2)}) collective-permute-start(f32[256,128]{1,0:T(8,128)S(1)} %get-tuple-element.81), channel_id=1, source_target_pairs={{0,8},{8,16},{16,24},{1,9},{9,17},{17,25},{2,10},{10,18},{18,26},{... | collective-permute-start | bytes 393224 | tf_op jit(solution)/shard_map/ppermute | solution.py:729
  164.4 0.6 copy-start.9
  164.4 0.7 copy-start.10
  164.4 0.7 copy-start.11
